TPU v7x, 256 devices: a whole 4x4x8 slice. The times are simulated.
256 devices in a mesh: wide: 8 (over z_hi, core), narrow: 32 (over y, x, z_lo).
Axes of the slice: x: 4, y: 4, z: 8 (z_hi: 4, z_lo: 2; z = z_hi * 2 + z_lo), core: 2. Of those that a mesh axis runs over, the one named last changes fastest.
Arguments:
- queries: bfloat16 [32768, 2048], P(('narrow', 'wide')), may hold values from -4.5 to 4.5, as said below
- keys: bfloat16 [32768, 2048], P(('narrow', 'wide')), may hold values from -4.5 to 4.5, as said below
- values: bfloat16 [32768, 2048], P(('narrow', 'wide')), may hold values from -6 to 6, as said below
- grad_out: bfloat16 [32768, 2048], P(('narrow', 'wide')), may hold values from -6 to 6, as said below
Outputs:
- attended: bfloat16 [32768, 2048], P(('narrow', 'wide'))
- grad_queries: bfloat16 [32768, 2048], P(('narrow', 'wide'))
- grad_keys: bfloat16 [32768, 2048], P(('narrow', 'wide'))
- grad_values: bfloat16 [32768, 2048], P(('narrow', 'wide'))
Inputs may be any that keep to these rules, and one draw needn't show every extreme that they name: Entries of queries stay within this range. Entries of keys stay within this range. Entries of values stay within this range. Entries of grad_out stay within this range.
All inputs are finite; a program needn't handle non-finite values.
Results may differ from a plain program's by a relative error of at most 0.022.
Values may be sent and summed in bfloat16 or wider, within the bound.
No kernel may reach another device: no remote copies, remote signals or barrier semaphores. Data moves between devices by JAX's collectives and lax.ppermute only.
A program may use at most 128 MiB of HBM per device.

v0:
```python
import jax
import jax.numpy as jnp
from jax import lax
from jax.sharding import PartitionSpec as P

HEADS = 16
HEAD_DIM = 128
POOL_NEAR = 4
POOL_FAR = 64
NEAR_KEYS = 32
FAR_KEYS = 2


def shifted(value, axis, by):
    peers = lax.axis_size(axis)
    pairs = [(i, i + by) for i in range(peers) if 0 <= i + by < peers]
    return lax.ppermute(value, axis, pairs)


def pool_rows(matrix, factor):
    grouped = matrix.astype(jnp.float32).reshape(-1, factor, matrix.shape[-1])
    return jnp.mean(grouped, axis=1).astype(jnp.bfloat16)


def spread_rows(matrix, factor):
    widened = jnp.broadcast_to(matrix[:, None, :], (matrix.shape[0], factor, matrix.shape[1]))
    return widened.reshape(-1, matrix.shape[1])


def build_bias(row_count, span_len, far_total, far_span, wide_at, narrow_at):
    row_ids = jnp.arange(row_count, dtype=jnp.int32)
    blocked = jnp.float32(-jnp.inf)
    causal = jnp.where(row_ids[None, :] <= row_ids[:, None], jnp.float32(0.0), blocked)
    near_blocks = jnp.arange(span_len, dtype=jnp.int32) // NEAR_KEYS
    near_bias = jnp.where(near_blocks <= wide_at - 1, jnp.float32(0.0), blocked)
    far_spans = jnp.arange(far_total, dtype=jnp.int32) // far_span
    far_bias = jnp.where(far_spans < narrow_at, jnp.float32(0.0), blocked)
    prior_bias = jnp.where(
        jnp.zeros((row_count,), jnp.int32) + wide_at > 0, jnp.float32(0.0), blocked
    )
    rest_bias = jnp.concatenate([near_bias, far_bias, prior_bias])
    spread_bias = jnp.broadcast_to(rest_bias[None, :], (row_count, rest_bias.shape[0]))
    return jnp.concatenate([causal, spread_bias], axis=1)


def shards(queries, keys, values, grad_out):
    row_count, feat_count = queries.shape
    wide_count = lax.axis_size("wide")
    narrow_count = lax.axis_size("narrow")
    wide_at = lax.axis_index("wide")
    narrow_at = lax.axis_index("narrow")
    score_scale = HEAD_DIM ** (-0.5)
    pair_width = 2 * HEAD_DIM
    pair_total = HEADS // 2
    prior_keys, prior_values = shifted((keys, values), "wide", 1)
    near_keys = pool_rows(keys, POOL_NEAR)
    near_values = pool_rows(values, POOL_NEAR)
    span_keys, span_values = (
        lax.all_gather(near_keys, "wide", axis=0, tiled=True),
        lax.all_gather(near_values, "wide", axis=0, tiled=True),
    )
    group_keys = pool_rows(span_keys, POOL_FAR // POOL_NEAR)
    group_values = pool_rows(span_values, POOL_FAR // POOL_NEAR)
    far_keys, far_values = (
        lax.all_gather(group_keys, "narrow", axis=0, tiled=True),
        lax.all_gather(group_values, "narrow", axis=0, tiled=True),
    )
    span_len = span_keys.shape[0]
    far_total = far_keys.shape[0]
    key_list = jnp.concatenate([keys, span_keys, far_keys, prior_keys], axis=0)
    value_list = jnp.concatenate([values, span_values, far_values, prior_values], axis=0)
    key_count = key_list.shape[0]
    bias = build_bias(row_count, span_len, far_total, wide_count * FAR_KEYS, wide_at, narrow_at)

    def pair_step(pair_index, carried):
        out_acc, dq_acc, dk_acc, dv_acc, total_acc, dot_acc = carried
        column_start = pair_index * pair_width
        query_pair = lax.dynamic_slice_in_dim(queries, column_start, pair_width, 1).reshape(
            row_count, 2, HEAD_DIM
        )
        grad_pair = lax.dynamic_slice_in_dim(grad_out, column_start, pair_width, 1).reshape(
            row_count, 2, HEAD_DIM
        )
        key_pair = lax.dynamic_slice_in_dim(key_list, column_start, pair_width, 1).reshape(
            key_count, 2, HEAD_DIM
        )
        value_pair = lax.dynamic_slice_in_dim(value_list, column_start, pair_width, 1).reshape(
            key_count, 2, HEAD_DIM
        )
        scores = (
            jnp.einsum("qhd,khd->hqk", query_pair, key_pair, preferred_element_type=jnp.float32)
            * score_scale
            + bias[None]
        )
        row_max = jnp.max(scores, axis=2, keepdims=True)
        log_total = row_max + jnp.log(jnp.sum(jnp.exp(scores - row_max), axis=2, keepdims=True))
        softmax = jnp.exp(scores - log_total)
        weights = softmax.astype(jnp.bfloat16)
        attended = jnp.einsum(
            "hqk,khd->qhd", weights, value_pair, preferred_element_type=jnp.float32
        ).astype(jnp.bfloat16)
        row_dot = jnp.einsum("qhd,qhd->hq", grad_pair, attended, preferred_element_type=jnp.float32)
        dprob = jnp.einsum(
            "qhd,khd->hqk", grad_pair, value_pair, preferred_element_type=jnp.float32
        )
        dscore = (softmax * (dprob - row_dot[:, :, None])).astype(jnp.bfloat16)
        grad_query = (
            jnp.einsum("hqk,khd->qhd", dscore, key_pair, preferred_element_type=jnp.float32)
            * score_scale
        )
        key_terms = (
            jnp.einsum("hqk,qhd->khd", dscore, query_pair, preferred_element_type=jnp.float32)
            * score_scale
        )
        value_terms = jnp.einsum(
            "hqk,qhd->khd", weights, grad_pair, preferred_element_type=jnp.float32
        )
        out_acc = lax.dynamic_update_slice_in_dim(
            out_acc, attended.reshape(row_count, pair_width), column_start, 1
        )
        dq_acc = lax.dynamic_update_slice_in_dim(
            dq_acc, grad_query.reshape(row_count, pair_width), column_start, 1
        )
        dk_acc = lax.dynamic_update_slice_in_dim(
            dk_acc, key_terms.reshape(key_count, pair_width), column_start, 1
        )
        dv_acc = lax.dynamic_update_slice_in_dim(
            dv_acc, value_terms.reshape(key_count, pair_width), column_start, 1
        )
        total_acc = lax.dynamic_update_slice_in_dim(
            total_acc, log_total[:, :, 0], pair_index * 2, 0
        )
        dot_acc = lax.dynamic_update_slice_in_dim(dot_acc, row_dot, pair_index * 2, 0)
        return (out_acc, dq_acc, dk_acc, dv_acc, total_acc, dot_acc)

    initial = (
        jnp.zeros((row_count, feat_count), jnp.bfloat16),
        jnp.zeros((row_count, feat_count), jnp.float32),
        jnp.zeros((key_count, feat_count), jnp.float32),
        jnp.zeros((key_count, feat_count), jnp.float32),
        jnp.zeros((HEADS, row_count), jnp.float32),
        jnp.zeros((HEADS, row_count), jnp.float32),
    )
    attended, grad_query, key_terms, value_terms, total_rows, dot_rows = lax.fori_loop(
        0, pair_total, pair_step, initial
    )
    next_k, next_v = (
        shifted(key_terms[key_count - row_count :].astype(jnp.bfloat16), "wide", -1).astype(
            jnp.float32
        ),
        shifted(value_terms[key_count - row_count :].astype(jnp.bfloat16), "wide", -1).astype(
            jnp.float32
        ),
    )
    own_keys = key_terms[:row_count] + next_k
    own_values = value_terms[:row_count] + next_v
    near_end = row_count + span_len
    far_end = near_end + far_total
    near_k, near_v = (
        lax.psum_scatter(
            key_terms[row_count:near_end].astype(jnp.bfloat16),
            "wide",
            scatter_dimension=0,
            tiled=True,
        ).astype(jnp.float32),
        lax.psum_scatter(
            value_terms[row_count:near_end].astype(jnp.bfloat16),
            "wide",
            scatter_dimension=0,
            tiled=True,
        ).astype(jnp.float32),
    )
    far_k_terms = key_terms[near_end:far_end].reshape(
        narrow_count, wide_count, FAR_KEYS, feat_count
    )
    far_v_terms = value_terms[near_end:far_end].reshape(
        narrow_count, wide_count, FAR_KEYS, feat_count
    )
    span_k, span_v = (
        lax.psum_scatter(
            far_k_terms.astype(jnp.bfloat16), "narrow", scatter_dimension=0, tiled=True
        ).astype(jnp.float32),
        lax.psum_scatter(
            far_v_terms.astype(jnp.bfloat16), "narrow", scatter_dimension=0, tiled=True
        ).astype(jnp.float32),
    )
    far_k, far_v = (
        lax.psum_scatter(
            span_k.astype(jnp.bfloat16), "wide", scatter_dimension=1, tiled=True
        ).astype(jnp.float32),
        lax.psum_scatter(
            span_v.astype(jnp.bfloat16), "wide", scatter_dimension=1, tiled=True
        ).astype(jnp.float32),
    )
    far_k = far_k.reshape(FAR_KEYS, feat_count)
    far_v = far_v.reshape(FAR_KEYS, feat_count)
    grad_keys = (
        own_keys
        + spread_rows(near_k / POOL_NEAR, POOL_NEAR)
        + spread_rows(far_k / POOL_FAR, POOL_FAR)
    )
    grad_values = (
        own_values
        + spread_rows(near_v / POOL_NEAR, POOL_NEAR)
        + spread_rows(far_v / POOL_FAR, POOL_FAR)
    )
    return (
        attended,
        grad_query.astype(jnp.bfloat16),
        grad_keys.astype(jnp.bfloat16),
        grad_values.astype(jnp.bfloat16),
    )


def solution(mesh):
    return jax.shard_map(
        shards,
        mesh=mesh,
        in_specs=(
            P(("narrow", "wide"), None),
            P(("narrow", "wide"), None),
            P(("narrow", "wide"), None),
            P(("narrow", "wide"), None),
        ),
        out_specs=(
            P(("narrow", "wide"), None),
            P(("narrow", "wide"), None),
            P(("narrow", "wide"), None),
            P(("narrow", "wide"), None),
        ),
        check_vma=False,
    )
```

profile of v0, /device:TPU:34, one launch (start us, length us, event | category | flops | bytes accessed | tf_op | source)
XLA Modules:
  0.0 1018.1 jit_solution(17605822567763792410)
XLA Ops:
  12.8 29.5 %all-gather.5.cloned.1.call-done = bf16[256,2048]{1,0:T(8,128)(2,1)} async-done(((bf16[32,2048]{1,0:T(8,128)(2,1)}), bf16[256,2048]{1,0:T(8,128)(2,1)}) %all-gather.5.cloned.1.call-update) | async-done | bytes 1048592 | tf_op jit(solution)/shard_map/all_gather | solution.py:60
  42.3 1.6 convert_reduce_fusion.1
  44.6 28.6 %all-gather.9.cloned.1.call-done = bf16[256,2048]{1,0:T(8,128)(2,1)} async-done(((bf16[32,2048]{1,0:T(8,128)(2,1)}), bf16[256,2048]{1,0:T(8,128)(2,1)}) %all-gather.9.cloned.1.call-update) | async-done | bytes 1048592 | tf_op jit(solution)/shard_map/all_gather | solution.py:59
  73.2 1.7 convert_reduce_fusion
  75.6 2.2 collective-permute-start
  77.8 3.5 collective-permute-start.1
  82.2 146.6 %all-gather.7.cloned.1.call-done = bf16[512,2048]{1,0:T(8,128)(2,1)} async-done(((bf16[16,2048]{1,0:T(8,128)(2,1)}), bf16[512,2048]{1,0:T(8,128)(2,1)}) %all-gather.7.cloned.1.call-update) | async-done | bytes 2097168 | tf_op jit(solution)/shard_map/all_gather | solution.py:66
  228.8 3.5 pad_maximum_fusion
  232.3 163.1 %all-gather.11.cloned.1.call-done = bf16[512,2048]{1,0:T(8,128)(2,1)} async-done(((bf16[16,2048]{1,0:T(8,128)(2,1)}), bf16[512,2048]{1,0:T(8,128)(2,1)}) %all-gather.11.cloned.1.call-update) | async-done | bytes 2097168 | tf_op jit(solution)/shard_map/all_gather | solution.py:65
  395.4 3.5 pad_maximum_fusion.1
  400.5 4.3 broadcast.85.clone
  404.8 4.3 broadcast.85.clone2
  409.1 89.8 %while.19 = (s32[]{:T(128)}, bf16[128,2048]{1,0:T(8,128)(2,1)}, bf16[128,2048]{1,0:T(8,128)(2,1)}, f32[1024,2048]{1,0:T(8,128)}, f32[1024,2048]{1,0:T(8,128)}, /...) while((s32[]{:T(128)}, bf16[128,2048]{1,0:T(8,128)(2,1)}, ...), condition=%wide.region_7.8_spmd, body=%wide.region_4.7_spmd.sunk | while | flops 406552064 | bytes 25636052 | solution.py:144
  413.6 1.5 fusion.53
  418.8 1.6 constant_dynamic-update-slice_fusion.7
  424.9 1.5 fusion.53
  430.1 1.5 constant_dynamic-update-slice_fusion.7
  436.1 1.5 fusion.53
  441.3 1.6 constant_dynamic-update-slice_fusion.7
  447.4 1.5 fusion.53
  452.5 1.5 constant_dynamic-update-slice_fusion.7
  463.7 1.6 constant_dynamic-update-slice_fusion.7
  469.8 1.5 fusion.53
  475.0 1.5 constant_dynamic-update-slice_fusion.7
  486.1 1.5 constant_dynamic-update-slice_fusion.7
  492.2 1.5 fusion.53
  497.3 1.5 constant_dynamic-update-slice_fusion.7
  498.9 4.0 convert.14
  502.9 1.9 copy-done
  506.0 3.2 slice.40
  509.2 3.2 convert_element_type.90
  512.3 2.2 copy.48
  514.9 4.0 convert.15
  518.9 2.0 copy-done.1
  522.3 3.2 convert_element_type.95
  525.5 2.2 copy.52
  527.8 2.3 slice.42
  530.8 1.9 slice.38
  532.7 1.9 slice.41
  537.2 11.5 %reduce-scatter.7.cloned.1.call-done = bf16[32,2048]{1,0:T(8,128)(2,1)} async-done(((bf16[256,2048]{1,0:T(8,128)(2,1)}), bf16[32,2048]{1,0:T(8,128)(2,1)}) %reduce-scatter.7.cloned.1.call-update) | async-done | bytes 131088 | tf_op jit(solution)/shard_map/reduce_scatter | solution.py:160
  549.6 170.6 %reduce-scatter.9.cloned.1.call-done = bf16[1,8,2,2048]{3,1,2,0:T(8,128)(2,1)} async-done(((bf16[32,8,2,2048]{3,1,2,0:T(8,128)(2,1)}), bf16[1,8,2,2048]{3,1,2,0:T(8,128)(2,1)}) %reduce-scatter.9.cloned.1.call-update) | async-done | bytes 65552 | tf_op jit(solution)/shard_map/reduce_scatter | solution.py:180
  720.2 1.5 copy.49
  721.8 164.3 %reduce-scatter.13.cloned.1.call-done = bf16[1,8,2,2048]{3,1,2,0:T(8,128)(2,1)} async-done(((bf16[32,8,2,2048]{3,1,2,0:T(8,128)(2,1)}), bf16[1,8,2,2048]{3,1,2,0:T(8,128)(2,1)}) %reduce-scatter.13.cloned.1.call-update) | async-done | bytes 65552 | tf_op jit(solution)/shard_map/reduce_scatter | solution.py:183
  886.0 1.5 copy.53
  887.6 44.1 %reduce-scatter.11.cloned.1.call-done = bf16[32,2048]{1,0:T(8,128)(2,1)} async-done(((bf16[256,2048]{1,0:T(8,128)(2,1)}), bf16[32,2048]{1,0:T(8,128)(2,1)}) %reduce-scatter.11.cloned.1.call-update) | async-done | bytes 131088 | tf_op jit(solution)/shard_map/reduce_scatter | solution.py:166
  933.9 71.7 %all-reduce.5.cloned.1.call-done = (bf16[1,8,2,2048]{3,2,1,0:T(2,128)(2,1)}, bf16[1,8,2,2048]{3,2,1,0:T(2,128)(2,1)}) async-done(((bf16[1,8,2,2048]{3,2,1,0:T(2,128)(2,1)}, bf16[1,8,2,2048]{3,2,1,0:T(2,128)(2,1)}), (bf16[1,8,2,2048]{3,2,1,0:T(2,128)(2,1)}, bf16[1,8,2,2048]{3,2,1,0:T(2,128)(2,1)})) %all-reduce.5.cloned.1.call-update) | async-done | bytes 131088
  1006.9 2.4 fusion.9
  1009.2 2.4 fusion.8
  (222 shorter events, 87.9 us)
Async XLA Ops:
  7.2 68.4 %copy-start.3 = (bf16[128,2048]{1,0:T(8,128)(2,1)S(1)}, bf16[128,2048]{1,0:T(8,128)(2,1)}, u32[]{:S(2)}) copy-start(bf16[128,2048]{1,0:T(8,128)(2,1)} %param.8) | copy-start | bytes 1572868
  7.2 70.6 %copy-start.4 = (bf16[128,2048]{1,0:T(8,128)(2,1)S(1)}, bf16[128,2048]{1,0:T(8,128)(2,1)}, u32[]{:S(2)}) copy-start(bf16[128,2048]{1,0:T(8,128)(2,1)} %param.7) | copy-start | bytes 1572868
  7.2 35.1 %all-gather.5.cloned.1.call-start = ((), (), s32[]{:S(2)}) async-start(), calls=%async_computation.4 | async-start | bytes 1179648 | tf_op jit(solution)/shard_map/all_gather | solution.py:60
  10.0 63.2 %all-gather.9.cloned.1.call-start = ((), (), s32[]{:S(2)}) async-start(), calls=%async_computation.6 | async-start | bytes 1179648 | tf_op jit(solution)/shard_map/all_gather | solution.py:59
  12.8 216.0 %all-gather.7.cloned.1.call-start = ((), (), s32[]{:S(2)}) async-start(), calls=%async_computation.5 | async-start | bytes 2162688 | tf_op jit(solution)/shard_map/all_gather | solution.py:66
  44.5 350.8 %all-gather.11.cloned.1.call-start = ((), (), s32[]{:S(2)}) async-start(), calls=%async_computation.7 | async-start | bytes 2162688 | tf_op jit(solution)/shard_map/all_gather | solution.py:65
  73.2 322.2 %copy-start.2 = (bf16[256,2048]{1,0:T(8,128)(2,1)S(1)}, bf16[256,2048]{1,0:T(8,128)(2,1)}, u32[]{:S(2)}) copy-start(bf16[256,2048]{1,0:T(8,128)(2,1)} %all-gather.9.cloned.1.call-done) | copy-start | bytes 3145732
  75.5 473.1 %reduce-scatter.7.cloned.1.call-start = ((), (), s32[]{:S(2)}) async-start(), calls=%async_computation.8 | async-start | bytes 1179648 | tf_op jit(solution)/shard_map/reduce_scatter | solution.py:160
  75.6 6.6 collective-permute-start
  77.8 154.5 %collective-permute-start.1 = (bf16[128,2048]{1,0:T(8,128)(2,1)S(1)}, bf16[128,2048]{1,0:T(8,128)(2,1)S(1)}, u32[]{:S(2)}, u32[]{:S(2)}) collective-permute-start(bf16[128,2048]{1,0:T(8,128)(2,1)S(1)} %copy-done.4), channel_id=1, source_target_pairs={{0,32},{32,64},{64,96},{96,128},{128,160},{160,192},{192,224},{1,3... | collective-permute-start | bytes 1572872 | tf_op jit(solution)/shard_map/ppermute | solution.py:17
  502.9 1.9 copy-start
  506.0 214.3 %reduce-scatter.9.cloned.1.call-start = ((), (), s32[]{:S(2)}) async-start(), calls=%async_computation.9 | async-start | bytes 2162688 | tf_op jit(solution)/shard_map/reduce_scatter | solution.py:180
  514.6 371.4 %reduce-scatter.13.cloned.1.call-start = ((), (), s32[]{:S(2)}) async-start(), calls=%async_computation.11 | async-start | bytes 2162688 | tf_op jit(solution)/shard_map/reduce_scatter | solution.py:183
  518.9 2.0 copy-start.1
  520.9 9.3 copy-start.5
  527.8 403.9 %reduce-scatter.11.cloned.1.call-start = ((), (), s32[]{:S(2)}) async-start(), calls=%async_computation.10 | async-start | bytes 1179648 | tf_op jit(solution)/shard_map/reduce_scatter | solution.py:166
  530.1 475.4 %all-reduce.5.cloned.1.call-start = ((), (), s32[]{:S(2)}) async-start(), calls=%async_computation.12 | async-start | bytes 262144
  534.6 472.3 %collective-permute-start.2 = (bf16[128,2048]{1,0:T(8,128)(2,1)}, bf16[128,2048]{1,0:T(8,128)(2,1)}, u32[]{:S(2)}, u32[]{:S(2)}) collective-permute-start(bf16[128,2048]{1,0:T(8,128)(2,1)} %slice.38), channel_id=1, source_target_pairs={{32,0},{64,32},{96,64},{128,96},{160,128},{192,160},{224,192},{33,... | collective-permute-start | bytes 1572872 | tf_op jit(solution)/shard_map/ppermute | solution.py:17
  535.9 473.4 %collective-permute-start.3 = (bf16[128,2048]{1,0:T(8,128)(2,1)}, bf16[128,2048]{1,0:T(8,128)(2,1)}, u32[]{:S(2)}, u32[]{:S(2)}) collective-permute-start(bf16[128,2048]{1,0:T(8,128)(2,1)} %slice.41), channel_id=1, source_target_pairs={{32,0},{64,32},{96,64},{128,96},{160,128},{192,160},{224,192},{33,... | collective-permute-start | bytes 1572872 | tf_op jit(solution)/shard_map/ppermute | solution.py:17
Sparse Core Ops, SparseCore 0:
  10.5 31.7 all-gather.4
  44.7 28.4 all-gather.8
  75.6 153.1 all-gather.6
  231.0 164.3 all-gather.10
  506.1 42.5 reduce-scatter.6
  551.1 169.1 reduce-scatter.8
  722.9 163.0 reduce-scatter.12
  888.6 43.0 reduce-scatter.10
  934.9 70.6 all-reduce.4
where the time goes:
time: 1020 us
  waiting for transfers between devices  830 us (81%)
  local copies, waits for them, and re-layouts  105 us (10%)
  other arithmetic  33.5 us (3%)
  matrix products  25.7 us (3%)
  between operations  14.1 us (1%)
    reduce_scatter x1, waiting for transfers between devices, shards(): lax.psum_scatter(far_k_terms.astype(jnp.bfloat16), 'narrow', scatter_dime...  171 us
    reduce_scatter x1, waiting for transfers between devices, shards(): lax.psum_scatter(far_v_terms.astype(jnp.bfloat16), 'narrow', scatter_dime...  164 us
    all_gather x1, waiting for transfers between devices, shards(): lax.all_gather(group_keys, 'narrow', axis=0, tiled=True)  163 us
    all_gather x1, waiting for transfers between devices, shards(): lax.all_gather(group_values, 'narrow', axis=0, tiled=True)  147 us
    unnamed x10, waiting for transfers between devices  71.8 us
    reduce_scatter x1, waiting for transfers between devices, shards(): lax.psum_scatter(value_terms[row_count:near_end].astype(jnp.bfloat16), 'w...  44.1 us
    all_gather x1, waiting for transfers between devices, shards(): lax.all_gather(near_values, 'wide', axis=0, tiled=True)  29.5 us
    all_gather x1, waiting for transfers between devices, shards(): lax.all_gather(near_keys, 'wide', axis=0, tiled=True)  28.6 us
  transfers between devices with their start and end apart: 13, of which 9 were waited for; matrix products, arithmetic and copies ran while one was open for 5% of the time, Pallas kernels for 0%

commit v1 on v0

v1 whole, which is shorter than its diff:
```python
import functools

import jax
import jax.numpy as jnp
from jax import lax
from jax.experimental import pallas as pl
from jax.experimental.pallas import tpu as pltpu
from jax.sharding import PartitionSpec as P

HEAD_DIM = 128
BLOCK = 128
NEAR = 4
FAR = 64
NEAR_ROWS = 32
FAR_ROWS = 2
WIDE = 8
NARROW = 32
SPAN = WIDE * BLOCK
SPAN_NEAR = WIDE * NEAR_ROWS
SPAN_FAR = WIDE * FAR_ROWS
FAR_ALL = NARROW * SPAN_FAR
FEAT = 2048
PAIR = 2 * HEAD_DIM
SCALE = HEAD_DIM**-0.5
LOG2E = 1.4426950408889634
BLOCKED = -1e30
F32 = jnp.float32
BF16 = jnp.bfloat16

STEPS = [(2, 0), (2, 1), (1, 0), (3, 0), (1, 1), (3, 1), (0, 1), (0, 0)]
SENT = len(STEPS) - 1


def target(at, step):
    chip, core = step
    return ((at // 2 + chip) % 4) * 2 + (at % 2 + core) % 2


def source(at, step):
    chip, core = step
    return ((at // 2 + 4 - chip) % 4) * 2 + (at % 2 + core) % 2


def send(buffers):
    moved = [
        lax.ppermute(b, "wide", [(s, target(s, step)) for s in range(WIDE)])
        for b, step in zip(buffers[:SENT], STEPS)
    ]
    return moved + [buffers[SENT]]


def nt(a, b):
    return lax.dot_general(a, b, (((1,), (1,)), ((), ())), preferred_element_type=F32)


def nn(a, b):
    return lax.dot_general(a, b, (((1,), (0,)), ((), ())), preferred_element_type=F32)


def tn(a, b):
    return lax.dot_general(a, b, (((0,), (0,)), ((), ())), preferred_element_type=F32)


def pooling(rows, factor):
    shape = (rows, rows * factor)
    group = lax.broadcasted_iota(jnp.int32, shape, 1) // factor
    member = group == lax.broadcasted_iota(jnp.int32, shape, 0)
    return jnp.where(member, F32(1.0 / factor), F32(0.0)).astype(BF16)


def spreading(rows, factor):
    shape = (rows * factor, rows)
    group = lax.broadcasted_iota(jnp.int32, shape, 0) // factor
    member = group == lax.broadcasted_iota(jnp.int32, shape, 1)
    return jnp.where(member, F32(1.0 / factor), F32(0.0)).astype(BF16)


def pack_kernel(at_ref, q_ref, k_ref, v_ref, g_ref, *outs):
    wide_at = at_ref[0]
    far_ref = outs[-1]
    for part, step in enumerate(STEPS):
        to = target(wide_at, step)
        for half in range(2):
            columns = pl.ds(pl.multiple_of(to * PAIR + half * HEAD_DIM, HEAD_DIM), HEAD_DIM)
            out = outs[half * len(STEPS) + part]
            for i, ref in enumerate((k_ref, v_ref, q_ref, g_ref)):
                out[i * BLOCK : (i + 1) * BLOCK, :] = ref[:, columns]
    pool_near = pooling(NEAR_ROWS, NEAR)
    pool_far = pooling(FAR_ROWS, FAR // NEAR)
    for i, ref in enumerate((k_ref, v_ref)):
        near = nn(pool_near, ref[...]).astype(BF16)
        far = nn(pool_far, near).astype(BF16)
        for to in range(WIDE):
            far_ref[to, i * FAR_ROWS : (i + 1) * FAR_ROWS, :] = far[:, to * PAIR : (to + 1) * PAIR]


def pack(at, queries, keys, values, grad_out):
    part = jax.ShapeDtypeStruct((4 * BLOCK, HEAD_DIM), BF16)
    far = jax.ShapeDtypeStruct((WIDE, 2 * FAR_ROWS, PAIR), BF16)
    vmem = pl.BlockSpec(memory_space=pltpu.VMEM)
    outs = pl.pallas_call(
        pack_kernel,
        out_shape=[part] * (2 * len(STEPS)) + [far],
        in_specs=[pl.BlockSpec(memory_space=pltpu.SMEM)] + [vmem] * 4,
        out_specs=[vmem] * (2 * len(STEPS) + 1),
        compiler_params=pltpu.CompilerParams(vmem_limit_bytes=24 << 20),
        name="pack",
    )(at, queries, keys, values, grad_out)
    n = len(STEPS)
    return outs[:n], outs[n : 2 * n], outs[2 * n]


def attend_kernel(half, at_ref, *refs):
    n_steps = len(STEPS)
    ins = refs[:n_steps]
    far_ref = refs[n_steps]
    outs = refs[n_steps + 1 : 2 * n_steps + 1]
    far_out = refs[2 * n_steps + 1]
    (q_s, g_s, k_s, v_s, kn_s, vn_s, kf_s, vf_s, o_s, dq_s, dk_s, dv_s, dkn_s, dvn_s, dkf_s, dvf_s, s_s, w_s, d_s) = refs[2 * n_steps + 2 :]
    wide_at = at_ref[0]
    far_seen = at_ref[1] * SPAN_FAR
    pool_near = pooling(NEAR_ROWS, NEAR)
    for part, step in enumerate(STEPS):
        block = source(wide_at, step)
        rows = pl.ds(pl.multiple_of(block * BLOCK, BLOCK), BLOCK)
        near_rows = pl.ds(pl.multiple_of(block * NEAR_ROWS, NEAR_ROWS), NEAR_ROWS)
        piece = [ins[part][i * BLOCK : (i + 1) * BLOCK, :] for i in range(4)]
        k_s[rows, :], v_s[rows, :], q_s[rows, :], g_s[rows, :] = piece
        kn_s[near_rows, :] = nn(pool_near, piece[0]).astype(BF16)
        vn_s[near_rows, :] = nn(pool_near, piece[1]).astype(BF16)
    lanes = slice(half * HEAD_DIM, (half + 1) * HEAD_DIM)
    kf_s[...] = far_ref[:, :SPAN_FAR, lanes].reshape(FAR_ALL, HEAD_DIM)
    vf_s[...] = far_ref[:, SPAN_FAR:, lanes].reshape(FAR_ALL, HEAD_DIM)
    for ref in (dk_s, dv_s, dkn_s, dvn_s, dkf_s, dvf_s):
        ref[...] = jnp.zeros(ref.shape, F32)

    later = lax.broadcasted_iota(jnp.int32, (BLOCK, BLOCK), 0) > lax.broadcasted_iota(
        jnp.int32, (BLOCK, BLOCK), 1
    )
    far_blocked = lax.broadcasted_iota(jnp.int32, (FAR_ALL, 1), 0) >= far_seen
    far_bias = jnp.where(far_blocked, F32(BLOCKED), F32(0.0))
    exponent = SCALE * LOG2E
    wide2 = 2 * BLOCK

    for pair in range(WIDE // 2):
        q_rows = slice(pair * wide2, (pair + 1) * wide2)
        q, g = q_s[q_rows, :], g_s[q_rows, :]
        near = 2 * NEAR_ROWS * pair + NEAR_ROWS
        far_from = wide2 + near
        total = far_from + FAR_ALL
        lists = []
        for b in range(2):
            block = 2 * pair + b
            lists.append((max(block - 1, 0) * BLOCK, block * BLOCK))
        for b in range(2):
            q_b = q[b * BLOCK : (b + 1) * BLOCK]
            cols = slice(b * BLOCK, (b + 1) * BLOCK)
            before, own = lists[b]
            if before == own:
                s_s[0:BLOCK, cols] = jnp.full((BLOCK, BLOCK), BLOCKED, F32)
            else:
                s_s[0:BLOCK, cols] = nt(k_s[before : before + BLOCK, :], q_b)
            s_s[BLOCK:wide2, cols] = jnp.where(later, F32(BLOCKED), nt(k_s[own : own + BLOCK, :], q_b))
        s_s[wide2:far_from, :] = nt(kn_s[0:near, :], q)
        s_s[far_from - NEAR_ROWS : far_from, 0:BLOCK] = jnp.full((NEAR_ROWS, BLOCK), BLOCKED, F32)
        for i in range(0, FAR_ALL, BLOCK):
            s_s[far_from + i : far_from + i + BLOCK, :] = nt(kf_s[i : i + BLOCK, :], q) + far_bias[i : i + BLOCK]
        chunks = [(0, BLOCK), (BLOCK, BLOCK)]
        chunks += [(wide2 + i, min(BLOCK, near - i)) for i in range(0, near, BLOCK)]
        chunks += [(far_from + i, BLOCK) for i in range(0, FAR_ALL, BLOCK)]
        top = None
        for start, size in chunks:
            here = jnp.max(s_s[start : start + size, :].reshape(size // 8, 8, wide2), axis=0)
            top = here if top is None else jnp.maximum(top, here)
        top = jnp.max(top, axis=0, keepdims=True)
        norm = None
        for start, size in chunks:
            e = jnp.exp2((s_s[start : start + size, :] - top) * exponent)
            s_s[start : start + size, :] = e
            here = jnp.sum(e.reshape(size // 8, 8, wide2), axis=0)
            norm = here if norm is None else norm + here
        inverse = 1.0 / jnp.sum(norm, axis=0, keepdims=True)
        for start, size in chunks:
            e = s_s[start : start + size, :] * inverse
            s_s[start : start + size, :] = e
            w_s[start : start + size, :] = e.astype(BF16)
        sides = []
        for b in range(2):
            cols = slice(b * BLOCK, (b + 1) * BLOCK)
            before, own = lists[b]
            sides.append(
                tn(v_s[before : before + BLOCK, :], w_s[0:BLOCK, cols])
                + tn(v_s[own : own + BLOCK, :], w_s[BLOCK:wide2, cols])
            )
        attended = jnp.concatenate(sides, axis=1)
        attended += tn(vn_s[0:near, :], w_s[wide2:far_from, :])
        attended += tn(vf_s[...], w_s[far_from:total, :])
        attended = attended.astype(BF16).astype(F32)
        o_s[q_rows, :] = attended.T.astype(BF16)
        row_dot = jnp.sum(g.astype(F32).T * attended, axis=0, keepdims=True)

        def put(start, size, cols, dprob, dot):
            d_s[start : start + size, cols] = (s_s[start : start + size, cols] * (dprob - dot)).astype(BF16)

        every = slice(0, wide2)
        for b in range(2):
            g_b = g[b * BLOCK : (b + 1) * BLOCK]
            cols = slice(b * BLOCK, (b + 1) * BLOCK)
            before, own = lists[b]
            put(0, BLOCK, cols, nt(v_s[before : before + BLOCK, :], g_b), row_dot[:, cols])
            put(BLOCK, BLOCK, cols, nt(v_s[own : own + BLOCK, :], g_b), row_dot[:, cols])
        put(wide2, near, every, nt(vn_s[0:near, :], g), row_dot)
        for i in range(0, FAR_ALL, BLOCK):
            put(far_from + i, BLOCK, every, nt(vf_s[i : i + BLOCK, :], g), row_dot)
        sides = []
        for b in range(2):
            cols = slice(b * BLOCK, (b + 1) * BLOCK)
            before, own = lists[b]
            q_b, g_b = q[cols], g[cols]
            sides.append(
                tn(k_s[before : before + BLOCK, :], d_s[0:BLOCK, cols])
                + tn(k_s[own : own + BLOCK, :], d_s[BLOCK:wide2, cols])
            )
            if before != own:
                dk_s[before : before + BLOCK, :] += nn(d_s[0:BLOCK, cols], q_b)
                dv_s[before : before + BLOCK, :] += nn(w_s[0:BLOCK, cols], g_b)
            dk_s[own : own + BLOCK, :] += nn(d_s[BLOCK:wide2, cols], q_b)
            dv_s[own : own + BLOCK, :] += nn(w_s[BLOCK:wide2, cols], g_b)
        grad_query = jnp.concatenate(sides, axis=1)
        grad_query += tn(kn_s[0:near, :], d_s[wide2:far_from, :])
        grad_query += tn(kf_s[...], d_s[far_from:total, :])
        dq_s[q_rows, :] = (grad_query * SCALE).T.astype(BF16)
        dkn_s[0:near, :] += nn(d_s[wide2:far_from, :], q)
        dvn_s[0:near, :] += nn(w_s[wide2:far_from, :], g)
        dkf_s[...] += nn(d_s[far_from:total, :], q)
        dvf_s[...] += nn(w_s[far_from:total, :], g)

    spread_near = spreading(NEAR_ROWS, NEAR)
    for block in range(WIDE):
        rows = slice(block * BLOCK, (block + 1) * BLOCK)
        near_rows = slice(block * NEAR_ROWS, (block + 1) * NEAR_ROWS)
        dk_s[rows, :] = (dk_s[rows, :] + nn(spread_near, dkn_s[near_rows, :].astype(BF16))) * SCALE
        dv_s[rows, :] = dv_s[rows, :] + nn(spread_near, dvn_s[near_rows, :].astype(BF16))
    for part, step in enumerate(STEPS):
        rows = pl.ds(pl.multiple_of(target(wide_at, step) * BLOCK, BLOCK), BLOCK)
        outs[part][0:BLOCK, :] = o_s[rows, :]
        outs[part][BLOCK : 2 * BLOCK, :] = dq_s[rows, :]
        outs[part][2 * BLOCK : 3 * BLOCK, :] = dk_s[rows, :].astype(BF16)
        outs[part][3 * BLOCK :, :] = dv_s[rows, :].astype(BF16)
    far_out[:, :SPAN_FAR, :] = (dkf_s[...] * SCALE).astype(BF16).reshape(NARROW, SPAN_FAR, HEAD_DIM)
    far_out[:, SPAN_FAR:, :] = dvf_s[...].astype(BF16).reshape(NARROW, SPAN_FAR, HEAD_DIM)


def attend(half, at, parts, far):
    n = len(STEPS)
    vmem = pl.BlockSpec(memory_space=pltpu.VMEM)
    bf = lambda rows: pltpu.VMEM((rows, HEAD_DIM), BF16)
    fl = lambda rows: pltpu.VMEM((rows, HEAD_DIM), F32)
    outs = pl.pallas_call(
        functools.partial(attend_kernel, half),
        out_shape=[jax.ShapeDtypeStruct((4 * BLOCK, HEAD_DIM), BF16)] * n
        + [jax.ShapeDtypeStruct((NARROW, 2 * SPAN_FAR, HEAD_DIM), BF16)],
        in_specs=[pl.BlockSpec(memory_space=pltpu.SMEM)] + [vmem] * (n + 1),
        out_specs=[vmem] * (n + 1),
        scratch_shapes=[bf(SPAN)] * 4 + [bf(SPAN_NEAR)] * 2 + [bf(FAR_ALL)] * 2 + [bf(SPAN)] * 2
        + [fl(SPAN)] * 2 + [fl(SPAN_NEAR)] * 2 + [fl(FAR_ALL)] * 2
        + [pltpu.VMEM((SPAN, 2 * BLOCK), F32), pltpu.VMEM((SPAN, 2 * BLOCK), BF16), pltpu.VMEM((SPAN, 2 * BLOCK), BF16)],
        compiler_params=pltpu.CompilerParams(vmem_limit_bytes=32 << 20),
        cost_estimate=pl.CostEstimate(flops=1_600_000_000, bytes_accessed=4 << 20, transcendentals=1 << 20),
        name=f"attend{half}",
    )(at, *parts, far)
    return outs[:n], outs[n]


def unpack_kernel(at_ref, *refs):
    n = len(STEPS)
    ins, far_ref, outs = refs[: 2 * n], refs[2 * n], refs[2 * n + 1 :]
    wide_at = at_ref[0]
    for part, step in enumerate(STEPS):
        block = source(wide_at, step)
        for half in range(2):
            columns = pl.ds(pl.multiple_of(block * PAIR + half * HEAD_DIM, HEAD_DIM), HEAD_DIM)
            piece = ins[half * n + part]
            outs[0][:, columns] = piece[0:BLOCK, :]
            outs[1][:, columns] = piece[BLOCK : 2 * BLOCK, :]
            far = far_ref[block, :, half * HEAD_DIM : (half + 1) * HEAD_DIM].astype(F32) * (1.0 / FAR)
            for i in range(2):
                terms = piece[(2 + i) * BLOCK : (3 + i) * BLOCK, :].astype(F32)
                rows = [
                    terms[r * FAR : (r + 1) * FAR] + far[i * FAR_ROWS + r : i * FAR_ROWS + r + 1]
                    for r in range(FAR_ROWS)
                ]
                outs[2 + i][:, columns] = jnp.concatenate(rows, axis=0).astype(BF16)


def unpack(at, parts, far):
    n = len(STEPS)
    vmem = pl.BlockSpec(memory_space=pltpu.VMEM)
    return pl.pallas_call(
        unpack_kernel,
        out_shape=[jax.ShapeDtypeStruct((BLOCK, FEAT), BF16)] * 4,
        in_specs=[pl.BlockSpec(memory_space=pltpu.SMEM)] + [vmem] * (2 * n + 1),
        out_specs=[vmem] * 4,
        compiler_params=pltpu.CompilerParams(vmem_limit_bytes=24 << 20),
        name="unpack",
    )(at, *parts, far)


def shards(queries, keys, values, grad_out):
    at = jnp.stack([lax.axis_index("wide"), lax.axis_index("narrow")]).astype(jnp.int32)
    first, second, far = pack(at, queries, keys, values, grad_out)
    first = send(first)
    far = lax.all_to_all(far, "wide", 0, 0, tiled=True)
    far = far.reshape(WIDE, 2, FAR_ROWS, PAIR).transpose(1, 0, 2, 3).reshape(1, 2 * SPAN_FAR, PAIR)
    far = jnp.broadcast_to(far, (NARROW, 2 * SPAN_FAR, PAIR))
    far = lax.all_to_all(far, "narrow", 0, 0, tiled=True)
    chained = lax.optimization_barrier(tuple(first) + tuple(second))
    first, second = list(chained[: len(STEPS)]), list(chained[len(STEPS) :])
    second = send(second)
    first, far_first = attend(0, at, first, far)
    first = send(first)
    second, far_second = attend(1, at, second, far)
    second = send(second)
    far = jnp.concatenate([far_first, far_second], axis=2)
    far = lax.all_to_all(far, "narrow", 0, 0, tiled=True)
    far = jnp.sum(far.astype(F32), axis=0).astype(BF16)
    far = far.reshape(2, WIDE, FAR_ROWS, PAIR).transpose(1, 0, 2, 3).reshape(WIDE, 2 * FAR_ROWS, PAIR)
    far = lax.all_to_all(far, "wide", 0, 0, tiled=True)
    return tuple(unpack(at, list(first) + list(second), far))


def solution(mesh):
    rows = P(("narrow", "wide"), None)
    return jax.shard_map(
        shards, mesh=mesh, in_specs=(rows,) * 4, out_specs=(rows,) * 4, check_vma=False
    )
```

time: 1020 us -> 181 us (0.18)
  waiting for transfers between devices: 830 us -> 67.5 us
  local copies, waits for them, and re-layouts: 105 us -> 14.8 us
  starting transfers between devices: 8.76 us -> 63.8 us
  other arithmetic: 33.5 us -> 2.07 us
  matrix products: 25.7 us -> 0 us
  Pallas kernels: 0 us -> 16.1 us
  blocking collectives: 0 us -> 15.2 us
  between operations: 14.1 us -> 0.77 us
    reduce_scatter x4 -> x0, waiting for transfers between devices: 390 us -> none  [the longest x1 171 us: shards(): lax.psum_scatter(far_k_terms.astype(jnp.bfloat16), 'narrow', scatter_dime...]
    all_gather x4 -> x0, waiting for transfers between devices: 368 us -> none  [the longest x1 163 us: shards(): lax.all_gather(group_keys, 'narrow', axis=0, tiled=True)]
    unnamed x10 -> x0, waiting for transfers between devices: 71.8 us -> none
    ppermute x4 -> x28, waiting for transfers between devices: 0.01 us -> 61.3 us  [send(): lax.ppermute(b, 'wide', [(s, target(s, step)) for s in range(WIDE)])]
    dynamic_slice x64 -> x0, local copies, waits for them, and re-layouts: 36 us -> none  [the longest x16 10.3 us: pair_step(): lax.dynamic_slice_in_dim(value_list, column_start, pair_width, 1)]
    ppermute x4 -> x28, starting transfers between devices: 8.21 us -> 42.7 us  [send(): lax.ppermute(b, 'wide', [(s, target(s, step)) for s in range(WIDE)])]
    dot_general x48 -> x0, matrix products: 25.7 us -> none  [the longest x8 11.8 us: pair_step(): jnp.einsum('qhd,khd->hqk', query_pair, key_pair, preferred_element_type=j...]
    dynamic_update_slice x48 -> x0, local copies, waits for them, and re-layouts: 24.7 us -> none  [the longest x16 15 us: pair_step(): lax.dynamic_update_slice_in_dim(dv_acc, value_terms.reshape(key_count, pa...]
  transfers between devices with their start and end apart: 13 -> 31, of which waited for: 9 -> 15; matrix products, arithmetic and copies ran while one was open for 5% -> 1% of each run, Pallas kernels for 0% -> 0%
where the time goes in v1:
time: 181 us; the launch traced here: 180 us
  waiting for transfers between devices  67.5 us (37%)
  starting transfers between devices  63.8 us (35%)
  Pallas kernels  16.1 us (9%)
  blocking collectives  15.2 us (8%)
  local copies, waits for them, and re-layouts  14.8 us (8%)
  other arithmetic  2.07 us (1%)
    ppermute x28, waiting for transfers between devices, send(): lax.ppermute(b, 'wide', [(s, target(s, step)) for s in range(WIDE)])  61.3 us
    ppermute x28, starting transfers between devices, send(): lax.ppermute(b, 'wide', [(s, target(s, step)) for s in range(WIDE)])  42.7 us
    all_to_all x2, starting transfers between devices, shards(): far = lax.all_to_all(far, 'narrow', 0, 0, tiled=True)  16.9 us
    all_to_all x1, blocking collectives, shards(): far = lax.all_to_all(far, 'wide', 0, 0, tiled=True)  15.2 us
    unnamed x36, local copies, waits for them, and re-layouts  13.3 us
    pallas_call x2, Pallas kernels, attend(): pl.pallas_call(functools.partial(attend_kernel, half), out_shape=[jax.Sha...  12.2 us
    all_to_all x1, waiting for transfers between devices, shards(): far = lax.all_to_all(far, 'wide', 0, 0, tiled=True)  6.21 us
    all_to_all x1, starting transfers between devices, shards(): far = lax.all_to_all(far, 'wide', 0, 0, tiled=True)  4.23 us
  transfers between devices with their start and end apart: 31, of which 15 were waited for; matrix products, arithmetic and copies ran while one was open for 1% of the time, Pallas kernels for 0%

profile of v1, /device:TPU:34, one launch (start us, length us, event | category | flops | bytes accessed | tf_op | source)
XLA Modules:
  0.0 180.2 jit_solution(604154928916329038)
XLA Ops:
  0.7 1.0 copy-done
  1.8 1.0 copy-done.1
  2.8 1.0 copy-done.2
  3.8 1.0 copy-done.3
  4.9 1.4 pack.1
  6.3 15.2 %all_to_all.20 = bf16[8,4,256]{2,1,0:T(4,128)(2,1)S(1)} all-to-all(bf16[8,4,256]{2,1,0:T(4,128)(2,1)S(1)} %get-tuple-element.79), channel_id=1, replica_groups=mesh['wide'=8,'narrow'=32] {'wide'}, dimensions={0} | all-to-all | bytes 32768 | tf_op jit(solution)/shard_map/all_to_all | solution.py:313
  22.4 8.5 %all-to-all-start.1 = ((bf16[32,32,256]{2,1,0:T(8,128)(2,1)}), bf16[32,32,256]{2,1,0:T(8,128)(2,1)S(1)}, u32[]{:S(2)}, u32[]{:S(2)}) async-start(bf16[32,32,256]{2,1,0:T(8,128)(2,1)} %broadcast_in_dim.8), calls=%async_computation.1 | async-start | bytes 1048576 | tf_op jit(solution)/shard_map/all_to_all | solution.py:316
  31.5 4.0 %collective-permute-start.1 = (bf16[512,128]{1,0:T(8,128)(2,1)S(1)}, bf16[512,128]{1,0:T(8,128)(2,1)S(1)}, u32[]{:S(2)}, u32[]{:S(2)}) collective-permute-start(bf16[512,128]{1,0:T(8,128)(2,1)S(1)} %get-tuple-element.56), channel_id=1, source_target_pairs={{0,160},{32,128},{64,224},{96,192},{128,32},{160,0},{192,96},{224,... | collective-permute-start | bytes 393224 | tf_op jit(solution)/shard_map/ppermute | solution.py:46
  36.3 3.4 %collective-permute-start.3 = (bf16[512,128]{1,0:T(8,128)(2,1)S(1)}, bf16[512,128]{1,0:T(8,128)(2,1)S(1)}, u32[]{:S(2)}, u32[]{:S(2)}) collective-permute-start(bf16[512,128]{1,0:T(8,128)(2,1)S(1)} %get-tuple-element.58), channel_id=1, source_target_pairs={{0,192},{32,224},{64,0},{96,32},{128,64},{160,96},{192,128},{224,1... | collective-permute-start | bytes 393224 | tf_op jit(solution)/shard_map/ppermute | solution.py:46
  39.7 5.7 %collective-permute-done.refs_0_ = bf16[512,128]{1,0:T(8,128)(2,1)S(1)} collective-permute-done((bf16[512,128]{1,0:T(8,128)(2,1)S(1)}, bf16[512,128]{1,0:T(8,128)(2,1)S(1)}, u32[]{:S(2)}, u32[]{:S(2)}) %collective-permute-start) | collective-permute-done | bytes 131104 | tf_op jit(solution)/shard_map/ppermute | solution.py:46
  45.4 3.7 %collective-permute-done.1.refs_1_ = bf16[512,128]{1,0:T(8,128)(2,1)S(1)} collective-permute-done((bf16[512,128]{1,0:T(8,128)(2,1)S(1)}, bf16[512,128]{1,0:T(8,128)(2,1)S(1)}, u32[]{:S(2)}, u32[]{:S(2)}) %collective-permute-start.1) | collective-permute-done | bytes 131104 | tf_op jit(solution)/shard_map/ppermute | solution.py:46
  49.6 7.2 %collective-permute-done.2.refs_2_ = bf16[512,128]{1,0:T(8,128)(2,1)S(1)} collective-permute-done((bf16[512,128]{1,0:T(8,128)(2,1)S(1)}, bf16[512,128]{1,0:T(8,128)(2,1)S(1)}, u32[]{:S(2)}, u32[]{:S(2)}) %collective-permute-start.2) | collective-permute-done | bytes 131104 | tf_op jit(solution)/shard_map/ppermute | solution.py:46
  56.8 3.1 %collective-permute-done.4.refs_4_ = bf16[512,128]{1,0:T(8,128)(2,1)S(1)} collective-permute-done((bf16[512,128]{1,0:T(8,128)(2,1)S(1)}, bf16[512,128]{1,0:T(8,128)(2,1)S(1)}, u32[]{:S(2)}, u32[]{:S(2)}) %collective-permute-start.4) | collective-permute-done | bytes 131104 | tf_op jit(solution)/shard_map/ppermute | solution.py:46
  59.9 3.3 %collective-permute-start.14 = (bf16[512,128]{1,0:T(8,128)(2,1)S(1)}, bf16[512,128]{1,0:T(8,128)(2,1)S(1)}, u32[]{:S(2)}, u32[]{:S(2)}) collective-permute-start(bf16[512,128]{1,0:T(8,128)(2,1)S(1)} %get-tuple-element.88), channel_id=1, source_target_pairs={{0,128},{32,160},{64,192},{96,224},{128,0},{160,32},{192,64},{224,... | collective-permute-start | bytes 393224 | tf_op jit(solution)/shard_map/ppermute | solution.py:46
  63.2 2.0 %collective-permute-start.15 = (bf16[512,128]{1,0:T(8,128)(2,1)S(1)}, bf16[512,128]{1,0:T(8,128)(2,1)S(1)}, u32[]{:S(2)}, u32[]{:S(2)}) collective-permute-start(bf16[512,128]{1,0:T(8,128)(2,1)S(1)} %get-tuple-element.89), channel_id=1, source_target_pairs={{0,160},{32,128},{64,224},{96,192},{128,32},{160,0},{192,96},{224,... | collective-permute-start | bytes 393224 | tf_op jit(solution)/shard_map/ppermute | solution.py:46
  65.2 1.7 collective-permute-start.16
  66.9 2.4 %collective-permute-start.17 = (bf16[512,128]{1,0:T(8,128)(2,1)S(1)}, bf16[512,128]{1,0:T(8,128)(2,1)S(1)}, u32[]{:S(2)}, u32[]{:S(2)}) collective-permute-start(bf16[512,128]{1,0:T(8,128)(2,1)S(1)} %get-tuple-element.91), channel_id=1, source_target_pairs={{0,192},{32,224},{64,0},{96,32},{128,64},{160,96},{192,128},{224,1... | collective-permute-start | bytes 393224 | tf_op jit(solution)/shard_map/ppermute | solution.py:46
  69.7 5.7 %collective-permute-done.14.refs_0_ = bf16[512,128]{1,0:T(8,128)(2,1)S(1)} collective-permute-done((bf16[512,128]{1,0:T(8,128)(2,1)S(1)}, bf16[512,128]{1,0:T(8,128)(2,1)S(1)}, u32[]{:S(2)}, u32[]{:S(2)}) %collective-permute-start.14) | collective-permute-done | bytes 131104 | tf_op jit(solution)/shard_map/ppermute | solution.py:46
  75.4 1.4 collective-permute-done.15.refs_1_
  76.8 1.7 collective-permute-start.20
  78.5 6.9 %collective-permute-done.16.refs_2_ = bf16[512,128]{1,0:T(8,128)(2,1)S(1)} collective-permute-done((bf16[512,128]{1,0:T(8,128)(2,1)S(1)}, bf16[512,128]{1,0:T(8,128)(2,1)S(1)}, u32[]{:S(2)}, u32[]{:S(2)}) %collective-permute-start.16) | collective-permute-done | bytes 131104 | tf_op jit(solution)/shard_map/ppermute | solution.py:46
  86.7 1.5 collective-permute-done.18.refs_4_
  90.2 0.9 copy-done.9
  91.1 0.9 copy-done.11
  92.0 0.9 copy-done.13
  92.9 0.9 copy-done.15
  93.8 0.9 copy-done.17
  94.7 6.1 %attend1.1 = (bf16[512,128]{1,0:T(8,128)(2,1)S(1)}, bf16[512,128]{1,0:T(8,128)(2,1)S(1)}, bf16[512,128]{1,0:T(8,128)(2,1)S(1)}, bf16[512,128]{1,0:T(8,128)(2,1)S...) custom-call(s32[2]{0:T(128)S(1)} %pad_add_fusion.at_ref, ...), custom_call_target="tpu_custom_call" | custom-call | flops 1600000000 | bytes 4194304 | tf_op jit(solution)/shard_map/attend1/pallas_call | solution.py:259
  102.1 6.1 %attend0.1 = (bf16[512,128]{1,0:T(8,128)(2,1)S(1)}, bf16[512,128]{1,0:T(8,128)(2,1)S(1)}, bf16[512,128]{1,0:T(8,128)(2,1)S(1)}, bf16[512,128]{1,0:T(8,128)(2,1)S...) custom-call(s32[2]{0:T(128)S(1)} %pad_add_fusion.at_ref, ...), custom_call_target="tpu_custom_call" | custom-call | flops 1600000000 | bytes 4194304 | tf_op jit(solution)/shard_map/attend0/pallas_call | solution.py:259
  108.2 0.9 pad_maximum_fusion
  109.1 8.4 %all-to-all-start.2 = ((bf16[32,32,256]{2,1,0:T(8,128)(2,1)}), bf16[32,32,256]{2,1,0:T(8,128)(2,1)}, u32[]{:S(2)}, u32[]{:S(2)}) async-start(bf16[32,32,256]{2,1,0:T(8,128)(2,1)} %pad_maximum_fusion), calls=%async_computation.2 | async-start | bytes 1048576 | tf_op jit(solution)/shard_map/all_to_all | solution.py:325
  117.5 4.3 %collective-permute-start.21 = (bf16[512,128]{1,0:T(8,128)(2,1)S(1)}, bf16[512,128]{1,0:T(8,128)(2,1)S(1)}, u32[]{:S(2)}, u32[]{:S(2)}) collective-permute-start(bf16[512,128]{1,0:T(8,128)(2,1)S(1)} %copy-done.7), channel_id=1, source_target_pairs={{0,128},{32,160},{64,192},{96,224},{128,0},{160,32},{192,64},{224,... | collective-permute-start | bytes 393224 | tf_op jit(solution)/shard_map/ppermute | solution.py:46
  122.4 1.3 collective-permute-start.23
  123.7 2.9 %collective-permute-start.24 = (bf16[512,128]{1,0:T(8,128)(2,1)S(1)}, bf16[512,128]{1,0:T(8,128)(2,1)S(1)}, u32[]{:S(2)}, u32[]{:S(2)}) collective-permute-start(bf16[512,128]{1,0:T(8,128)(2,1)S(1)} %get-tuple-element.99), channel_id=1, source_target_pairs={{0,192},{32,224},{64,0},{96,32},{128,64},{160,96},{192,128},{224,1... | collective-permute-start | bytes 393224 | tf_op jit(solution)/shard_map/ppermute | solution.py:46
  126.5 1.2 collective-permute-start.25
  127.7 9.8 %collective-permute-done.21.refs_8_ = bf16[512,128]{1,0:T(8,128)(2,1)S(1)} collective-permute-done((bf16[512,128]{1,0:T(8,128)(2,1)S(1)}, bf16[512,128]{1,0:T(8,128)(2,1)S(1)}, u32[]{:S(2)}, u32[]{:S(2)}) %collective-permute-start.21) | collective-permute-done | bytes 131104 | tf_op jit(solution)/shard_map/ppermute | solution.py:46
  138.2 2.2 %collective-permute-start.27 = (bf16[512,128]{1,0:T(8,128)(2,1)S(1)}, bf16[512,128]{1,0:T(8,128)(2,1)S(1)}, u32[]{:S(2)}, u32[]{:S(2)}) collective-permute-start(bf16[512,128]{1,0:T(8,128)(2,1)S(1)} %get-tuple-element.102), channel_id=1, source_target_pairs={{0,32},{32,0},{64,96},{96,64},{128,160},{160,128},{192,224},{224,1... | collective-permute-start | bytes 393224 | tf_op jit(solution)/shard_map/ppermute | solution.py:46
  140.4 6.5 %collective-permute-done.23.refs_10_ = bf16[512,128]{1,0:T(8,128)(2,1)S(1)} collective-permute-done((bf16[512,128]{1,0:T(8,128)(2,1)S(1)}, bf16[512,128]{1,0:T(8,128)(2,1)S(1)}, u32[]{:S(2)}, u32[]{:S(2)}) %collective-permute-start.23) | collective-permute-done | bytes 131104 | tf_op jit(solution)/shard_map/ppermute | solution.py:46
  146.9 1.2 collective-permute-start.7
  148.1 4.0 %collective-permute-start.8 = (bf16[512,128]{1,0:T(8,128)(2,1)S(1)}, bf16[512,128]{1,0:T(8,128)(2,1)S(1)}, u32[]{:S(2)}, u32[]{:S(2)}) collective-permute-start(bf16[512,128]{1,0:T(8,128)(2,1)S(1)} %get-tuple-element.81), channel_id=1, source_target_pairs={{0,160},{32,128},{64,224},{96,192},{128,32},{160,0},{192,96},{224,... | collective-permute-start | bytes 393224 | tf_op jit(solution)/shard_map/ppermute | solution.py:46
  152.2 4.1 %collective-permute-start.10 = (bf16[512,128]{1,0:T(8,128)(2,1)S(1)}, bf16[512,128]{1,0:T(8,128)(2,1)S(1)}, u32[]{:S(2)}, u32[]{:S(2)}) collective-permute-start(bf16[512,128]{1,0:T(8,128)(2,1)S(1)} %get-tuple-element.83), channel_id=1, source_target_pairs={{0,192},{32,224},{64,0},{96,32},{128,64},{160,96},{192,128},{224,1... | collective-permute-start | bytes 393224 | tf_op jit(solution)/shard_map/ppermute | solution.py:46
  156.3 4.9 %collective-permute-done.7.refs_0_ = bf16[512,128]{1,0:T(8,128)(2,1)S(1)} collective-permute-done((bf16[512,128]{1,0:T(8,128)(2,1)S(1)}, bf16[512,128]{1,0:T(8,128)(2,1)S(1)}, u32[]{:S(2)}, u32[]{:S(2)}) %collective-permute-start.7) | collective-permute-done | bytes 131104 | tf_op jit(solution)/shard_map/ppermute | solution.py:46
  161.2 2.6 %collective-permute-done.8.refs_1_ = bf16[512,128]{1,0:T(8,128)(2,1)S(1)} collective-permute-done((bf16[512,128]{1,0:T(8,128)(2,1)S(1)}, bf16[512,128]{1,0:T(8,128)(2,1)S(1)}, u32[]{:S(2)}, u32[]{:S(2)}) %collective-permute-start.8) | collective-permute-done | bytes 131104 | tf_op jit(solution)/shard_map/ppermute | solution.py:46
  163.9 1.1 reduce_sum.12
  165.7 4.2 %all-to-all-start.3 = ((bf16[8,4,256]{2,1,0:T(4,128)(2,1)}), bf16[8,4,256]{2,1,0:T(4,128)(2,1)S(1)}, u32[]{:S(2)}, u32[]{:S(2)}) async-start(bf16[8,4,256]{2,1,0:T(4,128)(2,1)} %reshape.21), calls=%async_computation.3 | async-start | bytes 32768 | tf_op jit(solution)/shard_map/all_to_all | solution.py:328
  170.0 1.5 collective-permute-done.11.refs_4_
  171.5 6.2 %all-to-all-done.3.refs_16_ = bf16[8,4,256]{2,1,0:T(4,128)(2,1)S(1)} async-done(((bf16[8,4,256]{2,1,0:T(4,128)(2,1)}), bf16[8,4,256]{2,1,0:T(4,128)(2,1)S(1)}, u32[]{:S(2)}, u32[]{:S(2)}) %all-to-all-start.3) | async-done | bytes 16416 | tf_op jit(solution)/shard_map/all_to_all | solution.py:328
  177.7 2.5 %unpack.1 = (bf16[128,2048]{1,0:T(8,128)(2,1)}, bf16[128,2048]{1,0:T(8,128)(2,1)}, bf16[128,2048]{1,0:T(8,128)(2,1)}, bf16[128,2048]{1,0:T(8,128)(2,1)}) custom-call(s32[2]{0:T(128)S(1)} %pad_add_fusion.at_ref, bf16[512,128]{1,0:T(8,128)(2,1)S(1)} %collective-permute-done.7.refs_0_, bf16[512,128]{1,0:T(8,128)(2,1)S(1)} %collective-permute-done.8.refs_1_, ...), custom_call_target="tpu_custom_call" | custom-call | tf_op jit(solution)/shard_map/unpack/pallas_call | solution.py:299
  (65 shorter events, 9.8 us)
Async XLA Ops:
  0.7 1.0 copy-start
  1.8 1.0 copy-start.1
  2.8 1.0 copy-start.2
  3.8 1.0 copy-start.3
  22.4 67.8 %all-to-all-start.1 = ((bf16[32,32,256]{2,1,0:T(8,128)(2,1)}), bf16[32,32,256]{2,1,0:T(8,128)(2,1)S(1)}, u32[]{:S(2)}, u32[]{:S(2)}) async-start(bf16[32,32,256]{2,1,0:T(8,128)(2,1)} %broadcast_in_dim.8), calls=%async_computation.1 | async-start | bytes 1048576 | tf_op jit(solution)/shard_map/all_to_all | solution.py:316
  30.9 14.5 %collective-permute-start = (bf16[512,128]{1,0:T(8,128)(2,1)S(1)}, bf16[512,128]{1,0:T(8,128)(2,1)S(1)}, u32[]{:S(2)}, u32[]{:S(2)}) collective-permute-start(bf16[512,128]{1,0:T(8,128)(2,1)S(1)} %get-tuple-element.55), channel_id=1, source_target_pairs={{0,128},{32,160},{64,192},{96,224},{128,0},{160,32},{192,64},{224,... | collective-permute-start | bytes 393224 | tf_op jit(solution)/shard_map/ppermute | solution.py:46
  31.5 17.6 %collective-permute-start.1 = (bf16[512,128]{1,0:T(8,128)(2,1)S(1)}, bf16[512,128]{1,0:T(8,128)(2,1)S(1)}, u32[]{:S(2)}, u32[]{:S(2)}) collective-permute-start(bf16[512,128]{1,0:T(8,128)(2,1)S(1)} %get-tuple-element.56), channel_id=1, source_target_pairs={{0,160},{32,128},{64,224},{96,192},{128,32},{160,0},{192,96},{224,... | collective-permute-start | bytes 393224 | tf_op jit(solution)/shard_map/ppermute | solution.py:46
  35.5 21.3 %collective-permute-start.2 = (bf16[512,128]{1,0:T(8,128)(2,1)S(1)}, bf16[512,128]{1,0:T(8,128)(2,1)S(1)}, u32[]{:S(2)}, u32[]{:S(2)}) collective-permute-start(bf16[512,128]{1,0:T(8,128)(2,1)S(1)} %get-tuple-element.57), channel_id=1, source_target_pairs={{0,64},{32,96},{64,128},{96,160},{128,192},{160,224},{192,0},{224,... | collective-permute-start | bytes 393224 | tf_op jit(solution)/shard_map/ppermute | solution.py:46
  36.3 20.5 %collective-permute-start.3 = (bf16[512,128]{1,0:T(8,128)(2,1)S(1)}, bf16[512,128]{1,0:T(8,128)(2,1)S(1)}, u32[]{:S(2)}, u32[]{:S(2)}) collective-permute-start(bf16[512,128]{1,0:T(8,128)(2,1)S(1)} %get-tuple-element.58), channel_id=1, source_target_pairs={{0,192},{32,224},{64,0},{96,32},{128,64},{160,96},{192,128},{224,1... | collective-permute-start | bytes 393224 | tf_op jit(solution)/shard_map/ppermute | solution.py:46
  39.7 20.2 %collective-permute-start.4 = (bf16[512,128]{1,0:T(8,128)(2,1)S(1)}, bf16[512,128]{1,0:T(8,128)(2,1)S(1)}, u32[]{:S(2)}, u32[]{:S(2)}) collective-permute-start(bf16[512,128]{1,0:T(8,128)(2,1)S(1)} %get-tuple-element.59), channel_id=1, source_target_pairs={{0,96},{32,64},{64,160},{96,128},{128,224},{160,192},{192,32},{224... | collective-permute-start | bytes 393224 | tf_op jit(solution)/shard_map/ppermute | solution.py:46
  45.4 14.5 %collective-permute-start.5 = (bf16[512,128]{1,0:T(8,128)(2,1)S(1)}, bf16[512,128]{1,0:T(8,128)(2,1)S(1)}, u32[]{:S(2)}, u32[]{:S(2)}) collective-permute-start(bf16[512,128]{1,0:T(8,128)(2,1)S(1)} %get-tuple-element.60), channel_id=1, source_target_pairs={{0,224},{32,192},{64,32},{96,0},{128,96},{160,64},{192,160},{224,1... | collective-permute-start | bytes 393224 | tf_op jit(solution)/shard_map/ppermute | solution.py:46
  49.1 10.8 %collective-permute-start.6 = (bf16[512,128]{1,0:T(8,128)(2,1)S(1)}, bf16[512,128]{1,0:T(8,128)(2,1)S(1)}, u32[]{:S(2)}, u32[]{:S(2)}) collective-permute-start(bf16[512,128]{1,0:T(8,128)(2,1)S(1)} %get-tuple-element.61), channel_id=1, source_target_pairs={{0,32},{32,0},{64,96},{96,64},{128,160},{160,128},{192,224},{224,1... | collective-permute-start | bytes 393224 | tf_op jit(solution)/shard_map/ppermute | solution.py:46
  59.9 15.5 %collective-permute-start.14 = (bf16[512,128]{1,0:T(8,128)(2,1)S(1)}, bf16[512,128]{1,0:T(8,128)(2,1)S(1)}, u32[]{:S(2)}, u32[]{:S(2)}) collective-permute-start(bf16[512,128]{1,0:T(8,128)(2,1)S(1)} %get-tuple-element.88), channel_id=1, source_target_pairs={{0,128},{32,160},{64,192},{96,224},{128,0},{160,32},{192,64},{224,... | collective-permute-start | bytes 393224 | tf_op jit(solution)/shard_map/ppermute | solution.py:46
  63.2 13.6 %collective-permute-start.15 = (bf16[512,128]{1,0:T(8,128)(2,1)S(1)}, bf16[512,128]{1,0:T(8,128)(2,1)S(1)}, u32[]{:S(2)}, u32[]{:S(2)}) collective-permute-start(bf16[512,128]{1,0:T(8,128)(2,1)S(1)} %get-tuple-element.89), channel_id=1, source_target_pairs={{0,160},{32,128},{64,224},{96,192},{128,32},{160,0},{192,96},{224,... | collective-permute-start | bytes 393224 | tf_op jit(solution)/shard_map/ppermute | solution.py:46
  65.2 20.2 %collective-permute-start.16 = (bf16[512,128]{1,0:T(8,128)(2,1)S(1)}, bf16[512,128]{1,0:T(8,128)(2,1)S(1)}, u32[]{:S(2)}, u32[]{:S(2)}) collective-permute-start(bf16[512,128]{1,0:T(8,128)(2,1)S(1)} %get-tuple-element.90), channel_id=1, source_target_pairs={{0,64},{32,96},{64,128},{96,160},{128,192},{160,224},{192,0},{224,... | collective-permute-start | bytes 393224 | tf_op jit(solution)/shard_map/ppermute | solution.py:46
  66.9 19.2 %collective-permute-start.17 = (bf16[512,128]{1,0:T(8,128)(2,1)S(1)}, bf16[512,128]{1,0:T(8,128)(2,1)S(1)}, u32[]{:S(2)}, u32[]{:S(2)}) collective-permute-start(bf16[512,128]{1,0:T(8,128)(2,1)S(1)} %get-tuple-element.91), channel_id=1, source_target_pairs={{0,192},{32,224},{64,0},{96,32},{128,64},{160,96},{192,128},{224,1... | collective-permute-start | bytes 393224 | tf_op jit(solution)/shard_map/ppermute | solution.py:46
  69.3 18.9 %collective-permute-start.18 = (bf16[512,128]{1,0:T(8,128)(2,1)S(1)}, bf16[512,128]{1,0:T(8,128)(2,1)S(1)}, u32[]{:S(2)}, u32[]{:S(2)}) collective-permute-start(bf16[512,128]{1,0:T(8,128)(2,1)S(1)} %get-tuple-element.92), channel_id=1, source_target_pairs={{0,96},{32,64},{64,160},{96,128},{128,224},{160,192},{192,32},{224... | collective-permute-start | bytes 393224 | tf_op jit(solution)/shard_map/ppermute | solution.py:46
  75.4 13.5 %collective-permute-start.19 = (bf16[512,128]{1,0:T(8,128)(2,1)S(1)}, bf16[512,128]{1,0:T(8,128)(2,1)S(1)}, u32[]{:S(2)}, u32[]{:S(2)}) collective-permute-start(bf16[512,128]{1,0:T(8,128)(2,1)S(1)} %get-tuple-element.93), channel_id=1, source_target_pairs={{0,224},{32,192},{64,32},{96,0},{128,96},{160,64},{192,160},{224,1... | collective-permute-start | bytes 393224 | tf_op jit(solution)/shard_map/ppermute | solution.py:46
  76.8 12.7 %collective-permute-start.20 = (bf16[512,128]{1,0:T(8,128)(2,1)S(1)}, bf16[512,128]{1,0:T(8,128)(2,1)S(1)}, u32[]{:S(2)}, u32[]{:S(2)}) collective-permute-start(bf16[512,128]{1,0:T(8,128)(2,1)S(1)} %get-tuple-element.94), channel_id=1, source_target_pairs={{0,32},{32,0},{64,96},{96,64},{128,160},{160,128},{192,224},{224,1... | collective-permute-start | bytes 393224 | tf_op jit(solution)/shard_map/ppermute | solution.py:46
  85.4 0.7 copy-start.8
  86.1 0.7 copy-start.10
  88.2 0.7 copy-start.12
  89.5 0.7 copy-start.16
  90.2 0.9 copy-start.9
  91.1 0.9 copy-start.11
  92.0 0.9 copy-start.13
  92.9 0.9 copy-start.15
  93.8 0.9 copy-start.17
  100.8 0.7 copy-start.4
  101.5 0.7 copy-start.6
  109.1 8.4 %copy-start.7 = (bf16[512,128]{1,0:T(8,128)(2,1)S(1)}, bf16[512,128]{1,0:T(8,128)(2,1)}, u32[]{:S(2)}) copy-start(bf16[512,128]{1,0:T(8,128)(2,1)} %copy-done.6) | copy-start | bytes 393220
  109.1 12.7 %copy-start.5 = (bf16[512,128]{1,0:T(8,128)(2,1)S(1)}, bf16[512,128]{1,0:T(8,128)(2,1)}, u32[]{:S(2)}) copy-start(bf16[512,128]{1,0:T(8,128)(2,1)} %copy-done.4) | copy-start | bytes 393220
  109.1 54.8 %all-to-all-start.2 = ((bf16[32,32,256]{2,1,0:T(8,128)(2,1)}), bf16[32,32,256]{2,1,0:T(8,128)(2,1)}, u32[]{:S(2)}, u32[]{:S(2)}) async-start(bf16[32,32,256]{2,1,0:T(8,128)(2,1)} %pad_maximum_fusion), calls=%async_computation.2 | async-start | bytes 1048576 | tf_op jit(solution)/shard_map/all_to_all | solution.py:325
  117.5 20.1 %collective-permute-start.21 = (bf16[512,128]{1,0:T(8,128)(2,1)S(1)}, bf16[512,128]{1,0:T(8,128)(2,1)S(1)}, u32[]{:S(2)}, u32[]{:S(2)}) collective-permute-start(bf16[512,128]{1,0:T(8,128)(2,1)S(1)} %copy-done.7), channel_id=1, source_target_pairs={{0,128},{32,160},{64,192},{96,224},{128,0},{160,32},{192,64},{224,... | collective-permute-start | bytes 393224 | tf_op jit(solution)/shard_map/ppermute | solution.py:46
  121.8 16.4 %collective-permute-start.22 = (bf16[512,128]{1,0:T(8,128)(2,1)S(1)}, bf16[512,128]{1,0:T(8,128)(2,1)S(1)}, u32[]{:S(2)}, u32[]{:S(2)}) collective-permute-start(bf16[512,128]{1,0:T(8,128)(2,1)S(1)} %copy-done.5), channel_id=1, source_target_pairs={{0,160},{32,128},{64,224},{96,192},{128,32},{160,0},{192,96},{224,... | collective-permute-start | bytes 393224 | tf_op jit(solution)/shard_map/ppermute | solution.py:46
  122.4 24.5 %collective-permute-start.23 = (bf16[512,128]{1,0:T(8,128)(2,1)S(1)}, bf16[512,128]{1,0:T(8,128)(2,1)S(1)}, u32[]{:S(2)}, u32[]{:S(2)}) collective-permute-start(bf16[512,128]{1,0:T(8,128)(2,1)S(1)} %get-tuple-element.98), channel_id=1, source_target_pairs={{0,64},{32,96},{64,128},{96,160},{128,192},{160,224},{192,0},{224,... | collective-permute-start | bytes 393224 | tf_op jit(solution)/shard_map/ppermute | solution.py:46
  123.7 24.5 %collective-permute-start.24 = (bf16[512,128]{1,0:T(8,128)(2,1)S(1)}, bf16[512,128]{1,0:T(8,128)(2,1)S(1)}, u32[]{:S(2)}, u32[]{:S(2)}) collective-permute-start(bf16[512,128]{1,0:T(8,128)(2,1)S(1)} %get-tuple-element.99), channel_id=1, source_target_pairs={{0,192},{32,224},{64,0},{96,32},{128,64},{160,96},{192,128},{224,1... | collective-permute-start | bytes 393224 | tf_op jit(solution)/shard_map/ppermute | solution.py:46
  126.5 25.6 %collective-permute-start.25 = (bf16[512,128]{1,0:T(8,128)(2,1)S(1)}, bf16[512,128]{1,0:T(8,128)(2,1)S(1)}, u32[]{:S(2)}, u32[]{:S(2)}) collective-permute-start(bf16[512,128]{1,0:T(8,128)(2,1)S(1)} %get-tuple-element.100), channel_id=1, source_target_pairs={{0,96},{32,64},{64,160},{96,128},{128,224},{160,192},{192,32},{224... | collective-permute-start | bytes 393224 | tf_op jit(solution)/shard_map/ppermute | solution.py:46
  137.5 14.6 %collective-permute-start.26 = (bf16[512,128]{1,0:T(8,128)(2,1)S(1)}, bf16[512,128]{1,0:T(8,128)(2,1)S(1)}, u32[]{:S(2)}, u32[]{:S(2)}) collective-permute-start(bf16[512,128]{1,0:T(8,128)(2,1)S(1)} %get-tuple-element.101), channel_id=1, source_target_pairs={{0,224},{32,192},{64,32},{96,0},{128,96},{160,64},{192,160},{224,1... | collective-permute-start | bytes 393224 | tf_op jit(solution)/shard_map/ppermute | solution.py:46
  138.2 18.1 %collective-permute-start.27 = (bf16[512,128]{1,0:T(8,128)(2,1)S(1)}, bf16[512,128]{1,0:T(8,128)(2,1)S(1)}, u32[]{:S(2)}, u32[]{:S(2)}) collective-permute-start(bf16[512,128]{1,0:T(8,128)(2,1)S(1)} %get-tuple-element.102), channel_id=1, source_target_pairs={{0,32},{32,0},{64,96},{96,64},{128,160},{160,128},{192,224},{224,1... | collective-permute-start | bytes 393224 | tf_op jit(solution)/shard_map/ppermute | solution.py:46
  146.9 14.3 %collective-permute-start.7 = (bf16[512,128]{1,0:T(8,128)(2,1)S(1)}, bf16[512,128]{1,0:T(8,128)(2,1)S(1)}, u32[]{:S(2)}, u32[]{:S(2)}) collective-permute-start(bf16[512,128]{1,0:T(8,128)(2,1)S(1)} %get-tuple-element.80), channel_id=1, source_target_pairs={{0,128},{32,160},{64,192},{96,224},{128,0},{160,32},{192,64},{224,... | collective-permute-start | bytes 393224 | tf_op jit(solution)/shard_map/ppermute | solution.py:46
  148.1 15.7 %collective-permute-start.8 = (bf16[512,128]{1,0:T(8,128)(2,1)S(1)}, bf16[512,128]{1,0:T(8,128)(2,1)S(1)}, u32[]{:S(2)}, u32[]{:S(2)}) collective-permute-start(bf16[512,128]{1,0:T(8,128)(2,1)S(1)} %get-tuple-element.81), channel_id=1, source_target_pairs={{0,160},{32,128},{64,224},{96,192},{128,32},{160,0},{192,96},{224,... | collective-permute-start | bytes 393224 | tf_op jit(solution)/shard_map/ppermute | solution.py:46
  152.2 17.8 %collective-permute-start.9 = (bf16[512,128]{1,0:T(8,128)(2,1)S(1)}, bf16[512,128]{1,0:T(8,128)(2,1)S(1)}, u32[]{:S(2)}, u32[]{:S(2)}) collective-permute-start(bf16[512,128]{1,0:T(8,128)(2,1)S(1)} %get-tuple-element.82), channel_id=1, source_target_pairs={{0,64},{32,96},{64,128},{96,160},{128,192},{160,224},{192,0},{224,... | collective-permute-start | bytes 393224 | tf_op jit(solution)/shard_map/ppermute | solution.py:46
  152.2 17.8 %collective-permute-start.10 = (bf16[512,128]{1,0:T(8,128)(2,1)S(1)}, bf16[512,128]{1,0:T(8,128)(2,1)S(1)}, u32[]{:S(2)}, u32[]{:S(2)}) collective-permute-start(bf16[512,128]{1,0:T(8,128)(2,1)S(1)} %get-tuple-element.83), channel_id=1, source_target_pairs={{0,192},{32,224},{64,0},{96,32},{128,64},{160,96},{192,128},{224,1... | collective-permute-start | bytes 393224 | tf_op jit(solution)/shard_map/ppermute | solution.py:46
  156.3 15.2 %collective-permute-start.11 = (bf16[512,128]{1,0:T(8,128)(2,1)S(1)}, bf16[512,128]{1,0:T(8,128)(2,1)S(1)}, u32[]{:S(2)}, u32[]{:S(2)}) collective-permute-start(bf16[512,128]{1,0:T(8,128)(2,1)S(1)} %get-tuple-element.84), channel_id=1, source_target_pairs={{0,96},{32,64},{64,160},{96,128},{128,224},{160,192},{192,32},{224... | collective-permute-start | bytes 393224 | tf_op jit(solution)/shard_map/ppermute | solution.py:46
  161.2 10.3 %collective-permute-start.12 = (bf16[512,128]{1,0:T(8,128)(2,1)S(1)}, bf16[512,128]{1,0:T(8,128)(2,1)S(1)}, u32[]{:S(2)}, u32[]{:S(2)}) collective-permute-start(bf16[512,128]{1,0:T(8,128)(2,1)S(1)} %get-tuple-element.85), channel_id=1, source_target_pairs={{0,224},{32,192},{64,32},{96,0},{128,96},{160,64},{192,160},{224,1... | collective-permute-start | bytes 393224 | tf_op jit(solution)/shard_map/ppermute | solution.py:46
  163.8 7.7 %collective-permute-start.13 = (bf16[512,128]{1,0:T(8,128)(2,1)S(1)}, bf16[512,128]{1,0:T(8,128)(2,1)S(1)}, u32[]{:S(2)}, u32[]{:S(2)}) collective-permute-start(bf16[512,128]{1,0:T(8,128)(2,1)S(1)} %get-tuple-element.86), channel_id=1, source_target_pairs={{0,32},{32,0},{64,96},{96,64},{128,160},{160,128},{192,224},{224,1... | collective-permute-start | bytes 393224 | tf_op jit(solution)/shard_map/ppermute | solution.py:46
  165.7 12.0 %all-to-all-start.3 = ((bf16[8,4,256]{2,1,0:T(4,128)(2,1)}), bf16[8,4,256]{2,1,0:T(4,128)(2,1)S(1)}, u32[]{:S(2)}, u32[]{:S(2)}) async-start(bf16[8,4,256]{2,1,0:T(4,128)(2,1)} %reshape.21), calls=%async_computation.3 | async-start | bytes 32768 | tf_op jit(solution)/shard_map/all_to_all | solution.py:328
  (1 other events, 0.7 us)

commit v2 on v1

v2 whole, which is shorter than its diff:
```python
import functools

import jax
import jax.numpy as jnp
from jax import lax
from jax.experimental import pallas as pl
from jax.experimental.pallas import tpu as pltpu
from jax.sharding import PartitionSpec as P

HEAD_DIM = 128
BLOCK = 128
NEAR = 4
FAR = 64
NEAR_ROWS = 32
FAR_ROWS = 2
WIDE = 8
NARROW = 32
SPAN = WIDE * BLOCK
SPAN_NEAR = WIDE * NEAR_ROWS
SPAN_FAR = WIDE * FAR_ROWS
FAR_ALL = NARROW * SPAN_FAR
FEAT = 2048
PAIR = 2 * HEAD_DIM
SCALE = HEAD_DIM**-0.5
LOG2E = 1.4426950408889634
BLOCKED = -1e30
F32 = jnp.float32
BF16 = jnp.bfloat16

CHIPS = [1, 3, 2, 0]
SENT = len(CHIPS) - 1
HALF = 4 * BLOCK
TAIL = 16
STEPS = [(chip, core) for core in range(2) for chip in CHIPS]


def target(at, step):
    chip, core = step
    return ((at // 2 + chip) % 4) * 2 + (at % 2 + core) % 2


def source(at, step):
    chip, core = step
    return ((at // 2 + 4 - chip) % 4) * 2 + (at % 2 + core) % 2


def move(buffer, step):
    return lax.ppermute(buffer, "wide", [(s, target(s, step)) for s in range(WIDE)])


def to_chips(parts):
    return [move(part, (chip, 0)) for part, chip in zip(parts[:SENT], CHIPS)] + [parts[SENT]]


def to_other_core(parts):
    return move(gather_halves(parts), (0, 1))


def after(values, others):
    tied = lax.optimization_barrier((list(values), list(others)))
    return tied[0], tied[1]


def copy_all(pairs, sems):
    copies = [pltpu.make_async_copy(src, dst, sems.at[i]) for i, (src, dst) in enumerate(pairs)]
    for copy in copies:
        copy.start()
    return copies


def gather_kernel(*refs):
    n = len(refs) - 2
    ins, out, sems = refs[:n], refs[n], refs[n + 1]
    pairs, row = [], 0
    for ref in ins:
        half = ref.shape[0] // 2
        pairs.append((ref.at[pl.ds(half, half), :], out.at[pl.ds(row, half), :]))
        row += half
    for copy in copy_all(pairs, sems):
        copy.wait()


def gather_halves(parts):
    n = len(parts)
    some = pl.BlockSpec(memory_space=pl.ANY)
    return pl.pallas_call(
        gather_kernel,
        out_shape=jax.ShapeDtypeStruct((sum(part.shape[0] for part in parts) // 2, HEAD_DIM), BF16),
        in_specs=[some] * n,
        out_specs=some,
        scratch_shapes=[pltpu.SemaphoreType.DMA((n,))],
        compiler_params=pltpu.CompilerParams(vmem_limit_bytes=1 << 20),
        name="gather_halves",
    )(*parts)


def nt(a, b):
    return lax.dot_general(a, b, (((1,), (1,)), ((), ())), preferred_element_type=F32)


def nn(a, b):
    return lax.dot_general(a, b, (((1,), (0,)), ((), ())), preferred_element_type=F32)


def tn(a, b):
    return lax.dot_general(a, b, (((0,), (0,)), ((), ())), preferred_element_type=F32)


def pooling(rows, factor):
    shape = (rows, rows * factor)
    group = lax.broadcasted_iota(jnp.int32, shape, 1) // factor
    member = group == lax.broadcasted_iota(jnp.int32, shape, 0)
    return jnp.where(member, F32(1.0 / factor), F32(0.0)).astype(BF16)


def spreading(rows, factor):
    shape = (rows * factor, rows)
    group = lax.broadcasted_iota(jnp.int32, shape, 0) // factor
    member = group == lax.broadcasted_iota(jnp.int32, shape, 1)
    return jnp.where(member, F32(1.0 / factor), F32(0.0)).astype(BF16)


def pack_kernel(at_ref, k_ref, v_ref, q_ref, g_ref, *refs):
    n = len(CHIPS)
    outs, (held, staged, far_s, in_sems, out_sems) = refs[: 2 * n], refs[2 * n :]
    wide_at = at_ref[0]
    strip = BLOCK // 4
    pairs = []
    for i, ref in enumerate((k_ref, v_ref, q_ref, g_ref)):
        for r in range(0, BLOCK, strip):
            pairs.append((ref.at[r : r + strip, :], held.at[i, r : r + strip, :]))
    copies = copy_all(pairs, in_sems)
    for copy in copies[:8]:
        copy.wait()
    pool_near = pooling(NEAR_ROWS, NEAR)
    group = lax.broadcasted_iota(jnp.int32, (TAIL, NEAR_ROWS), 1) // (FAR // NEAR)
    row = lax.broadcasted_iota(jnp.int32, (TAIL, NEAR_ROWS), 0)
    far = None
    for i in range(2):
        near = nn(pool_near, held[i]).astype(BF16)
        pool_far = jnp.where(row == group + i * FAR_ROWS, F32(NEAR / FAR), F32(0.0)).astype(BF16)
        far = nn(pool_far, near) if far is None else far + nn(pool_far, near)
    far_s[...] = far.astype(BF16)
    for copy in copies[8:]:
        copy.wait()
    last = []
    for head in range(2):
        half = HALF + 2 * TAIL * (1 - head)
        for part, chip in enumerate(CHIPS):
            at = head * n + part
            for core in range(2):
                column = target(wide_at, (chip, core)) * PAIR
                columns = pl.ds(pl.multiple_of(column + head * HEAD_DIM, HEAD_DIM), HEAD_DIM)
                for i in range(4):
                    row = core * half + i * BLOCK
                    staged[at, row : row + BLOCK, :] = held[i, :, columns]
                if head == 0:
                    for j in range(2):
                        row = core * half + HALF + j * TAIL
                        columns = pl.ds(pl.multiple_of(column + j * HEAD_DIM, HEAD_DIM), HEAD_DIM)
                        staged[at, row : row + TAIL, :] = far_s[:, columns]
            copy = pltpu.make_async_copy(staged.at[at, pl.ds(0, 2 * half), :], outs[at], out_sems.at[at])
            copy.start()
            last.append(copy)
    for copy in last:
        copy.wait()


def pack(at, queries, keys, values, grad_out):
    n = len(CHIPS)
    shapes = [jax.ShapeDtypeStruct((2 * HALF + extra, HEAD_DIM), BF16) for extra in (4 * TAIL, 0)]
    some = pl.BlockSpec(memory_space=pl.ANY)
    outs = pl.pallas_call(
        pack_kernel,
        out_shape=[shapes[0]] * n + [shapes[1]] * n,
        in_specs=[pl.BlockSpec(memory_space=pltpu.SMEM)] + [some] * 4,
        out_specs=[some] * (2 * n),
        scratch_shapes=[
            pltpu.VMEM((4, BLOCK, FEAT), BF16),
            pltpu.VMEM((2 * n, *shapes[0].shape), BF16),
            pltpu.VMEM((TAIL, FEAT), BF16),
            pltpu.SemaphoreType.DMA((16,)),
            pltpu.SemaphoreType.DMA((2 * n,)),
        ],
        compiler_params=pltpu.CompilerParams(vmem_limit_bytes=58 << 20),
        cost_estimate=pl.CostEstimate(flops=0, bytes_accessed=4 << 20, transcendentals=0),
        name="pack",
    )(at, keys, values, queries, grad_out)
    return outs[:n], outs[n:]


def arrivals(parts, swapped, place, start=0, rows=HALF):
    n = len(CHIPS)
    half = parts[0].shape[0] // 2
    pairs = [(parts[i].at[pl.ds(start, rows), :], place(i)) for i in range(n)]
    return pairs + [(swapped.at[pl.ds(i * half + start, rows), :], place(n + i)) for i in range(n)]


def collect_kernel(at_ref, *refs):
    n = len(CHIPS)
    ins, swapped, out, held, sems = refs[:n], refs[n], refs[n + 1], refs[n + 2], refs[n + 3]
    wide_at = at_ref[0]
    pairs = []
    for head in range(2):
        place = lambda i: held.at[head, source(wide_at, STEPS[i])]
        pairs += arrivals(ins, swapped, place, HALF + head * TAIL, TAIL)
    for copy in copy_all(pairs, sems):
        copy.wait()
    shape = (2 * SPAN_FAR, WIDE * TAIL)
    row, column = lax.broadcasted_iota(jnp.int32, shape, 0), lax.broadcasted_iota(jnp.int32, shape, 1)
    inner = row % SPAN_FAR
    wanted = (inner // FAR_ROWS) * TAIL + inner % FAR_ROWS + (row // SPAN_FAR) * FAR_ROWS
    choose = jnp.where(column == wanted, F32(1.0), F32(0.0)).astype(BF16)
    for head in range(2):
        rows = nn(choose, held[head].reshape(WIDE * TAIL, HEAD_DIM)).astype(BF16)
        mine = slice(2 * head * SPAN_FAR, 2 * (head + 1) * SPAN_FAR)
        out[:, mine, :] = jnp.broadcast_to(rows[None], (NARROW, 2 * SPAN_FAR, HEAD_DIM))


def collect(at, parts, swapped):
    n = len(CHIPS)
    return pl.pallas_call(
        collect_kernel,
        out_shape=jax.ShapeDtypeStruct((NARROW, 4 * SPAN_FAR, HEAD_DIM), BF16),
        in_specs=[pl.BlockSpec(memory_space=pltpu.SMEM)] + [pl.BlockSpec(memory_space=pl.ANY)] * (n + 1),
        out_specs=pl.BlockSpec(memory_space=pltpu.VMEM),
        scratch_shapes=[pltpu.VMEM((2, WIDE, TAIL, HEAD_DIM), BF16), pltpu.SemaphoreType.DMA((2 * WIDE,))],
        compiler_params=pltpu.CompilerParams(vmem_limit_bytes=4 << 20),
        name="collect",
    )(at, *parts, swapped)


def attend_kernel(head, at_ref, *refs):
    n = len(CHIPS)
    ins, swapped, far_ref, refs = refs[:n], refs[n], refs[n + 1], refs[n + 2 :]
    if head:
        other_far, refs = refs[0], refs[1:]
    outs, far_out = refs[:n], refs[n]
    held, kn_s, vn_s, o_s, dq_s, dk_s, dv_s, dkn_s, dvn_s, dkf_s, dvf_s, s_s, w_s, d_s, sems = refs[n + 1 :]
    wide_at = at_ref[0]
    far_seen = at_ref[1] * SPAN_FAR
    copies = copy_all(arrivals(ins, swapped, lambda i: held.at[source(wide_at, STEPS[i])]), sems)
    for ref in (dk_s, dv_s, dkn_s, dvn_s, dkf_s, dvf_s):
        ref[...] = jnp.zeros(ref.shape, F32)
    for copy in copies:
        copy.wait()
    pool_near = pooling(NEAR_ROWS, NEAR)
    spread_near = spreading(NEAR_ROWS, NEAR)
    later = lax.broadcasted_iota(jnp.int32, (BLOCK, BLOCK), 0) > lax.broadcasted_iota(
        jnp.int32, (BLOCK, BLOCK), 1
    )
    far_blocked = lax.broadcasted_iota(jnp.int32, (FAR_ALL, 1), 0) >= far_seen
    far_bias = jnp.where(far_blocked, F32(BLOCKED), F32(0.0))
    exponent = SCALE * LOG2E
    wide2 = 2 * BLOCK
    first = 2 * head * SPAN_FAR
    kf = far_ref[:, first : first + SPAN_FAR, :].reshape(FAR_ALL, HEAD_DIM)
    vf = far_ref[:, first + SPAN_FAR : first + 2 * SPAN_FAR, :].reshape(FAR_ALL, HEAD_DIM)

    def rows_of(array, block):
        row = array * BLOCK
        return held[block, row : row + BLOCK, :]

    key = functools.partial(rows_of, 0)
    value = functools.partial(rows_of, 1)
    query = functools.partial(rows_of, 2)
    grad = functools.partial(rows_of, 3)
    for block in range(WIDE):
        near_rows = slice(block * NEAR_ROWS, (block + 1) * NEAR_ROWS)
        kn_s[near_rows, :] = nn(pool_near, key(block)).astype(BF16)
        vn_s[near_rows, :] = nn(pool_near, value(block)).astype(BF16)
    for pair in range(WIDE // 2):
        blocks = (2 * pair, 2 * pair + 1)
        befores = tuple(max(b - 1, 0) for b in blocks)
        qs, gs = [query(b) for b in blocks], [grad(b) for b in blocks]
        q, g = jnp.concatenate(qs, axis=0), jnp.concatenate(gs, axis=0)
        near = 2 * NEAR_ROWS * pair + NEAR_ROWS
        far_from = wide2 + near
        total = far_from + FAR_ALL
        halves = [slice(b * BLOCK, (b + 1) * BLOCK) for b in range(2)]
        for b, cols in enumerate(halves):
            if blocks[b] == 0:
                s_s[0:BLOCK, cols] = jnp.full((BLOCK, BLOCK), BLOCKED, F32)
            else:
                s_s[0:BLOCK, cols] = nt(key(befores[b]), qs[b])
            s_s[BLOCK:wide2, cols] = jnp.where(later, F32(BLOCKED), nt(key(blocks[b]), qs[b]))
        s_s[wide2:far_from, :] = nt(kn_s[0:near, :], q)
        s_s[far_from - NEAR_ROWS : far_from, 0:BLOCK] = jnp.full((NEAR_ROWS, BLOCK), BLOCKED, F32)
        for i in range(0, FAR_ALL, BLOCK):
            s_s[far_from + i : far_from + i + BLOCK, :] = nt(kf[i : i + BLOCK, :], q) + far_bias[i : i + BLOCK]
        chunks = [(0, BLOCK), (BLOCK, BLOCK)]
        chunks += [(wide2 + i, min(BLOCK, near - i)) for i in range(0, near, BLOCK)]
        chunks += [(far_from + i, BLOCK) for i in range(0, FAR_ALL, BLOCK)]
        top = None
        for start, size in chunks:
            here = jnp.max(s_s[start : start + size, :].reshape(size // 8, 8, wide2), axis=0)
            top = here if top is None else jnp.maximum(top, here)
        top = jnp.max(top, axis=0, keepdims=True)
        norm = None
        for start, size in chunks:
            e = jnp.exp2((s_s[start : start + size, :] - top) * exponent)
            s_s[start : start + size, :] = e
            here = jnp.sum(e.reshape(size // 8, 8, wide2), axis=0)
            norm = here if norm is None else norm + here
        inverse = 1.0 / jnp.sum(norm, axis=0, keepdims=True)
        for start, size in chunks:
            e = s_s[start : start + size, :] * inverse
            s_s[start : start + size, :] = e
            w_s[start : start + size, :] = e.astype(BF16)
        sides = [
            tn(value(befores[b]), w_s[0:BLOCK, cols]) + tn(value(blocks[b]), w_s[BLOCK:wide2, cols])
            for b, cols in enumerate(halves)
        ]
        attended = jnp.concatenate(sides, axis=1)
        attended += tn(vn_s[0:near, :], w_s[wide2:far_from, :])
        attended += tn(vf, w_s[far_from:total, :])
        attended = attended.astype(BF16).astype(F32)
        q_rows = slice(pair * wide2, (pair + 1) * wide2)
        o_s[q_rows, :] = attended.T.astype(BF16)
        row_dot = jnp.sum(g.astype(F32).T * attended, axis=0, keepdims=True)

        def put(start, size, cols, dprob, dot):
            d_s[start : start + size, cols] = (s_s[start : start + size, cols] * (dprob - dot)).astype(BF16)

        every = slice(0, wide2)
        for b, cols in enumerate(halves):
            put(0, BLOCK, cols, nt(value(befores[b]), gs[b]), row_dot[:, cols])
            put(BLOCK, BLOCK, cols, nt(value(blocks[b]), gs[b]), row_dot[:, cols])
        put(wide2, near, every, nt(vn_s[0:near, :], g), row_dot)
        for i in range(0, FAR_ALL, BLOCK):
            put(far_from + i, BLOCK, every, nt(vf[i : i + BLOCK, :], g), row_dot)
        sides = []
        for b, cols in enumerate(halves):
            before, own = (slice(at * BLOCK, (at + 1) * BLOCK) for at in (befores[b], blocks[b]))
            sides.append(tn(key(befores[b]), d_s[0:BLOCK, cols]) + tn(key(blocks[b]), d_s[BLOCK:wide2, cols]))
            if blocks[b] > 0:
                dk_s[before, :] += nn(d_s[0:BLOCK, cols], qs[b])
                dv_s[before, :] += nn(w_s[0:BLOCK, cols], gs[b])
            dk_s[own, :] += nn(d_s[BLOCK:wide2, cols], qs[b])
            dv_s[own, :] += nn(w_s[BLOCK:wide2, cols], gs[b])
        grad_query = jnp.concatenate(sides, axis=1)
        grad_query += tn(kn_s[0:near, :], d_s[wide2:far_from, :])
        grad_query += tn(kf, d_s[far_from:total, :])
        dq_s[q_rows, :] = (grad_query * SCALE).T.astype(BF16)
        dkn_s[0:near, :] += nn(d_s[wide2:far_from, :], q)
        dvn_s[0:near, :] += nn(w_s[wide2:far_from, :], g)
        dkf_s[...] += nn(d_s[far_from:total, :], q)
        dvf_s[...] += nn(w_s[far_from:total, :], g)

    mine = slice(0, HEAD_DIM)
    if head:
        far_out[:, :, mine] = other_far[...]
        mine = slice(HEAD_DIM, PAIR)
    far_out[:, :SPAN_FAR, mine] = (dkf_s[...] * SCALE).astype(BF16).reshape(NARROW, SPAN_FAR, HEAD_DIM)
    far_out[:, SPAN_FAR:, mine] = dvf_s[...].astype(BF16).reshape(NARROW, SPAN_FAR, HEAD_DIM)
    for block in range(WIDE):
        rows = slice(block * BLOCK, (block + 1) * BLOCK)
        near_rows = slice(block * NEAR_ROWS, (block + 1) * NEAR_ROWS)
        dk_s[rows, :] = (dk_s[rows, :] + nn(spread_near, dkn_s[near_rows, :].astype(BF16))) * SCALE
        dv_s[rows, :] = dv_s[rows, :] + nn(spread_near, dvn_s[near_rows, :].astype(BF16))
    for part, chip in enumerate(CHIPS):
        for core in range(2):
            rows = pl.ds(pl.multiple_of(target(wide_at, (chip, core)) * BLOCK, BLOCK), BLOCK)
            for i, ref in enumerate((o_s, dq_s, dk_s, dv_s)):
                row = core * HALF + i * BLOCK
                outs[part][row : row + BLOCK, :] = ref[rows, :].astype(BF16)


def attend(head, at, parts, swapped, far, other_far=()):
    n = len(CHIPS)
    vmem, some = pl.BlockSpec(memory_space=pltpu.VMEM), pl.BlockSpec(memory_space=pl.ANY)
    rows = lambda count, kind: pltpu.VMEM((count, HEAD_DIM), kind)
    lists = lambda kind: pltpu.VMEM((SPAN, 2 * BLOCK), kind)
    outs = pl.pallas_call(
        functools.partial(attend_kernel, head),
        out_shape=[jax.ShapeDtypeStruct((2 * HALF, HEAD_DIM), BF16)] * n
        + [jax.ShapeDtypeStruct((NARROW, 2 * SPAN_FAR, (1 + head) * HEAD_DIM), BF16)],
        in_specs=[pl.BlockSpec(memory_space=pltpu.SMEM)] + [some] * (n + 1) + [vmem] * (1 + len(other_far)),
        out_specs=[vmem] * (n + 1),
        scratch_shapes=[pltpu.VMEM((WIDE, HALF, HEAD_DIM), BF16)]
        + [rows(SPAN_NEAR, BF16)] * 2 + [rows(SPAN, BF16)] * 2 + [rows(SPAN, F32)] * 2
        + [rows(SPAN_NEAR, F32)] * 2 + [rows(FAR_ALL, F32)] * 2
        + [lists(F32), lists(BF16), lists(BF16), pltpu.SemaphoreType.DMA((WIDE,))],
        compiler_params=pltpu.CompilerParams(vmem_limit_bytes=16 << 20),
        cost_estimate=pl.CostEstimate(flops=1_600_000_000, bytes_accessed=2 << 20, transcendentals=1 << 20),
        name=f"attend{head}",
    )(at, *parts, swapped, far, *other_far)
    return outs[:n], outs[n]


def total_kernel(at_ref, terms_ref, *outs):
    wide_at = at_ref[0]
    total = jnp.sum(terms_ref[...].astype(F32), axis=0).astype(BF16)
    shape = (TAIL, 2 * SPAN_FAR)
    row, column = lax.broadcasted_iota(jnp.int32, shape, 0), lax.broadcasted_iota(jnp.int32, shape, 1)
    for part, chip in enumerate(CHIPS):
        for core in range(2):
            first = target(wide_at, (chip, core)) * FAR_ROWS
            wanted = (row // FAR_ROWS) * SPAN_FAR + first + row % FAR_ROWS
            choose = jnp.where((column == wanted) & (row < 2 * FAR_ROWS), F32(1.0), F32(0.0)).astype(BF16)
            rows = nn(choose, total).astype(BF16)
            for head in range(2):
                at = (2 * core + head) * TAIL
                outs[part][at : at + TAIL, :] = rows[:, head * HEAD_DIM : (head + 1) * HEAD_DIM]


def total(at, terms):
    n = len(CHIPS)
    vmem = pl.BlockSpec(memory_space=pltpu.VMEM)
    return pl.pallas_call(
        total_kernel,
        out_shape=[jax.ShapeDtypeStruct((4 * TAIL, HEAD_DIM), BF16)] * n,
        in_specs=[pl.BlockSpec(memory_space=pltpu.SMEM), vmem],
        out_specs=[vmem] * n,
        compiler_params=pltpu.CompilerParams(vmem_limit_bytes=4 << 20),
        name="total",
    )(at, terms)


def unpack_kernel(at_ref, *refs):
    n = len(CHIPS)
    ins0, swapped0, ins1, swapped1 = refs[:n], refs[n], refs[n + 1 : 2 * n + 1], refs[2 * n + 1]
    tails, outs = refs[2 * n + 2 : 3 * n + 2], refs[3 * n + 2 : 3 * n + 6]
    held, far_s, sums, sems, far_sems = refs[3 * n + 6 :]
    wide_at = at_ref[0]
    pairs = arrivals(ins0, swapped0, lambda i: held.at[i])
    pairs += arrivals(ins1, swapped1, lambda i: held.at[WIDE + i])
    copies = copy_all(pairs, sems)
    rows = 2 * TAIL
    pairs = [(tails[i].at[pl.ds(0, rows), :], far_s.at[i]) for i in range(n)]
    pairs += [(swapped1.at[pl.ds(n * HALF + i * rows, rows), :], far_s.at[n + i]) for i in range(n)]
    for copy in copy_all(pairs, far_sems):
        copy.wait()
    for head in range(2):
        for part, step in enumerate(STEPS):
            copies[head * WIDE + part].wait()
            block = source(wide_at, step)
            columns = pl.ds(pl.multiple_of(block * PAIR + head * HEAD_DIM, HEAD_DIM), HEAD_DIM)
            far = far_s[part, head * TAIL : (head + 1) * TAIL, :].astype(F32) * (1.0 / FAR)
            for i in range(4):
                piece = held[head * WIDE + part, i * BLOCK : (i + 1) * BLOCK, :]
                if i >= 2:
                    terms = piece.astype(F32)
                    at = (i - 2) * FAR_ROWS
                    both = [terms[r * FAR : (r + 1) * FAR] + far[at + r : at + r + 1] for r in range(FAR_ROWS)]
                    piece = jnp.concatenate(both, axis=0).astype(BF16)
                sums[i, :, columns] = piece
    strip = BLOCK // 2
    pairs = []
    for i in range(4):
        for r in range(0, BLOCK, strip):
            pairs.append((sums.at[i, r : r + strip, :], outs[i].at[r : r + strip, :]))
    for copy in copy_all(pairs, sems):
        copy.wait()


def unpack(at, parts0, swapped0, parts1, swapped1, tails):
    n = len(CHIPS)
    some = pl.BlockSpec(memory_space=pl.ANY)
    return pl.pallas_call(
        unpack_kernel,
        out_shape=[jax.ShapeDtypeStruct((BLOCK, FEAT), BF16)] * 4,
        in_specs=[pl.BlockSpec(memory_space=pltpu.SMEM)] + [some] * (3 * n + 2),
        out_specs=[some] * 4,
        scratch_shapes=[
            pltpu.VMEM((2 * WIDE, HALF, HEAD_DIM), BF16),
            pltpu.VMEM((WIDE, 2 * TAIL, HEAD_DIM), BF16),
            pltpu.VMEM((4, BLOCK, FEAT), BF16),
            pltpu.SemaphoreType.DMA((2 * WIDE,)),
            pltpu.SemaphoreType.DMA((WIDE,)),
        ],
        compiler_params=pltpu.CompilerParams(vmem_limit_bytes=8 << 20),
        name="unpack",
    )(at, *parts0, swapped0, *parts1, swapped1, *tails)


def shards(queries, keys, values, grad_out):
    at = jnp.stack([lax.axis_index("wide"), lax.axis_index("narrow")]).astype(jnp.int32)
    parts0, parts1 = pack(at, queries, keys, values, grad_out)
    parts0 = to_chips(parts0)
    parts1, parts0 = after(parts1, parts0)
    parts1 = to_chips(parts1)
    swapped0 = to_other_core(parts0)
    far = lax.all_to_all(collect(at, parts0, swapped0), "narrow", 0, 0, tiled=True)
    out0, terms0 = attend(0, at, parts0, swapped0, far)
    parts1, own = after(parts1, out0[SENT:])
    out0 = [*out0[:SENT], *own]
    out1, terms = attend(1, at, parts1, to_other_core(parts1), far, (terms0,))
    out0 = to_chips(out0)
    swapped0 = to_other_core(out0)
    out1, (swapped0,) = after(out1, [swapped0])
    out1 = to_chips(out1)
    tails = to_chips(total(at, lax.all_to_all(terms, "narrow", 0, 0, tiled=True)))
    return tuple(unpack(at, out0, swapped0, out1, to_other_core([*out1, *tails]), tails))


def solution(mesh):
    rows = P(("narrow", "wide"), None)
    return jax.shard_map(
        shards, mesh=mesh, in_specs=(rows,) * 4, out_specs=(rows,) * 4, check_vma=False
    )
```

time: 181 us -> 163 us (0.901)
  Pallas kernels: 16.1 us -> 32.2 us
  blocking collectives: 15.2 us -> 0 us
  local copies, waits for them, and re-layouts: 14.8 us -> 1.66 us
  starting transfers between devices: 63.8 us -> 54.6 us
  waiting for transfers between devices: 67.5 us -> 72.7 us
    all_to_all x1 -> x0, blocking collectives: 15.2 us -> none  [shards(): far = lax.all_to_all(far, 'wide', 0, 0, tiled=True)]
    pallas_call x3 -> x9, Pallas kernels: 13.6 us -> 26.6 us  [the longest x2 16.7 us: attend(): pl.pallas_call(functools.partial(attend_kernel, head), out_shape=[jax.Sha...]
    unnamed x36 -> x12, local copies, waits for them, and re-layouts: 13.3 us -> 1.66 us
    ppermute x28 -> x19, starting transfers between devices: 42.7 us -> 37.7 us  [move(): lax.ppermute(buffer, 'wide', [(s, target(s, step)) for s in range(WIDE)])]
    all_to_all x3 -> x2, waiting for transfers between devices: 6.21 us -> 10.6 us  [the longest x1 10.6 us: shards(): lax.all_to_all(collect(at, parts0, swapped0), 'narrow', 0, 0, tiled=True)]
    all_to_all x3 -> x2, starting transfers between devices: 21.1 us -> 16.8 us  [the longest x1 8.53 us: shards(): lax.all_to_all(collect(at, parts0, swapped0), 'narrow', 0, 0, tiled=True)]
    pallas_call x1, Pallas kernels: 2.48 us -> 5.6 us  [unpack(): pl.pallas_call(unpack_kernel, out_shape=[jax.ShapeDtypeStruct((BLOCK, FEA...]
    ppermute x28 -> x19, waiting for transfers between devices: 61.3 us -> 62.1 us  [move(): lax.ppermute(buffer, 'wide', [(s, target(s, step)) for s in range(WIDE)])]
  transfers between devices with their start and end apart: 31 -> 21, of which waited for: 15 -> 10; matrix products, arithmetic and copies ran while one was open for 1% -> 0% of each run, Pallas kernels for 0% -> 11%
where the time goes in v2:
time: 163 us
  waiting for transfers between devices  72.7 us (45%)
  starting transfers between devices  54.6 us (33%)
  Pallas kernels  32.2 us (20%)
  local copies, waits for them, and re-layouts  1.66 us (1%)
    ppermute x19, waiting for transfers between devices, move(): lax.ppermute(buffer, 'wide', [(s, target(s, step)) for s in range(WIDE)])  62.1 us
    ppermute x19, starting transfers between devices, move(): lax.ppermute(buffer, 'wide', [(s, target(s, step)) for s in range(WIDE)])  37.7 us
    pallas_call x2, Pallas kernels, attend(): pl.pallas_call(functools.partial(attend_kernel, head), out_shape=[jax.Sha...  16.7 us
    all_to_all x1, waiting for transfers between devices, shards(): lax.all_to_all(collect(at, parts0, swapped0), 'narrow', 0, 0, tiled=True)  10.6 us
    all_to_all x1, starting transfers between devices, shards(): lax.all_to_all(collect(at, parts0, swapped0), 'narrow', 0, 0, tiled=True)  8.53 us
    all_to_all x1, starting transfers between devices, shards(): lax.all_to_all(terms, 'narrow', 0, 0, tiled=True)  8.32 us
    pallas_call x1, Pallas kernels, unpack(): pl.pallas_call(unpack_kernel, out_shape=[jax.ShapeDtypeStruct((BLOCK, FEA...  5.6 us
    pallas_call x1, Pallas kernels, pack(): pl.pallas_call(pack_kernel, out_shape=[shapes[0]] * n + [shapes[1]] * n,...  3.99 us
  transfers between devices with their start and end apart: 21, of which 10 were waited for; matrix products, arithmetic and copies ran while one was open for 0% of the time, Pallas kernels for 11%

profile of v2, /device:TPU:34, one launch (start us, length us, event | category | flops | bytes accessed | tf_op | source)
XLA Modules:
  0.0 162.7 jit_solution(9295421215262642201)
XLA Ops:
  0.6 0.6 pad_add_fusion.at_ref
  1.2 4.0 %pack.1 = (bf16[1088,128]{1,0:T(8,128)(2,1)}, bf16[1088,128]{1,0:T(8,128)(2,1)}, bf16[1088,128]{1,0:T(8,128)(2,1)}, bf16[1088,128]{1,0:T(8,128)(2,1)}, bf16[1024...) custom-call(s32[2]{0:T(128)} %pad_add_fusion.at_ref, ...), custom_call_target="tpu_custom_call" | custom-call | bytes 4194304 | tf_op jit(solution)/shard_map/pack/pallas_call | solution.py:173
  5.2 3.3 %collective-permute-start = (bf16[1088,128]{1,0:T(8,128)(2,1)}, bf16[1088,128]{1,0:T(8,128)(2,1)S(1)}, u32[]{:S(2)}, u32[]{:S(2)}) collective-permute-start(bf16[1088,128]{1,0:T(8,128)(2,1)} %get-tuple-element.48), channel_id=1, source_target_pairs={{0,64},{32,96},{64,128},{96,160},{128,192},{160,224},{192,0},{224,... | collective-permute-start | bytes 835592 | tf_op jit(solution)/shard_map/ppermute | solution.py:48
  8.6 2.2 %collective-permute-start.1 = (bf16[1088,128]{1,0:T(8,128)(2,1)}, bf16[1088,128]{1,0:T(8,128)(2,1)S(1)}, u32[]{:S(2)}, u32[]{:S(2)}) collective-permute-start(bf16[1088,128]{1,0:T(8,128)(2,1)} %get-tuple-element.49), channel_id=1, source_target_pairs={{0,192},{32,224},{64,0},{96,32},{128,64},{160,96},{192,128},{224,1... | collective-permute-start | bytes 835592 | tf_op jit(solution)/shard_map/ppermute | solution.py:48
  10.8 4.9 %collective-permute-start.2 = (bf16[1088,128]{1,0:T(8,128)(2,1)}, bf16[1088,128]{1,0:T(8,128)(2,1)S(1)}, u32[]{:S(2)}, u32[]{:S(2)}) collective-permute-start(bf16[1088,128]{1,0:T(8,128)(2,1)} %get-tuple-element.50), channel_id=1, source_target_pairs={{0,128},{32,160},{64,192},{96,224},{128,0},{160,32},{192,64},{224,... | collective-permute-start | bytes 835592 | tf_op jit(solution)/shard_map/ppermute | solution.py:48
  15.7 15.4 %collective-permute-done.refs_0_ = bf16[1088,128]{1,0:T(8,128)(2,1)S(1)} collective-permute-done((bf16[1088,128]{1,0:T(8,128)(2,1)}, bf16[1088,128]{1,0:T(8,128)(2,1)S(1)}, u32[]{:S(2)}, u32[]{:S(2)}) %collective-permute-start) | collective-permute-done | bytes 278560 | tf_op jit(solution)/shard_map/ppermute | solution.py:48
  31.2 0.0 collective-permute-done.1.refs_1_
  31.2 8.2 %collective-permute-done.2.refs_2_ = bf16[1088,128]{1,0:T(8,128)(2,1)S(1)} collective-permute-done((bf16[1088,128]{1,0:T(8,128)(2,1)}, bf16[1088,128]{1,0:T(8,128)(2,1)S(1)}, u32[]{:S(2)}, u32[]{:S(2)}) %collective-permute-start.2) | collective-permute-done | bytes 278560 | tf_op jit(solution)/shard_map/ppermute | solution.py:48
  39.4 1.0 copy-done
  40.3 0.7 gather_halves.4
  41.1 0.1 collective-permute-start.3
  41.2 1.9 %collective-permute-done.3.refs_4_ = bf16[2176,128]{1,0:T(8,128)(2,1)S(1)} collective-permute-done((bf16[2176,128]{1,0:T(8,128)(2,1)S(1)}, bf16[2176,128]{1,0:T(8,128)(2,1)S(1)}, u32[]{:S(2)}, u32[]{:S(2)}) %collective-permute-start.3) | collective-permute-done | bytes 557088 | tf_op jit(solution)/shard_map/ppermute | solution.py:48
  43.1 1.8 %collect.1 = bf16[32,64,128]{2,1,0:T(8,128)(2,1)} custom-call(s32[2]{0:T(128)S(1)} %copy-done.3, bf16[1088,128]{1,0:T(8,128)(2,1)S(1)} %collective-permute-done.refs_0_, bf16[1088,128]{1,0:T(8,128)(2,1)S(1)} %collective-permute-done.1.refs_1_, bf16[1088,128]{1,0:T(8,128)(2,1)S(1)} %collective-permute-done.2.refs_2_, bf16[1088,128]{1,0:T(8,128)(2,1)S(1)} %copy-done.1, ...), custom_call_target="tpu_custom_call" | custom-call | tf_op jit(solution)/shard_map/collect/pallas_call | solution.py:222
  45.0 8.5 %all-to-all-start = ((bf16[32,64,128]{2,1,0:T(8,128)(2,1)}), bf16[32,64,128]{2,1,0:T(8,128)(2,1)S(1)}, u32[]{:S(2)}, u32[]{:S(2)}) async-start(bf16[32,64,128]{2,1,0:T(8,128)(2,1)} %collect.1), calls=%async_computation | async-start | bytes 1048576 | tf_op jit(solution)/shard_map/all_to_all | solution.py:484
  53.5 0.7 collective-permute-start.7
  54.2 3.5 %collective-permute-start.8 = (bf16[1024,128]{1,0:T(8,128)(2,1)}, bf16[1024,128]{1,0:T(8,128)(2,1)}, u32[]{:S(2)}, u32[]{:S(2)}) collective-permute-start(bf16[1024,128]{1,0:T(8,128)(2,1)} %get-tuple-element.60), channel_id=1, source_target_pairs={{0,192},{32,224},{64,0},{96,32},{128,64},{160,96},{192,128},{224,1... | collective-permute-start | bytes 786440 | tf_op jit(solution)/shard_map/ppermute | solution.py:48
  57.7 1.8 %collective-permute-start.9 = (bf16[1024,128]{1,0:T(8,128)(2,1)}, bf16[1024,128]{1,0:T(8,128)(2,1)}, u32[]{:S(2)}, u32[]{:S(2)}) collective-permute-start(bf16[1024,128]{1,0:T(8,128)(2,1)} %get-tuple-element.61), channel_id=1, source_target_pairs={{0,128},{32,160},{64,192},{96,224},{128,0},{160,32},{192,64},{224,... | collective-permute-start | bytes 786440 | tf_op jit(solution)/shard_map/ppermute | solution.py:48
  59.6 10.6 %all-to-all-done.refs_5_ = bf16[32,64,128]{2,1,0:T(8,128)(2,1)S(1)} async-done(((bf16[32,64,128]{2,1,0:T(8,128)(2,1)}), bf16[32,64,128]{2,1,0:T(8,128)(2,1)S(1)}, u32[]{:S(2)}, u32[]{:S(2)}) %all-to-all-start) | async-done | bytes 524320 | tf_op jit(solution)/shard_map/all_to_all | solution.py:484
  70.2 8.4 %attend0.1 = (bf16[1024,128]{1,0:T(8,128)(2,1)}, bf16[1024,128]{1,0:T(8,128)(2,1)}, bf16[1024,128]{1,0:T(8,128)(2,1)}, bf16[1024,128]{1,0:T(8,128)(2,1)S(1)}, bf16[32,32,128]{2,1,0:T(8,128)(2,1)S(1)}) custom-call(s32[2]{0:T(128)S(1)} %copy-done.3, bf16[1088,128]{1,0:T(8,128)(2,1)S(1)} %collective-permute-done.refs_0_, ...), custom_call_target="tpu_custom_call" | custom-call | flops 1600000000 | bytes 2097152 | tf_op jit(solution)/shard_map/attend0/pallas_call | solution.py:374
  78.6 0.0 collective-permute-done.7.refs_0_
  78.6 0.0 collective-permute-done.8.refs_1_
  78.6 5.4 %collective-permute-done.9.refs_2_ = bf16[1024,128]{1,0:T(8,128)(2,1)} collective-permute-done((bf16[1024,128]{1,0:T(8,128)(2,1)}, bf16[1024,128]{1,0:T(8,128)(2,1)}, u32[]{:S(2)}, u32[]{:S(2)}) %collective-permute-start.9) | collective-permute-done | bytes 262176 | tf_op jit(solution)/shard_map/ppermute | solution.py:48
  84.0 1.2 gather_halves.5
  85.2 0.3 collective-permute-start.10
  85.5 0.1 collective-permute-start.4
  85.6 4.1 %collective-permute-start.5 = (bf16[1024,128]{1,0:T(8,128)(2,1)}, bf16[1024,128]{1,0:T(8,128)(2,1)S(1)}, u32[]{:S(2)}, u32[]{:S(2)}) collective-permute-start(bf16[1024,128]{1,0:T(8,128)(2,1)} %get-tuple-element.57), channel_id=1, source_target_pairs={{0,192},{32,224},{64,0},{96,32},{128,64},{160,96},{192,128},{224,1... | collective-permute-start | bytes 786440 | tf_op jit(solution)/shard_map/ppermute | solution.py:48
  89.7 4.1 %collective-permute-start.6 = (bf16[1024,128]{1,0:T(8,128)(2,1)}, bf16[1024,128]{1,0:T(8,128)(2,1)S(1)}, u32[]{:S(2)}, u32[]{:S(2)}) collective-permute-start(bf16[1024,128]{1,0:T(8,128)(2,1)} %get-tuple-element.58), channel_id=1, source_target_pairs={{0,128},{32,160},{64,192},{96,224},{128,0},{160,32},{192,64},{224,... | collective-permute-start | bytes 786440 | tf_op jit(solution)/shard_map/ppermute | solution.py:48
  93.8 8.2 %attend1.1 = (bf16[1024,128]{1,0:T(8,128)(2,1)}, bf16[1024,128]{1,0:T(8,128)(2,1)}, bf16[1024,128]{1,0:T(8,128)(2,1)S(1)}, bf16[1024,128]{1,0:T(8,128)(2,1)S(1)}, bf16[32,32,256]{2,1,0:T(8,128)(2,1)}) custom-call(s32[2]{0:T(128)S(1)} %copy-done.3, bf16[1024,128]{1,0:T(8,128)(2,1)S(1)} %collective-permute-done.7.refs_0_, ...), custom_call_target="tpu_custom_call" | custom-call | flops 1600000000 | bytes 2097152 | tf_op jit(solution)/shard_map/attend1/pallas_call | solution.py:374
  102.1 0.7 copy-done.4
  102.7 8.3 %all-to-all-start.1 = ((bf16[32,32,256]{2,1,0:T(8,128)(2,1)}), bf16[32,32,256]{2,1,0:T(8,128)(2,1)S(1)}, u32[]{:S(2)}, u32[]{:S(2)}) async-start(bf16[32,32,256]{2,1,0:T(8,128)(2,1)} %get-tuple-element.79), calls=%async_computation.1 | async-start | bytes 1048576 | tf_op jit(solution)/shard_map/all_to_all | solution.py:493
  111.1 0.0 collective-permute-done.4.refs_0_
  111.1 0.0 collective-permute-done.5.refs_1_
  111.1 5.7 %collective-permute-done.6.refs_2_ = bf16[1024,128]{1,0:T(8,128)(2,1)S(1)} collective-permute-done((bf16[1024,128]{1,0:T(8,128)(2,1)}, bf16[1024,128]{1,0:T(8,128)(2,1)S(1)}, u32[]{:S(2)}, u32[]{:S(2)}) %collective-permute-start.6) | collective-permute-done | bytes 262176 | tf_op jit(solution)/shard_map/ppermute | solution.py:48
  116.8 0.7 gather_halves.6
  117.5 0.1 collective-permute-start.11
  117.6 1.9 %collective-permute-done.11.refs_4_ = bf16[2048,128]{1,0:T(8,128)(2,1)S(1)} collective-permute-done((bf16[2048,128]{1,0:T(8,128)(2,1)S(1)}, bf16[2048,128]{1,0:T(8,128)(2,1)S(1)}, u32[]{:S(2)}, u32[]{:S(2)}) %collective-permute-start.11) | collective-permute-done | bytes 524320 | tf_op jit(solution)/shard_map/ppermute | solution.py:48
  119.5 4.1 %collective-permute-start.13 = (bf16[1024,128]{1,0:T(8,128)(2,1)}, bf16[1024,128]{1,0:T(8,128)(2,1)S(1)}, u32[]{:S(2)}, u32[]{:S(2)}) collective-permute-start(bf16[1024,128]{1,0:T(8,128)(2,1)} %get-tuple-element.76), channel_id=1, source_target_pairs={{0,192},{32,224},{64,0},{96,32},{128,64},{160,96},{192,128},{224,1... | collective-permute-start | bytes 786440 | tf_op jit(solution)/shard_map/ppermute | solution.py:48
  123.7 2.1 %collective-permute-start.14 = (bf16[1024,128]{1,0:T(8,128)(2,1)S(1)}, bf16[1024,128]{1,0:T(8,128)(2,1)S(1)}, u32[]{:S(2)}, u32[]{:S(2)}) collective-permute-start(bf16[1024,128]{1,0:T(8,128)(2,1)S(1)} %copy-done.5), channel_id=1, source_target_pairs={{0,128},{32,160},{64,192},{96,224},{128,0},{160,32},{192,64},{224,... | collective-permute-start | bytes 786440 | tf_op jit(solution)/shard_map/ppermute | solution.py:48
  125.8 0.8 total.1
  126.5 0.4 collective-permute-start.15
  126.9 3.8 %collective-permute-start.16 = (bf16[64,128]{1,0:T(8,128)(2,1)S(1)}, bf16[64,128]{1,0:T(8,128)(2,1)S(1)}, u32[]{:S(2)}, u32[]{:S(2)}) collective-permute-start(bf16[64,128]{1,0:T(8,128)(2,1)S(1)} %get-tuple-element.81), channel_id=1, source_target_pairs={{0,192},{32,224},{64,0},{96,32},{128,64},{160,96},{192,128},{224,1... | collective-permute-start | bytes 49160 | tf_op jit(solution)/shard_map/ppermute | solution.py:48
  130.7 15.8 %collective-permute-done.12.refs_0_.refs_5_ = bf16[1024,128]{1,0:T(8,128)(2,1)S(1)} collective-permute-done((bf16[1024,128]{1,0:T(8,128)(2,1)}, bf16[1024,128]{1,0:T(8,128)(2,1)S(1)}, u32[]{:S(2)}, u32[]{:S(2)}) %collective-permute-start.12) | collective-permute-done | bytes 262176 | tf_op jit(solution)/shard_map/ppermute | solution.py:48
  146.5 1.9 %collective-permute-start.17 = (bf16[64,128]{1,0:T(8,128)(2,1)S(1)}, bf16[64,128]{1,0:T(8,128)(2,1)S(1)}, u32[]{:S(2)}, u32[]{:S(2)}) collective-permute-start(bf16[64,128]{1,0:T(8,128)(2,1)S(1)} %get-tuple-element.82), channel_id=1, source_target_pairs={{0,128},{32,160},{64,192},{96,224},{128,0},{160,32},{192,64},{224,... | collective-permute-start | bytes 49160 | tf_op jit(solution)/shard_map/ppermute | solution.py:48
  148.4 5.7 %collective-permute-done.17.refs_6_.refs_12_ = bf16[64,128]{1,0:T(8,128)(2,1)S(1)} collective-permute-done((bf16[64,128]{1,0:T(8,128)(2,1)S(1)}, bf16[64,128]{1,0:T(8,128)(2,1)S(1)}, u32[]{:S(2)}, u32[]{:S(2)}) %collective-permute-start.17) | collective-permute-done | bytes 16416 | tf_op jit(solution)/shard_map/ppermute | solution.py:48
  154.1 0.8 gather_halves.7
  154.9 0.1 collective-permute-start.18
  155.0 1.9 %collective-permute-done.18.refs_9_ = bf16[2176,128]{1,0:T(8,128)(2,1)S(1)} collective-permute-done((bf16[2176,128]{1,0:T(8,128)(2,1)S(1)}, bf16[2176,128]{1,0:T(8,128)(2,1)S(1)}, u32[]{:S(2)}, u32[]{:S(2)}) %collective-permute-start.18) | collective-permute-done | bytes 557088 | tf_op jit(solution)/shard_map/ppermute | solution.py:48
  157.0 5.6 %unpack.1 = (bf16[128,2048]{1,0:T(8,128)(2,1)}, bf16[128,2048]{1,0:T(8,128)(2,1)}, bf16[128,2048]{1,0:T(8,128)(2,1)}, bf16[128,2048]{1,0:T(8,128)(2,1)}) custom-call(s32[2]{0:T(128)S(1)} %copy-done.3, bf16[1024,128]{1,0:T(8,128)(2,1)S(1)} %collective-permute-done.4.refs_0_, bf16[1024,128]{1,0:T(8,128)(2,1)S(1)} %collective-permute-done.5.refs_1_, ...), custom_call_target="tpu_custom_call" | custom-call | tf_op jit(solution)/shard_map/unpack/pallas_call | solution.py:460
  (17 shorter events, 0.0 us)
Async XLA Ops:
  5.2 25.9 %collective-permute-start = (bf16[1088,128]{1,0:T(8,128)(2,1)}, bf16[1088,128]{1,0:T(8,128)(2,1)S(1)}, u32[]{:S(2)}, u32[]{:S(2)}) collective-permute-start(bf16[1088,128]{1,0:T(8,128)(2,1)} %get-tuple-element.48), channel_id=1, source_target_pairs={{0,64},{32,96},{64,128},{96,160},{128,192},{160,224},{192,0},{224,... | collective-permute-start | bytes 835592 | tf_op jit(solution)/shard_map/ppermute | solution.py:48
  8.6 22.6 %collective-permute-start.1 = (bf16[1088,128]{1,0:T(8,128)(2,1)}, bf16[1088,128]{1,0:T(8,128)(2,1)S(1)}, u32[]{:S(2)}, u32[]{:S(2)}) collective-permute-start(bf16[1088,128]{1,0:T(8,128)(2,1)} %get-tuple-element.49), channel_id=1, source_target_pairs={{0,192},{32,224},{64,0},{96,32},{128,64},{160,96},{192,128},{224,1... | collective-permute-start | bytes 835592 | tf_op jit(solution)/shard_map/ppermute | solution.py:48
  10.8 28.6 %collective-permute-start.2 = (bf16[1088,128]{1,0:T(8,128)(2,1)}, bf16[1088,128]{1,0:T(8,128)(2,1)S(1)}, u32[]{:S(2)}, u32[]{:S(2)}) collective-permute-start(bf16[1088,128]{1,0:T(8,128)(2,1)} %get-tuple-element.50), channel_id=1, source_target_pairs={{0,128},{32,160},{64,192},{96,224},{128,0},{160,32},{192,64},{224,... | collective-permute-start | bytes 835592 | tf_op jit(solution)/shard_map/ppermute | solution.py:48
  39.4 1.0 copy-start
  40.3 2.8 %copy-start.1 = (bf16[1088,128]{1,0:T(8,128)(2,1)S(1)}, bf16[1088,128]{1,0:T(8,128)(2,1)}, u32[]{:S(2)}) copy-start(bf16[1088,128]{1,0:T(8,128)(2,1)} %get-tuple-element.55.refs_3_) | copy-start | bytes 835588
  40.3 2.8 %copy-start.3 = (s32[2]{0:T(128)S(1)}, s32[2]{0:T(128)}, u32[]{:S(2)}) copy-start(s32[2]{0:T(128)} %pad_add_fusion.at_ref) | copy-start | bytes 28
  41.1 2.0 %collective-permute-start.3 = (bf16[2176,128]{1,0:T(8,128)(2,1)S(1)}, bf16[2176,128]{1,0:T(8,128)(2,1)S(1)}, u32[]{:S(2)}, u32[]{:S(2)}) collective-permute-start(bf16[2176,128]{1,0:T(8,128)(2,1)S(1)} %gather_halves.4), channel_id=1, source_target_pairs={{0,32},{32,0},{64,96},{96,64},{128,160},{160,128},{192,224},{224,1... | collective-permute-start | bytes 1671176 | tf_op jit(solution)/shard_map/ppermute | solution.py:48
  45.0 25.2 %all-to-all-start = ((bf16[32,64,128]{2,1,0:T(8,128)(2,1)}), bf16[32,64,128]{2,1,0:T(8,128)(2,1)S(1)}, u32[]{:S(2)}, u32[]{:S(2)}) async-start(bf16[32,64,128]{2,1,0:T(8,128)(2,1)} %collect.1), calls=%async_computation | async-start | bytes 1048576 | tf_op jit(solution)/shard_map/all_to_all | solution.py:484
  53.5 30.6 %copy-start.2 = (bf16[1024,128]{1,0:T(8,128)(2,1)S(1)}, bf16[1024,128]{1,0:T(8,128)(2,1)}, u32[]{:S(2)}) copy-start(bf16[1024,128]{1,0:T(8,128)(2,1)} %get-tuple-element.68.refs_3_) | copy-start | bytes 786436
  53.5 25.1 %collective-permute-start.7 = (bf16[1024,128]{1,0:T(8,128)(2,1)}, bf16[1024,128]{1,0:T(8,128)(2,1)S(1)}, u32[]{:S(2)}, u32[]{:S(2)}) collective-permute-start(bf16[1024,128]{1,0:T(8,128)(2,1)} %get-tuple-element.59), channel_id=1, source_target_pairs={{0,64},{32,96},{64,128},{96,160},{128,192},{160,224},{192,0},{224,... | collective-permute-start | bytes 786440 | tf_op jit(solution)/shard_map/ppermute | solution.py:48
  54.2 24.3 %collective-permute-start.8 = (bf16[1024,128]{1,0:T(8,128)(2,1)}, bf16[1024,128]{1,0:T(8,128)(2,1)}, u32[]{:S(2)}, u32[]{:S(2)}) collective-permute-start(bf16[1024,128]{1,0:T(8,128)(2,1)} %get-tuple-element.60), channel_id=1, source_target_pairs={{0,192},{32,224},{64,0},{96,32},{128,64},{160,96},{192,128},{224,1... | collective-permute-start | bytes 786440 | tf_op jit(solution)/shard_map/ppermute | solution.py:48
  57.7 26.3 %collective-permute-start.9 = (bf16[1024,128]{1,0:T(8,128)(2,1)}, bf16[1024,128]{1,0:T(8,128)(2,1)}, u32[]{:S(2)}, u32[]{:S(2)}) collective-permute-start(bf16[1024,128]{1,0:T(8,128)(2,1)} %get-tuple-element.61), channel_id=1, source_target_pairs={{0,128},{32,160},{64,192},{96,224},{128,0},{160,32},{192,64},{224,... | collective-permute-start | bytes 786440 | tf_op jit(solution)/shard_map/ppermute | solution.py:48
  85.2 8.6 %collective-permute-start.10 = (bf16[2048,128]{1,0:T(8,128)(2,1)S(1)}, bf16[2048,128]{1,0:T(8,128)(2,1)S(1)}, u32[]{:S(2)}, u32[]{:S(2)}) collective-permute-start(bf16[2048,128]{1,0:T(8,128)(2,1)S(1)} %gather_halves.5), channel_id=1, source_target_pairs={{0,32},{32,0},{64,96},{96,64},{128,160},{160,128},{192,224},{224,1... | collective-permute-start | bytes 1572872 | tf_op jit(solution)/shard_map/ppermute | solution.py:48
  85.5 25.6 %collective-permute-start.4 = (bf16[1024,128]{1,0:T(8,128)(2,1)}, bf16[1024,128]{1,0:T(8,128)(2,1)S(1)}, u32[]{:S(2)}, u32[]{:S(2)}) collective-permute-start(bf16[1024,128]{1,0:T(8,128)(2,1)} %get-tuple-element.56), channel_id=1, source_target_pairs={{0,64},{32,96},{64,128},{96,160},{128,192},{160,224},{192,0},{224,... | collective-permute-start | bytes 786440 | tf_op jit(solution)/shard_map/ppermute | solution.py:48
  85.6 25.5 %collective-permute-start.5 = (bf16[1024,128]{1,0:T(8,128)(2,1)}, bf16[1024,128]{1,0:T(8,128)(2,1)S(1)}, u32[]{:S(2)}, u32[]{:S(2)}) collective-permute-start(bf16[1024,128]{1,0:T(8,128)(2,1)} %get-tuple-element.57), channel_id=1, source_target_pairs={{0,192},{32,224},{64,0},{96,32},{128,64},{160,96},{192,128},{224,1... | collective-permute-start | bytes 786440 | tf_op jit(solution)/shard_map/ppermute | solution.py:48
  89.7 27.1 %collective-permute-start.6 = (bf16[1024,128]{1,0:T(8,128)(2,1)}, bf16[1024,128]{1,0:T(8,128)(2,1)S(1)}, u32[]{:S(2)}, u32[]{:S(2)}) collective-permute-start(bf16[1024,128]{1,0:T(8,128)(2,1)} %get-tuple-element.58), channel_id=1, source_target_pairs={{0,128},{32,160},{64,192},{96,224},{128,0},{160,32},{192,64},{224,... | collective-permute-start | bytes 786440 | tf_op jit(solution)/shard_map/ppermute | solution.py:48
  102.0 0.7 copy-start.4
  102.7 23.0 %all-to-all-start.1 = ((bf16[32,32,256]{2,1,0:T(8,128)(2,1)}), bf16[32,32,256]{2,1,0:T(8,128)(2,1)S(1)}, u32[]{:S(2)}, u32[]{:S(2)}) async-start(bf16[32,32,256]{2,1,0:T(8,128)(2,1)} %get-tuple-element.79), calls=%async_computation.1 | async-start | bytes 1048576 | tf_op jit(solution)/shard_map/all_to_all | solution.py:493
  111.1 12.6 %copy-start.5 = (bf16[1024,128]{1,0:T(8,128)(2,1)S(1)}, bf16[1024,128]{1,0:T(8,128)(2,1)}, u32[]{:S(2)}) copy-start(bf16[1024,128]{1,0:T(8,128)(2,1)} %copy-done.4) | copy-start | bytes 786436
  117.5 2.0 %collective-permute-start.11 = (bf16[2048,128]{1,0:T(8,128)(2,1)S(1)}, bf16[2048,128]{1,0:T(8,128)(2,1)S(1)}, u32[]{:S(2)}, u32[]{:S(2)}) collective-permute-start(bf16[2048,128]{1,0:T(8,128)(2,1)S(1)} %gather_halves.6), channel_id=1, source_target_pairs={{0,32},{32,0},{64,96},{96,64},{128,160},{160,128},{192,224},{224,1... | collective-permute-start | bytes 1572872 | tf_op jit(solution)/shard_map/ppermute | solution.py:48
  119.5 27.0 %collective-permute-start.12 = (bf16[1024,128]{1,0:T(8,128)(2,1)}, bf16[1024,128]{1,0:T(8,128)(2,1)S(1)}, u32[]{:S(2)}, u32[]{:S(2)}) collective-permute-start(bf16[1024,128]{1,0:T(8,128)(2,1)} %get-tuple-element.75), channel_id=1, source_target_pairs={{0,64},{32,96},{64,128},{96,160},{128,192},{160,224},{192,0},{224,... | collective-permute-start | bytes 786440 | tf_op jit(solution)/shard_map/ppermute | solution.py:48
  119.5 28.8 %collective-permute-start.13 = (bf16[1024,128]{1,0:T(8,128)(2,1)}, bf16[1024,128]{1,0:T(8,128)(2,1)S(1)}, u32[]{:S(2)}, u32[]{:S(2)}) collective-permute-start(bf16[1024,128]{1,0:T(8,128)(2,1)} %get-tuple-element.76), channel_id=1, source_target_pairs={{0,192},{32,224},{64,0},{96,32},{128,64},{160,96},{192,128},{224,1... | collective-permute-start | bytes 786440 | tf_op jit(solution)/shard_map/ppermute | solution.py:48
  123.7 24.7 %collective-permute-start.14 = (bf16[1024,128]{1,0:T(8,128)(2,1)S(1)}, bf16[1024,128]{1,0:T(8,128)(2,1)S(1)}, u32[]{:S(2)}, u32[]{:S(2)}) collective-permute-start(bf16[1024,128]{1,0:T(8,128)(2,1)S(1)} %copy-done.5), channel_id=1, source_target_pairs={{0,128},{32,160},{64,192},{96,224},{128,0},{160,32},{192,64},{224,... | collective-permute-start | bytes 786440 | tf_op jit(solution)/shard_map/ppermute | solution.py:48
  126.5 21.9 %collective-permute-start.15 = (bf16[64,128]{1,0:T(8,128)(2,1)S(1)}, bf16[64,128]{1,0:T(8,128)(2,1)S(1)}, u32[]{:S(2)}, u32[]{:S(2)}) collective-permute-start(bf16[64,128]{1,0:T(8,128)(2,1)S(1)} %get-tuple-element.80), channel_id=1, source_target_pairs={{0,64},{32,96},{64,128},{96,160},{128,192},{160,224},{192,0},{224,... | collective-permute-start | bytes 49160 | tf_op jit(solution)/shard_map/ppermute | solution.py:48
  126.9 21.5 %collective-permute-start.16 = (bf16[64,128]{1,0:T(8,128)(2,1)S(1)}, bf16[64,128]{1,0:T(8,128)(2,1)S(1)}, u32[]{:S(2)}, u32[]{:S(2)}) collective-permute-start(bf16[64,128]{1,0:T(8,128)(2,1)S(1)} %get-tuple-element.81), channel_id=1, source_target_pairs={{0,192},{32,224},{64,0},{96,32},{128,64},{160,96},{192,128},{224,1... | collective-permute-start | bytes 49160 | tf_op jit(solution)/shard_map/ppermute | solution.py:48
  146.5 7.6 %collective-permute-start.17 = (bf16[64,128]{1,0:T(8,128)(2,1)S(1)}, bf16[64,128]{1,0:T(8,128)(2,1)S(1)}, u32[]{:S(2)}, u32[]{:S(2)}) collective-permute-start(bf16[64,128]{1,0:T(8,128)(2,1)S(1)} %get-tuple-element.82), channel_id=1, source_target_pairs={{0,128},{32,160},{64,192},{96,224},{128,0},{160,32},{192,64},{224,... | collective-permute-start | bytes 49160 | tf_op jit(solution)/shard_map/ppermute | solution.py:48
  154.9 2.0 %collective-permute-start.18 = (bf16[2176,128]{1,0:T(8,128)(2,1)S(1)}, bf16[2176,128]{1,0:T(8,128)(2,1)S(1)}, u32[]{:S(2)}, u32[]{:S(2)}) collective-permute-start(bf16[2176,128]{1,0:T(8,128)(2,1)S(1)} %gather_halves.7), channel_id=1, source_target_pairs={{0,32},{32,0},{64,96},{96,64},{128,160},{160,128},{192,224},{224,1... | collective-permute-start | bytes 1671176 | tf_op jit(solution)/shard_map/ppermute | solution.py:48

commit v3 on v2

v3 whole, which is shorter than its diff:
```python
import functools

import jax
import jax.numpy as jnp
from jax import lax
from jax.experimental import pallas as pl
from jax.experimental.pallas import tpu as pltpu
from jax.sharding import PartitionSpec as P

HEAD_DIM = 128
BLOCK = 128
NEAR = 4
FAR = 64
NEAR_ROWS = 32
FAR_ROWS = 2
WIDE = 8
NARROW = 32
SPAN = WIDE * BLOCK
SPAN_NEAR = WIDE * NEAR_ROWS
SPAN_FAR = WIDE * FAR_ROWS
FAR_ALL = NARROW * SPAN_FAR
FEAT = 2048
PAIR = 2 * HEAD_DIM
SCALE = HEAD_DIM**-0.5
LOG2E = 1.4426950408889634
BLOCKED = -1e30
F32 = jnp.float32
BF16 = jnp.bfloat16

CHIPS = [1, 3, 2, 0]
SENT = len(CHIPS) - 1
PART = 8 * BLOCK
TAIL = 16
STEPS = [(chip, core) for core in range(2) for chip in CHIPS]


def target(at, step):
    chip, core = step
    return ((at // 2 + chip) % 4) * 2 + (at % 2 + core) % 2


def source(at, step):
    chip, core = step
    return ((at // 2 + 4 - chip) % 4) * 2 + (at % 2 + core) % 2


def move(buffer, step):
    return lax.ppermute(buffer, "wide", [(s, target(s, step)) for s in range(WIDE)])


def to_chips(parts):
    return [move(part, (chip, 0)) for part, chip in zip(parts[:SENT], CHIPS)] + [parts[SENT]]


def to_chips_in_turn(parts):
    sides = [move(part, (chip, 0)) for part, chip in zip(parts[:2], CHIPS)]
    *sides, across = lax.optimization_barrier((*sides, parts[2]))
    return [*sides, move(across, (CHIPS[2], 0)), parts[SENT]]


def to_other_core(parts):
    return move(gather_halves(parts), (0, 1))


def copy_all(pairs, sems):
    copies = [pltpu.make_async_copy(src, dst, sems.at[i]) for i, (src, dst) in enumerate(pairs)]
    for copy in copies:
        copy.start()
    return copies


def gather_kernel(*refs):
    n = len(refs) - 2
    ins, out, sems = refs[:n], refs[n], refs[n + 1]
    pairs, row = [], 0
    for ref in ins:
        half = ref.shape[0] // 2
        pairs.append((ref.at[pl.ds(half, half), :], out.at[pl.ds(row, half), :]))
        row += half
    for copy in copy_all(pairs, sems):
        copy.wait()


def gather_halves(parts):
    n = len(parts)
    some = pl.BlockSpec(memory_space=pl.ANY)
    return pl.pallas_call(
        gather_kernel,
        out_shape=jax.ShapeDtypeStruct((sum(part.shape[0] for part in parts) // 2, HEAD_DIM), BF16),
        in_specs=[some] * n,
        out_specs=some,
        scratch_shapes=[pltpu.SemaphoreType.DMA((n,))],
        compiler_params=pltpu.CompilerParams(vmem_limit_bytes=1 << 20),
        name="gather_halves",
    )(*parts)


def nt(a, b):
    return lax.dot_general(a, b, (((1,), (1,)), ((), ())), preferred_element_type=F32)


def nn(a, b):
    return lax.dot_general(a, b, (((1,), (0,)), ((), ())), preferred_element_type=F32)


def tn(a, b):
    return lax.dot_general(a, b, (((0,), (0,)), ((), ())), preferred_element_type=F32)


def pooling(rows, factor):
    shape = (rows, rows * factor)
    group = lax.broadcasted_iota(jnp.int32, shape, 1) // factor
    member = group == lax.broadcasted_iota(jnp.int32, shape, 0)
    return jnp.where(member, F32(1.0 / factor), F32(0.0)).astype(BF16)


def spreading(rows, factor):
    shape = (rows * factor, rows)
    group = lax.broadcasted_iota(jnp.int32, shape, 0) // factor
    member = group == lax.broadcasted_iota(jnp.int32, shape, 1)
    return jnp.where(member, F32(1.0 / factor), F32(0.0)).astype(BF16)


def tail_kernel(at_ref, k_ref, v_ref, *refs):
    n = len(CHIPS)
    tails, (held, far_s, sems) = refs[:n], refs[n:]
    wide_at = at_ref[0]
    strip = BLOCK // 4
    pairs = []
    for i, ref in enumerate((k_ref, v_ref)):
        for r in range(0, BLOCK, strip):
            pairs.append((ref.at[r : r + strip, :], held.at[i, r : r + strip, :]))
    for copy in copy_all(pairs, sems):
        copy.wait()
    pool_near = pooling(NEAR_ROWS, NEAR)
    group = lax.broadcasted_iota(jnp.int32, (TAIL, NEAR_ROWS), 1) // (FAR // NEAR)
    row = lax.broadcasted_iota(jnp.int32, (TAIL, NEAR_ROWS), 0)
    far = None
    for i in range(2):
        near = nn(pool_near, held[i]).astype(BF16)
        pool_far = jnp.where(row == group + i * FAR_ROWS, F32(NEAR / FAR), F32(0.0)).astype(BF16)
        far = nn(pool_far, near) if far is None else far + nn(pool_far, near)
    far_s[...] = far.astype(BF16)
    for part, chip in enumerate(CHIPS):
        for core in range(2):
            for head in range(2):
                column = target(wide_at, (chip, core)) * PAIR + head * HEAD_DIM
                row = (2 * core + head) * TAIL
                tails[part][row : row + TAIL, :] = far_s[:, pl.ds(pl.multiple_of(column, HEAD_DIM), HEAD_DIM)]


def tails_of(at, keys, values):
    n = len(CHIPS)
    some = pl.BlockSpec(memory_space=pl.ANY)
    return pl.pallas_call(
        tail_kernel,
        out_shape=[jax.ShapeDtypeStruct((4 * TAIL, HEAD_DIM), BF16)] * n,
        in_specs=[pl.BlockSpec(memory_space=pltpu.SMEM)] + [some] * 2,
        out_specs=[pl.BlockSpec(memory_space=pltpu.VMEM)] * n,
        scratch_shapes=[
            pltpu.VMEM((2, BLOCK, FEAT), BF16),
            pltpu.VMEM((TAIL, FEAT), BF16),
            pltpu.SemaphoreType.DMA((8,)),
        ],
        compiler_params=pltpu.CompilerParams(vmem_limit_bytes=58 << 20),
        name="tails_of",
    )(at, keys, values)


def pack_kernel(at_ref, k_ref, v_ref, q_ref, g_ref, *refs):
    n = len(CHIPS)
    outs, (held, staged, in_sems, out_sems) = refs[:n], refs[n:]
    wide_at = at_ref[0]
    strip = BLOCK // 4
    pairs = []
    for i, ref in enumerate((k_ref, v_ref, q_ref, g_ref)):
        for r in range(0, BLOCK, strip):
            pairs.append((ref.at[r : r + strip, :], held.at[i, r : r + strip, :]))
    for copy in copy_all(pairs, in_sems):
        copy.wait()
    last = []
    for part, chip in enumerate(CHIPS):
        for core in range(2):
            for head in range(2):
                column = target(wide_at, (chip, core)) * PAIR + head * HEAD_DIM
                columns = pl.ds(pl.multiple_of(column, HEAD_DIM), HEAD_DIM)
                for i in range(4):
                    row = core * PART + (2 * i + head) * BLOCK
                    staged[part, row : row + BLOCK, :] = held[i, :, columns]
        last.append(pltpu.make_async_copy(staged.at[part], outs[part], out_sems.at[part]))
        last[-1].start()
    for copy in last:
        copy.wait()


def pack(at, queries, keys, values, grad_out):
    n = len(CHIPS)
    part = jax.ShapeDtypeStruct((2 * PART, HEAD_DIM), BF16)
    some = pl.BlockSpec(memory_space=pl.ANY)
    return pl.pallas_call(
        pack_kernel,
        out_shape=[part] * n,
        in_specs=[pl.BlockSpec(memory_space=pltpu.SMEM)] + [some] * 4,
        out_specs=[some] * n,
        scratch_shapes=[
            pltpu.VMEM((4, BLOCK, FEAT), BF16),
            pltpu.VMEM((n, *part.shape), BF16),
            pltpu.SemaphoreType.DMA((16,)),
            pltpu.SemaphoreType.DMA((n,)),
        ],
        compiler_params=pltpu.CompilerParams(vmem_limit_bytes=58 << 20),
        cost_estimate=pl.CostEstimate(flops=0, bytes_accessed=4 << 20, transcendentals=0),
        name="pack",
    )(at, keys, values, queries, grad_out)


def arrivals(parts, swapped, place, start=0, rows=PART):
    n = len(CHIPS)
    half = parts[0].shape[0] // 2
    pairs = [(parts[i].at[pl.ds(start, rows), :], place(i)) for i in range(n)]
    return pairs + [(swapped.at[pl.ds(i * half + start, rows), :], place(n + i)) for i in range(n)]


def collect_kernel(at_ref, *refs):
    n = len(CHIPS)
    ins, swapped, out, held, sems = refs[:n], refs[n], refs[n + 1], refs[n + 2], refs[n + 3]
    wide_at = at_ref[0]
    pairs = []
    for head in range(2):
        place = lambda i: held.at[head, source(wide_at, STEPS[i])]
        pairs += arrivals(ins, swapped, place, head * TAIL, TAIL)
    for copy in copy_all(pairs, sems):
        copy.wait()
    shape = (2 * SPAN_FAR, WIDE * TAIL)
    row, column = lax.broadcasted_iota(jnp.int32, shape, 0), lax.broadcasted_iota(jnp.int32, shape, 1)
    inner = row % SPAN_FAR
    wanted = (inner // FAR_ROWS) * TAIL + inner % FAR_ROWS + (row // SPAN_FAR) * FAR_ROWS
    choose = jnp.where(column == wanted, F32(1.0), F32(0.0)).astype(BF16)
    for head in range(2):
        rows = nn(choose, held[head].reshape(WIDE * TAIL, HEAD_DIM)).astype(BF16)
        lanes = slice(head * HEAD_DIM, (head + 1) * HEAD_DIM)
        out[:, :, lanes] = jnp.broadcast_to(rows[None], (NARROW, 2 * SPAN_FAR, HEAD_DIM))


def collect(at, parts, swapped):
    n = len(CHIPS)
    return pl.pallas_call(
        collect_kernel,
        out_shape=jax.ShapeDtypeStruct((NARROW, 2 * SPAN_FAR, PAIR), BF16),
        in_specs=[pl.BlockSpec(memory_space=pltpu.SMEM)] + [pl.BlockSpec(memory_space=pl.ANY)] * (n + 1),
        out_specs=pl.BlockSpec(memory_space=pltpu.VMEM),
        scratch_shapes=[pltpu.VMEM((2, WIDE, TAIL, HEAD_DIM), BF16), pltpu.SemaphoreType.DMA((2 * WIDE,))],
        compiler_params=pltpu.CompilerParams(vmem_limit_bytes=4 << 20),
        name="collect",
    )(at, *parts, swapped)


def attend_kernel(at_ref, *refs):
    n = len(CHIPS)
    ins, swapped, far_ref, outs, far_out = refs[:n], refs[n], refs[n + 1], refs[n + 2 : 2 * n + 2], refs[2 * n + 2]
    held, kn_s, vn_s, o_s, dq_s, dk_s, dv_s, dkn_s, dvn_s, dkf_s, dvf_s, s_s, w_s, d_s, sems = refs[2 * n + 3 :]
    wide_at = at_ref[0]
    far_seen = at_ref[1] * SPAN_FAR
    copies = copy_all(arrivals(ins, swapped, lambda i: held.at[source(wide_at, STEPS[i])]), sems)
    for ref in (dk_s, dv_s, dkn_s, dvn_s, dkf_s, dvf_s):
        ref[...] = jnp.zeros(ref.shape, F32)
    for copy in copies:
        copy.wait()
    pool_near = pooling(NEAR_ROWS, NEAR)
    spread_near = spreading(NEAR_ROWS, NEAR)
    later = lax.broadcasted_iota(jnp.int32, (BLOCK, BLOCK), 0) > lax.broadcasted_iota(
        jnp.int32, (BLOCK, BLOCK), 1
    )
    far_blocked = lax.broadcasted_iota(jnp.int32, (FAR_ALL, 1), 0) >= far_seen
    far_bias = jnp.where(far_blocked, F32(BLOCKED), F32(0.0))
    exponent = SCALE * LOG2E
    wide2 = 2 * BLOCK
    for head in range(2):
        lanes = slice(head * HEAD_DIM, (head + 1) * HEAD_DIM)
        kf = far_ref[:, :SPAN_FAR, lanes].reshape(FAR_ALL, HEAD_DIM)
        vf = far_ref[:, SPAN_FAR:, lanes].reshape(FAR_ALL, HEAD_DIM)

        def rows_of(array, block):
            row = (2 * array + head) * BLOCK
            return held[block, row : row + BLOCK, :]

        key = functools.partial(rows_of, 0)
        value = functools.partial(rows_of, 1)
        query = functools.partial(rows_of, 2)
        grad = functools.partial(rows_of, 3)
        for block in range(WIDE):
            near_rows = slice(block * NEAR_ROWS, (block + 1) * NEAR_ROWS)
            kn_s[head, near_rows, :] = nn(pool_near, key(block)).astype(BF16)
            vn_s[head, near_rows, :] = nn(pool_near, value(block)).astype(BF16)
        for pair in range(WIDE // 2):
            blocks = (2 * pair, 2 * pair + 1)
            befores = tuple(max(b - 1, 0) for b in blocks)
            qs, gs = [query(b) for b in blocks], [grad(b) for b in blocks]
            q, g = jnp.concatenate(qs, axis=0), jnp.concatenate(gs, axis=0)
            near = 2 * NEAR_ROWS * pair + NEAR_ROWS
            far_from = wide2 + near
            total = far_from + FAR_ALL
            halves = [slice(b * BLOCK, (b + 1) * BLOCK) for b in range(2)]
            for b, cols in enumerate(halves):
                if blocks[b] == 0:
                    s_s[0:BLOCK, cols] = jnp.full((BLOCK, BLOCK), BLOCKED, F32)
                else:
                    s_s[0:BLOCK, cols] = nt(key(befores[b]), qs[b])
                s_s[BLOCK:wide2, cols] = jnp.where(later, F32(BLOCKED), nt(key(blocks[b]), qs[b]))
            s_s[wide2:far_from, :] = nt(kn_s[head, 0:near, :], q)
            s_s[far_from - NEAR_ROWS : far_from, 0:BLOCK] = jnp.full((NEAR_ROWS, BLOCK), BLOCKED, F32)
            for i in range(0, FAR_ALL, BLOCK):
                s_s[far_from + i : far_from + i + BLOCK, :] = nt(kf[i : i + BLOCK, :], q) + far_bias[i : i + BLOCK]
            chunks = [(0, BLOCK), (BLOCK, BLOCK)]
            chunks += [(wide2 + i, min(BLOCK, near - i)) for i in range(0, near, BLOCK)]
            chunks += [(far_from + i, BLOCK) for i in range(0, FAR_ALL, BLOCK)]
            top = None
            for start, size in chunks:
                here = jnp.max(s_s[start : start + size, :].reshape(size // 8, 8, wide2), axis=0)
                top = here if top is None else jnp.maximum(top, here)
            top = jnp.max(top, axis=0, keepdims=True)
            norm = None
            for start, size in chunks:
                e = jnp.exp2((s_s[start : start + size, :] - top) * exponent)
                w_s[start : start + size, :] = e.astype(BF16)
                here = jnp.sum(e.reshape(size // 8, 8, wide2), axis=0)
                norm = here if norm is None else norm + here
            inverse = 1.0 / jnp.sum(norm, axis=0, keepdims=True)
            sides = [
                tn(value(befores[b]), w_s[0:BLOCK, cols]) + tn(value(blocks[b]), w_s[BLOCK:wide2, cols])
                for b, cols in enumerate(halves)
            ]
            attended = jnp.concatenate(sides, axis=1)
            attended += tn(vn_s[head, 0:near, :], w_s[wide2:far_from, :])
            attended += tn(vf, w_s[far_from:total, :])
            attended = (attended * inverse).astype(BF16).astype(F32)
            q_rows = slice(pair * wide2, (pair + 1) * wide2)
            o_s[head, q_rows, :] = attended.T.astype(BF16)
            grad_t = g.astype(F32).T
            row_dot = jnp.sum(grad_t * attended, axis=0, keepdims=True) * inverse
            g = (grad_t * inverse).T.astype(BF16)
            gs = [g[cols] for cols in halves]

            def put(start, size, cols, dprob, dot):
                d_s[start : start + size, cols] = (w_s[start : start + size, cols].astype(F32) * (dprob - dot)).astype(BF16)

            every = slice(0, wide2)
            for b, cols in enumerate(halves):
                put(0, BLOCK, cols, nt(value(befores[b]), gs[b]), row_dot[:, cols])
                put(BLOCK, BLOCK, cols, nt(value(blocks[b]), gs[b]), row_dot[:, cols])
            put(wide2, near, every, nt(vn_s[head, 0:near, :], g), row_dot)
            for i in range(0, FAR_ALL, BLOCK):
                put(far_from + i, BLOCK, every, nt(vf[i : i + BLOCK, :], g), row_dot)
            sides = []
            for b, cols in enumerate(halves):
                before, own = (slice(at * BLOCK, (at + 1) * BLOCK) for at in (befores[b], blocks[b]))
                sides.append(tn(key(befores[b]), d_s[0:BLOCK, cols]) + tn(key(blocks[b]), d_s[BLOCK:wide2, cols]))
                if blocks[b] > 0:
                    dk_s[head, before, :] += nn(d_s[0:BLOCK, cols], qs[b])
                    dv_s[head, before, :] += nn(w_s[0:BLOCK, cols], gs[b])
                dk_s[head, own, :] += nn(d_s[BLOCK:wide2, cols], qs[b])
                dv_s[head, own, :] += nn(w_s[BLOCK:wide2, cols], gs[b])
            grad_query = jnp.concatenate(sides, axis=1)
            grad_query += tn(kn_s[head, 0:near, :], d_s[wide2:far_from, :])
            grad_query += tn(kf, d_s[far_from:total, :])
            dq_s[head, q_rows, :] = (grad_query * SCALE).T.astype(BF16)
            dkn_s[head, 0:near, :] += nn(d_s[wide2:far_from, :], q)
            dvn_s[head, 0:near, :] += nn(w_s[wide2:far_from, :], g)
            dkf_s[head] += nn(d_s[far_from:total, :], q)
            dvf_s[head] += nn(w_s[far_from:total, :], g)

        far_out[:, :SPAN_FAR, lanes] = (dkf_s[head] * SCALE).astype(BF16).reshape(NARROW, SPAN_FAR, HEAD_DIM)
        far_out[:, SPAN_FAR:, lanes] = dvf_s[head].astype(BF16).reshape(NARROW, SPAN_FAR, HEAD_DIM)
        for block in range(WIDE):
            rows = slice(block * BLOCK, (block + 1) * BLOCK)
            near_rows = slice(block * NEAR_ROWS, (block + 1) * NEAR_ROWS)
            dk_s[head, rows, :] = (dk_s[head, rows, :] + nn(spread_near, dkn_s[head, near_rows, :].astype(BF16))) * SCALE
            dv_s[head, rows, :] = dv_s[head, rows, :] + nn(spread_near, dvn_s[head, near_rows, :].astype(BF16))
        for part, chip in enumerate(CHIPS):
            for core in range(2):
                rows = pl.ds(pl.multiple_of(target(wide_at, (chip, core)) * BLOCK, BLOCK), BLOCK)
                for i, ref in enumerate((o_s, dq_s, dk_s, dv_s)):
                    row = core * PART + (2 * i + head) * BLOCK
                    outs[part][row : row + BLOCK, :] = ref[head, rows, :].astype(BF16)


def attend(at, parts, swapped, far):
    n = len(CHIPS)
    vmem, some = pl.BlockSpec(memory_space=pltpu.VMEM), pl.BlockSpec(memory_space=pl.ANY)
    both = lambda rows, kind: pltpu.VMEM((2, rows, HEAD_DIM), kind)
    lists = lambda kind: pltpu.VMEM((SPAN, 2 * BLOCK), kind)
    outs = pl.pallas_call(
        attend_kernel,
        out_shape=[jax.ShapeDtypeStruct((2 * PART, HEAD_DIM), BF16)] * n
        + [jax.ShapeDtypeStruct((NARROW, 2 * SPAN_FAR, PAIR), BF16)],
        in_specs=[pl.BlockSpec(memory_space=pltpu.SMEM)] + [some] * (n + 1) + [vmem],
        out_specs=[vmem] * (n + 1),
        scratch_shapes=[pltpu.VMEM((WIDE, PART, HEAD_DIM), BF16)]
        + [both(SPAN_NEAR, BF16)] * 2 + [both(SPAN, BF16)] * 2 + [both(SPAN, F32)] * 2
        + [both(SPAN_NEAR, F32)] * 2 + [both(FAR_ALL, F32)] * 2
        + [lists(F32), lists(BF16), lists(BF16), pltpu.SemaphoreType.DMA((WIDE,))],
        compiler_params=pltpu.CompilerParams(vmem_limit_bytes=20 << 20),
        cost_estimate=pl.CostEstimate(flops=3_200_000_000, bytes_accessed=4 << 20, transcendentals=2 << 20),
        name="attend",
    )(at, *parts, swapped, far)
    return outs[:n], outs[n]


def total_kernel(at_ref, terms_ref, *outs):
    wide_at = at_ref[0]
    total = jnp.sum(terms_ref[...].astype(F32), axis=0).astype(BF16)
    shape = (TAIL, 2 * SPAN_FAR)
    row, column = lax.broadcasted_iota(jnp.int32, shape, 0), lax.broadcasted_iota(jnp.int32, shape, 1)
    for part, chip in enumerate(CHIPS):
        for core in range(2):
            first = target(wide_at, (chip, core)) * FAR_ROWS
            wanted = (row // FAR_ROWS) * SPAN_FAR + first + row % FAR_ROWS
            choose = jnp.where((column == wanted) & (row < 2 * FAR_ROWS), F32(1.0), F32(0.0)).astype(BF16)
            rows = nn(choose, total).astype(BF16)
            for head in range(2):
                at = (2 * core + head) * TAIL
                outs[part][at : at + TAIL, :] = rows[:, head * HEAD_DIM : (head + 1) * HEAD_DIM]


def total(at, terms):
    n = len(CHIPS)
    vmem = pl.BlockSpec(memory_space=pltpu.VMEM)
    return pl.pallas_call(
        total_kernel,
        out_shape=[jax.ShapeDtypeStruct((4 * TAIL, HEAD_DIM), BF16)] * n,
        in_specs=[pl.BlockSpec(memory_space=pltpu.SMEM), vmem],
        out_specs=[vmem] * n,
        compiler_params=pltpu.CompilerParams(vmem_limit_bytes=4 << 20),
        name="total",
    )(at, terms)


def unpack_kernel(at_ref, *refs):
    n = len(CHIPS)
    ins, swapped, tails, outs = refs[:n], refs[n], refs[n + 1 : 2 * n + 1], refs[2 * n + 1 : 2 * n + 5]
    held, far_s, sums, sems, far_sems, out_sems = refs[2 * n + 5 :]
    wide_at = at_ref[0]
    copies = copy_all(arrivals(ins, swapped, lambda i: held.at[i]), sems)
    rows = 2 * TAIL
    pairs = [(tails[i].at[pl.ds(0, rows), :], far_s.at[i]) for i in range(n)]
    pairs += [(swapped.at[pl.ds(n * PART + i * rows, rows), :], far_s.at[n + i]) for i in range(n)]
    for copy in copy_all(pairs, far_sems):
        copy.wait()
    for part, step in enumerate(STEPS):
        copies[part].wait()
        block = source(wide_at, step)
        for head in range(2):
            columns = pl.ds(pl.multiple_of(block * PAIR + head * HEAD_DIM, HEAD_DIM), HEAD_DIM)
            far = far_s[part, head * TAIL : (head + 1) * TAIL, :].astype(F32) * (1.0 / FAR)
            for i in range(4):
                row = (2 * i + head) * BLOCK
                piece = held[part, row : row + BLOCK, :]
                if i >= 2:
                    terms = piece.astype(F32)
                    at = (i - 2) * FAR_ROWS
                    both = [terms[r * FAR : (r + 1) * FAR] + far[at + r : at + r + 1] for r in range(FAR_ROWS)]
                    piece = jnp.concatenate(both, axis=0).astype(BF16)
                sums[i, :, columns] = piece
    strip = BLOCK // 4
    pairs = []
    for i in range(4):
        for r in range(0, BLOCK, strip):
            pairs.append((sums.at[i, r : r + strip, :], outs[i].at[r : r + strip, :]))
    for copy in copy_all(pairs, out_sems):
        copy.wait()


def unpack(at, parts, swapped, tails):
    n = len(CHIPS)
    some = pl.BlockSpec(memory_space=pl.ANY)
    return pl.pallas_call(
        unpack_kernel,
        out_shape=[jax.ShapeDtypeStruct((BLOCK, FEAT), BF16)] * 4,
        in_specs=[pl.BlockSpec(memory_space=pltpu.SMEM)] + [some] * (2 * n + 1),
        out_specs=[some] * 4,
        scratch_shapes=[
            pltpu.VMEM((WIDE, PART, HEAD_DIM), BF16),
            pltpu.VMEM((WIDE, 2 * TAIL, HEAD_DIM), BF16),
            pltpu.VMEM((4, BLOCK, FEAT), BF16),
            pltpu.SemaphoreType.DMA((WIDE,)),
            pltpu.SemaphoreType.DMA((WIDE,)),
            pltpu.SemaphoreType.DMA((16,)),
        ],
        compiler_params=pltpu.CompilerParams(vmem_limit_bytes=8 << 20),
        name="unpack",
    )(at, *parts, swapped, *tails)


def shards(queries, keys, values, grad_out):
    at = jnp.stack([lax.axis_index("wide"), lax.axis_index("narrow")]).astype(jnp.int32)
    tails = to_chips(tails_of(at, keys, values))
    parts = pack(at, queries, keys, values, grad_out)
    tails, parts = lax.optimization_barrier((list(tails), list(parts)))
    swapped = to_other_core(tails)
    swapped, *parts = lax.optimization_barrier((swapped, *parts))
    parts = to_chips_in_turn(parts)
    far = lax.all_to_all(collect(at, tails, swapped), "narrow", 0, 0, tiled=True)
    far, *parts = lax.optimization_barrier((far, *parts))
    outs, terms = attend(at, parts, to_other_core(parts), far)
    outs = to_chips_in_turn(outs)
    tails = to_chips(total(at, lax.all_to_all(terms, "narrow", 0, 0, tiled=True)))
    return tuple(unpack(at, outs, to_other_core([*outs, *tails]), tails))


def solution(mesh):
    rows = P(("narrow", "wide"), None)
    return jax.shard_map(
        shards, mesh=mesh, in_specs=(rows,) * 4, out_specs=(rows,) * 4, check_vma=False
    )
```

time: 163 us -> 160 us (0.982)
  waiting for transfers between devices: 72.7 us -> 81.2 us
  Pallas kernels: 32.2 us -> 25.5 us
  starting transfers between devices: 54.6 us -> 49.8 us
    ppermute x19 -> x15, waiting for transfers between devices: 62.1 us -> 72.8 us  [move(): lax.ppermute(buffer, 'wide', [(s, target(s, step)) for s in range(WIDE)])]
    all_to_all x1, waiting for transfers between devices: 10.6 us -> 3.02 us  [shards(): lax.all_to_all(collect(at, tails, swapped), 'narrow', 0, 0, tiled=True)]
    all_to_all x1, waiting for transfers between devices: 0.01 us -> 5.35 us  [shards(): lax.all_to_all(terms, 'narrow', 0, 0, tiled=True)]
    ppermute x19 -> x15, starting transfers between devices: 37.7 us -> 32.7 us  [move(): lax.ppermute(buffer, 'wide', [(s, target(s, step)) for s in range(WIDE)])]
    pallas_call x4 -> x3, Pallas kernels: 3.35 us -> 0.4 us  [gather_halves(): pl.pallas_call(gather_kernel, out_shape=jax.ShapeDtypeStruct((sum((part.s...]
    pallas_call x1, Pallas kernels: 5.6 us -> 2.98 us  [unpack(): pl.pallas_call(unpack_kernel, out_shape=[jax.ShapeDtypeStruct((BLOCK, FEA...]
  transfers between devices with their start and end apart: 21 -> 17, of which waited for: 10 -> 13; matrix products, arithmetic and copies ran while one was open for 0% -> 0% of each run, Pallas kernels for 11% -> 4%
where the time goes in v3:
time: 160 us; the launch traced here: 159 us
  waiting for transfers between devices  81.2 us (51%)
  starting transfers between devices  49.8 us (31%)
  Pallas kernels  25.5 us (16%)
    ppermute x15, waiting for transfers between devices, move(): lax.ppermute(buffer, 'wide', [(s, target(s, step)) for s in range(WIDE)])  72.8 us
    ppermute x15, starting transfers between devices, move(): lax.ppermute(buffer, 'wide', [(s, target(s, step)) for s in range(WIDE)])  32.7 us
    pallas_call x1, Pallas kernels, attend(): pl.pallas_call(attend_kernel, out_shape=[jax.ShapeDtypeStruct((2 * PART,...  12.5 us
    all_to_all x1, starting transfers between devices, shards(): lax.all_to_all(collect(at, tails, swapped), 'narrow', 0, 0, tiled=True)  8.53 us
    all_to_all x1, starting transfers between devices, shards(): lax.all_to_all(terms, 'narrow', 0, 0, tiled=True)  8.52 us
    all_to_all x1, waiting for transfers between devices, shards(): lax.all_to_all(terms, 'narrow', 0, 0, tiled=True)  5.35 us
    pallas_call x1, Pallas kernels, pack(): pl.pallas_call(pack_kernel, out_shape=[part] * n, in_specs=[pl.BlockSpec(...  3.88 us
  transfers between devices with their start and end apart: 17, of which 13 were waited for; matrix products, arithmetic and copies ran while one was open for 0% of the time, Pallas kernels for 4%

profile of v3, /device:TPU:34, one launch (start us, length us, event | category | flops | bytes accessed | tf_op | source)
XLA Modules:
  0.0 158.9 jit_solution(12414338574587212833)
XLA Ops:
  0.6 0.7 pad_add_fusion.at_ref
  1.3 3.1 %tails_of.1 = (bf16[64,128]{1,0:T(8,128)(2,1)}, bf16[64,128]{1,0:T(8,128)(2,1)}, bf16[64,128]{1,0:T(8,128)(2,1)}, bf16[64,128]{1,0:T(8,128)(2,1)}) custom-call(s32[2]{0:T(128)} %pad_add_fusion.at_ref, bf16[128,2048]{1,0:T(8,128)(2,1)} %k_ref.3, bf16[128,2048]{1,0:T(8,128)(2,1)} %v_ref.3), custom_call_target="tpu_custom_call" | custom-call | tf_op jit(solution)/shard_map/tails_of/pallas_call | solution.py:155
  4.4 3.3 %collective-permute-start = (bf16[64,128]{1,0:T(8,128)(2,1)}, bf16[64,128]{1,0:T(8,128)(2,1)S(1)}, u32[]{:S(2)}, u32[]{:S(2)}) collective-permute-start(bf16[64,128]{1,0:T(8,128)(2,1)} %get-tuple-element.45), channel_id=1, source_target_pairs={{0,64},{32,96},{64,128},{96,160},{128,192},{160,224},{192,0},{224,... | collective-permute-start | bytes 49160 | tf_op jit(solution)/shard_map/ppermute | solution.py:48
  7.7 2.2 %collective-permute-start.1 = (bf16[64,128]{1,0:T(8,128)(2,1)}, bf16[64,128]{1,0:T(8,128)(2,1)S(1)}, u32[]{:S(2)}, u32[]{:S(2)}) collective-permute-start(bf16[64,128]{1,0:T(8,128)(2,1)} %get-tuple-element.46), channel_id=1, source_target_pairs={{0,192},{32,224},{64,0},{96,32},{128,64},{160,96},{192,128},{224,1... | collective-permute-start | bytes 49160 | tf_op jit(solution)/shard_map/ppermute | solution.py:48
  10.0 4.9 %collective-permute-start.2 = (bf16[64,128]{1,0:T(8,128)(2,1)}, bf16[64,128]{1,0:T(8,128)(2,1)S(1)}, u32[]{:S(2)}, u32[]{:S(2)}) collective-permute-start(bf16[64,128]{1,0:T(8,128)(2,1)} %get-tuple-element.47), channel_id=1, source_target_pairs={{0,128},{32,160},{64,192},{96,224},{128,0},{160,32},{192,64},{224,... | collective-permute-start | bytes 49160 | tf_op jit(solution)/shard_map/ppermute | solution.py:48
  14.9 3.9 %pack.1 = (bf16[2048,128]{1,0:T(8,128)(2,1)}, bf16[2048,128]{1,0:T(8,128)(2,1)}, bf16[2048,128]{1,0:T(8,128)(2,1)}, bf16[2048,128]{1,0:T(8,128)(2,1)}) custom-call(s32[2]{0:T(128)} %pad_add_fusion.at_ref, bf16[128,2048]{1,0:T(8,128)(2,1)} %k_ref.3, bf16[128,2048]{1,0:T(8,128)(2,1)} %v_ref.3, bf16[128,2048]{1,0:T(8,128)(2,1)} %q_ref.1, bf16[128,2048]{1,0:T(8,128)(2,1)} %g_ref.1), custom_call_target="tpu_custom_call" | custom-call | bytes 4194304 | tf_op jit(solution)/shard_map/pack/pallas_call | solution.py:200
  18.8 0.0 copy-start.4
  18.8 0.0 copy-start
  18.8 0.0 collective-permute-done.refs_0_
  18.8 0.0 collective-permute-done.1.refs_1_
  18.8 0.0 collective-permute-done.2.refs_2_
  18.8 0.1 gather_halves.3
  18.9 0.1 collective-permute-start.3
  19.0 1.2 collective-permute-done.3.refs_4_
  20.2 0.3 collective-permute-start.4
  20.6 3.8 %collective-permute-start.5 = (bf16[2048,128]{1,0:T(8,128)(2,1)}, bf16[2048,128]{1,0:T(8,128)(2,1)S(1)}, u32[]{:S(2)}, u32[]{:S(2)}) collective-permute-start(bf16[2048,128]{1,0:T(8,128)(2,1)} %get-tuple-element.63), channel_id=1, source_target_pairs={{0,192},{32,224},{64,0},{96,32},{128,64},{160,96},{192,128},{224,1... | collective-permute-start | bytes 1572872 | tf_op jit(solution)/shard_map/ppermute | solution.py:48
  24.4 1.9 %collect.1 = bf16[32,32,256]{2,1,0:T(8,128)(2,1)} custom-call(s32[2]{0:T(128)S(1)} %copy-done.2, bf16[64,128]{1,0:T(8,128)(2,1)S(1)} %collective-permute-done.refs_0_, bf16[64,128]{1,0:T(8,128)(2,1)S(1)} %collective-permute-done.1.refs_1_, bf16[64,128]{1,0:T(8,128)(2,1)S(1)} %collective-permute-done.2.refs_2_, bf16[64,128]{1,0:T(8,128)(2,1)S(1)} %copy-done.1, ...), custom_call_target="tpu_custom_call" | custom-call | tf_op jit(solution)/shard_map/collect/pallas_call | solution.py:247
  26.3 8.5 %all-to-all-start = ((bf16[32,32,256]{2,1,0:T(8,128)(2,1)}), bf16[32,32,256]{2,1,0:T(8,128)(2,1)S(1)}, u32[]{:S(2)}, u32[]{:S(2)}) async-start(bf16[32,32,256]{2,1,0:T(8,128)(2,1)} %collect.1), calls=%async_computation | async-start | bytes 1048576 | tf_op jit(solution)/shard_map/all_to_all | solution.py:502
  34.8 12.7 %collective-permute-done.4.refs_0_ = bf16[2048,128]{1,0:T(8,128)(2,1)S(1)} collective-permute-done((bf16[2048,128]{1,0:T(8,128)(2,1)}, bf16[2048,128]{1,0:T(8,128)(2,1)S(1)}, u32[]{:S(2)}, u32[]{:S(2)}) %collective-permute-start.4) | collective-permute-done | bytes 524320 | tf_op jit(solution)/shard_map/ppermute | solution.py:48
  47.5 0.2 collective-permute-done.5.refs_1_
  47.7 3.9 %collective-permute-start.6 = (bf16[2048,128]{1,0:T(8,128)(2,1)S(1)}, bf16[2048,128]{1,0:T(8,128)(2,1)S(1)}, u32[]{:S(2)}, u32[]{:S(2)}) collective-permute-start(bf16[2048,128]{1,0:T(8,128)(2,1)S(1)} %copy-done.4), channel_id=1, source_target_pairs={{0,128},{32,160},{64,192},{96,224},{128,0},{160,32},{192,64},{224,... | collective-permute-start | bytes 1572872 | tf_op jit(solution)/shard_map/ppermute | solution.py:48
  51.6 3.0 %all-to-all-done.refs_5_ = bf16[32,32,256]{2,1,0:T(8,128)(2,1)S(1)} async-done(((bf16[32,32,256]{2,1,0:T(8,128)(2,1)}), bf16[32,32,256]{2,1,0:T(8,128)(2,1)S(1)}, u32[]{:S(2)}, u32[]{:S(2)}) %all-to-all-start) | async-done | bytes 524320 | tf_op jit(solution)/shard_map/all_to_all | solution.py:502
  54.6 24.4 %collective-permute-done.6.refs_2_ = bf16[2048,128]{1,0:T(8,128)(2,1)S(1)} collective-permute-done((bf16[2048,128]{1,0:T(8,128)(2,1)S(1)}, bf16[2048,128]{1,0:T(8,128)(2,1)S(1)}, u32[]{:S(2)}, u32[]{:S(2)}) %collective-permute-start.6) | collective-permute-done | bytes 524320 | tf_op jit(solution)/shard_map/ppermute | solution.py:48
  79.0 0.1 gather_halves.4
  79.1 0.3 collective-permute-start.7
  79.4 2.6 %collective-permute-done.7.refs_4_ = bf16[4096,128]{1,0:T(8,128)(2,1)S(1)} collective-permute-done((bf16[4096,128]{1,0:T(8,128)(2,1)S(1)}, bf16[4096,128]{1,0:T(8,128)(2,1)S(1)}, u32[]{:S(2)}, u32[]{:S(2)}) %collective-permute-start.7) | collective-permute-done | bytes 1048608 | tf_op jit(solution)/shard_map/ppermute | solution.py:48
  82.0 12.5 %attend.1 = (bf16[2048,128]{1,0:T(8,128)(2,1)}, bf16[2048,128]{1,0:T(8,128)(2,1)}, bf16[2048,128]{1,0:T(8,128)(2,1)S(1)}, bf16[2048,128]{1,0:T(8,128)(2,1)S(1)}, bf16[32,32,256]{2,1,0:T(8,128)(2,1)}) custom-call(s32[2]{0:T(128)S(1)} %copy-done.2, bf16[2048,128]{1,0:T(8,128)(2,1)S(1)} %collective-permute-done.4.refs_0_, ...), custom_call_target="tpu_custom_call" | custom-call | flops 3200000000 | bytes 4194304 | tf_op jit(solution)/shard_map/attend/pallas_call | solution.py:392
  94.5 0.0 copy-start.3
  94.5 0.8 copy-done.3
  95.3 0.0 collective-permute-start.8
  95.3 4.1 %collective-permute-start.9 = (bf16[2048,128]{1,0:T(8,128)(2,1)}, bf16[2048,128]{1,0:T(8,128)(2,1)S(1)}, u32[]{:S(2)}, u32[]{:S(2)}) collective-permute-start(bf16[2048,128]{1,0:T(8,128)(2,1)} %get-tuple-element.75), channel_id=1, source_target_pairs={{0,192},{32,224},{64,0},{96,32},{128,64},{160,96},{192,128},{224,1... | collective-permute-start | bytes 1572872 | tf_op jit(solution)/shard_map/ppermute | solution.py:48
  99.5 8.5 %all-to-all-start.1 = ((bf16[32,32,256]{2,1,0:T(8,128)(2,1)}), bf16[32,32,256]{2,1,0:T(8,128)(2,1)S(1)}, u32[]{:S(2)}, u32[]{:S(2)}) async-start(bf16[32,32,256]{2,1,0:T(8,128)(2,1)} %get-tuple-element.81), calls=%async_computation.1 | async-start | bytes 1048576 | tf_op jit(solution)/shard_map/all_to_all | solution.py:506
  108.0 13.0 %collective-permute-done.8.refs_0_ = bf16[2048,128]{1,0:T(8,128)(2,1)S(1)} collective-permute-done((bf16[2048,128]{1,0:T(8,128)(2,1)}, bf16[2048,128]{1,0:T(8,128)(2,1)S(1)}, u32[]{:S(2)}, u32[]{:S(2)}) %collective-permute-start.8) | collective-permute-done | bytes 524320 | tf_op jit(solution)/shard_map/ppermute | solution.py:48
  121.0 1.0 collective-permute-done.9.refs_1_
  122.0 2.8 %collective-permute-start.10 = (bf16[2048,128]{1,0:T(8,128)(2,1)}, bf16[2048,128]{1,0:T(8,128)(2,1)S(1)}, u32[]{:S(2)}, u32[]{:S(2)}) collective-permute-start(bf16[2048,128]{1,0:T(8,128)(2,1)} %copy-done.3), channel_id=1, source_target_pairs={{0,128},{32,160},{64,192},{96,224},{128,0},{160,32},{192,64},{224,... | collective-permute-start | bytes 1572872 | tf_op jit(solution)/shard_map/ppermute | solution.py:48
  124.8 5.3 %all-to-all-done.1.terms_ref = bf16[32,32,256]{2,1,0:T(8,128)(2,1)S(1)} async-done(((bf16[32,32,256]{2,1,0:T(8,128)(2,1)}), bf16[32,32,256]{2,1,0:T(8,128)(2,1)S(1)}, u32[]{:S(2)}, u32[]{:S(2)}) %all-to-all-start.1) | async-done | bytes 524320 | tf_op jit(solution)/shard_map/all_to_all | solution.py:506
  130.1 0.8 total.1
  130.9 0.1 collective-permute-start.11
  131.0 4.1 %collective-permute-start.12 = (bf16[64,128]{1,0:T(8,128)(2,1)S(1)}, bf16[64,128]{1,0:T(8,128)(2,1)S(1)}, u32[]{:S(2)}, u32[]{:S(2)}) collective-permute-start(bf16[64,128]{1,0:T(8,128)(2,1)S(1)} %get-tuple-element.83), channel_id=1, source_target_pairs={{0,192},{32,224},{64,0},{96,32},{128,64},{160,96},{192,128},{224,1... | collective-permute-start | bytes 49160 | tf_op jit(solution)/shard_map/ppermute | solution.py:48
  135.1 2.6 %collective-permute-start.13 = (bf16[64,128]{1,0:T(8,128)(2,1)S(1)}, bf16[64,128]{1,0:T(8,128)(2,1)S(1)}, u32[]{:S(2)}, u32[]{:S(2)}) collective-permute-start(bf16[64,128]{1,0:T(8,128)(2,1)S(1)} %get-tuple-element.84), channel_id=1, source_target_pairs={{0,128},{32,160},{64,192},{96,224},{128,0},{160,32},{192,64},{224,... | collective-permute-start | bytes 49160 | tf_op jit(solution)/shard_map/ppermute | solution.py:48
  137.7 2.1 %collective-permute-done.11.refs_4_.refs_5_ = bf16[64,128]{1,0:T(8,128)(2,1)S(1)} collective-permute-done((bf16[64,128]{1,0:T(8,128)(2,1)S(1)}, bf16[64,128]{1,0:T(8,128)(2,1)S(1)}, u32[]{:S(2)}, u32[]{:S(2)}) %collective-permute-start.11) | collective-permute-done | bytes 16416 | tf_op jit(solution)/shard_map/ppermute | solution.py:48
  139.8 11.5 %collective-permute-done.12.refs_5_.refs_6_ = bf16[64,128]{1,0:T(8,128)(2,1)S(1)} collective-permute-done((bf16[64,128]{1,0:T(8,128)(2,1)S(1)}, bf16[64,128]{1,0:T(8,128)(2,1)S(1)}, u32[]{:S(2)}, u32[]{:S(2)}) %collective-permute-start.12) | collective-permute-done | bytes 16416 | tf_op jit(solution)/shard_map/ppermute | solution.py:48
  151.3 1.4 collective-permute-done.13.refs_6_.refs_7_
  152.7 0.0 collective-permute-done.10.refs_2_
  152.7 0.2 gather_halves.5
  152.9 0.1 collective-permute-start.14
  153.0 2.7 %collective-permute-done.14.refs_4_ = bf16[4224,128]{1,0:T(8,128)(2,1)S(1)} collective-permute-done((bf16[4224,128]{1,0:T(8,128)(2,1)S(1)}, bf16[4224,128]{1,0:T(8,128)(2,1)S(1)}, u32[]{:S(2)}, u32[]{:S(2)}) %collective-permute-start.14) | collective-permute-done | bytes 1081376 | tf_op jit(solution)/shard_map/ppermute | solution.py:48
  155.7 3.0 %unpack.1 = (bf16[128,2048]{1,0:T(8,128)(2,1)}, bf16[128,2048]{1,0:T(8,128)(2,1)}, bf16[128,2048]{1,0:T(8,128)(2,1)}, bf16[128,2048]{1,0:T(8,128)(2,1)}) custom-call(s32[2]{0:T(128)S(1)} %copy-done.2, bf16[2048,128]{1,0:T(8,128)(2,1)S(1)} %collective-permute-done.8.refs_0_, bf16[2048,128]{1,0:T(8,128)(2,1)S(1)} %collective-permute-done.9.refs_1_, ...), custom_call_target="tpu_custom_call" | custom-call | tf_op jit(solution)/shard_map/unpack/pallas_call | solution.py:476
  (6 shorter events, 0.0 us)
Async XLA Ops:
  4.4 14.5 %copy-start.1 = (bf16[64,128]{1,0:T(8,128)(2,1)S(1)}, bf16[64,128]{1,0:T(8,128)(2,1)}, u32[]{:S(2)}) copy-start(bf16[64,128]{1,0:T(8,128)(2,1)} %get-tuple-element.56.refs_3_) | copy-start | bytes 49156
  4.4 14.4 %collective-permute-start = (bf16[64,128]{1,0:T(8,128)(2,1)}, bf16[64,128]{1,0:T(8,128)(2,1)S(1)}, u32[]{:S(2)}, u32[]{:S(2)}) collective-permute-start(bf16[64,128]{1,0:T(8,128)(2,1)} %get-tuple-element.45), channel_id=1, source_target_pairs={{0,64},{32,96},{64,128},{96,160},{128,192},{160,224},{192,0},{224,... | collective-permute-start | bytes 49160 | tf_op jit(solution)/shard_map/ppermute | solution.py:48
  7.7 11.1 %collective-permute-start.1 = (bf16[64,128]{1,0:T(8,128)(2,1)}, bf16[64,128]{1,0:T(8,128)(2,1)S(1)}, u32[]{:S(2)}, u32[]{:S(2)}) collective-permute-start(bf16[64,128]{1,0:T(8,128)(2,1)} %get-tuple-element.46), channel_id=1, source_target_pairs={{0,192},{32,224},{64,0},{96,32},{128,64},{160,96},{192,128},{224,1... | collective-permute-start | bytes 49160 | tf_op jit(solution)/shard_map/ppermute | solution.py:48
  10.0 14.4 %copy-start.2 = (s32[2]{0:T(128)S(1)}, s32[2]{0:T(128)}, u32[]{:S(2)}) copy-start(s32[2]{0:T(128)} %pad_add_fusion.at_ref) | copy-start | bytes 28
  10.0 8.9 %collective-permute-start.2 = (bf16[64,128]{1,0:T(8,128)(2,1)}, bf16[64,128]{1,0:T(8,128)(2,1)S(1)}, u32[]{:S(2)}, u32[]{:S(2)}) collective-permute-start(bf16[64,128]{1,0:T(8,128)(2,1)} %get-tuple-element.47), channel_id=1, source_target_pairs={{0,128},{32,160},{64,192},{96,224},{128,0},{160,32},{192,64},{224,... | collective-permute-start | bytes 49160 | tf_op jit(solution)/shard_map/ppermute | solution.py:48
  18.8 28.9 %copy-start.4 = (bf16[2048,128]{1,0:T(8,128)(2,1)S(1)}, bf16[2048,128]{1,0:T(8,128)(2,1)}, u32[]{:S(2)}) copy-start(bf16[2048,128]{1,0:T(8,128)(2,1)} %get-tuple-element.67) | copy-start | bytes 1572868
  18.8 60.2 %copy-start = (bf16[2048,128]{1,0:T(8,128)(2,1)S(1)}, bf16[2048,128]{1,0:T(8,128)(2,1)}, u32[]{:S(2)}) copy-start(bf16[2048,128]{1,0:T(8,128)(2,1)} %get-tuple-element.72.refs_3_) | copy-start | bytes 1572868
  18.9 1.3 collective-permute-start.3
  20.2 27.2 %collective-permute-start.4 = (bf16[2048,128]{1,0:T(8,128)(2,1)}, bf16[2048,128]{1,0:T(8,128)(2,1)S(1)}, u32[]{:S(2)}, u32[]{:S(2)}) collective-permute-start(bf16[2048,128]{1,0:T(8,128)(2,1)} %get-tuple-element.62), channel_id=1, source_target_pairs={{0,64},{32,96},{64,128},{96,160},{128,192},{160,224},{192,0},{224,... | collective-permute-start | bytes 1572872 | tf_op jit(solution)/shard_map/ppermute | solution.py:48
  20.6 27.1 %collective-permute-start.5 = (bf16[2048,128]{1,0:T(8,128)(2,1)}, bf16[2048,128]{1,0:T(8,128)(2,1)S(1)}, u32[]{:S(2)}, u32[]{:S(2)}) collective-permute-start(bf16[2048,128]{1,0:T(8,128)(2,1)} %get-tuple-element.63), channel_id=1, source_target_pairs={{0,192},{32,224},{64,0},{96,32},{128,64},{160,96},{192,128},{224,1... | collective-permute-start | bytes 1572872 | tf_op jit(solution)/shard_map/ppermute | solution.py:48
  26.3 28.3 %all-to-all-start = ((bf16[32,32,256]{2,1,0:T(8,128)(2,1)}), bf16[32,32,256]{2,1,0:T(8,128)(2,1)S(1)}, u32[]{:S(2)}, u32[]{:S(2)}) async-start(bf16[32,32,256]{2,1,0:T(8,128)(2,1)} %collect.1), calls=%async_computation | async-start | bytes 1048576 | tf_op jit(solution)/shard_map/all_to_all | solution.py:502
  47.7 31.3 %collective-permute-start.6 = (bf16[2048,128]{1,0:T(8,128)(2,1)S(1)}, bf16[2048,128]{1,0:T(8,128)(2,1)S(1)}, u32[]{:S(2)}, u32[]{:S(2)}) collective-permute-start(bf16[2048,128]{1,0:T(8,128)(2,1)S(1)} %copy-done.4), channel_id=1, source_target_pairs={{0,128},{32,160},{64,192},{96,224},{128,0},{160,32},{192,64},{224,... | collective-permute-start | bytes 1572872 | tf_op jit(solution)/shard_map/ppermute | solution.py:48
  79.1 2.9 %collective-permute-start.7 = (bf16[4096,128]{1,0:T(8,128)(2,1)S(1)}, bf16[4096,128]{1,0:T(8,128)(2,1)S(1)}, u32[]{:S(2)}, u32[]{:S(2)}) collective-permute-start(bf16[4096,128]{1,0:T(8,128)(2,1)S(1)} %gather_halves.4), channel_id=1, source_target_pairs={{0,32},{32,0},{64,96},{96,64},{128,160},{160,128},{192,224},{224,1... | collective-permute-start | bytes 3145736 | tf_op jit(solution)/shard_map/ppermute | solution.py:48
  94.5 0.8 copy-start.3
  95.3 25.7 %collective-permute-start.8 = (bf16[2048,128]{1,0:T(8,128)(2,1)}, bf16[2048,128]{1,0:T(8,128)(2,1)S(1)}, u32[]{:S(2)}, u32[]{:S(2)}) collective-permute-start(bf16[2048,128]{1,0:T(8,128)(2,1)} %get-tuple-element.74), channel_id=1, source_target_pairs={{0,64},{32,96},{64,128},{96,160},{128,192},{160,224},{192,0},{224,... | collective-permute-start | bytes 1572872 | tf_op jit(solution)/shard_map/ppermute | solution.py:48
  95.3 26.7 %collective-permute-start.9 = (bf16[2048,128]{1,0:T(8,128)(2,1)}, bf16[2048,128]{1,0:T(8,128)(2,1)S(1)}, u32[]{:S(2)}, u32[]{:S(2)}) collective-permute-start(bf16[2048,128]{1,0:T(8,128)(2,1)} %get-tuple-element.75), channel_id=1, source_target_pairs={{0,192},{32,224},{64,0},{96,32},{128,64},{160,96},{192,128},{224,1... | collective-permute-start | bytes 1572872 | tf_op jit(solution)/shard_map/ppermute | solution.py:48
  99.5 30.7 %all-to-all-start.1 = ((bf16[32,32,256]{2,1,0:T(8,128)(2,1)}), bf16[32,32,256]{2,1,0:T(8,128)(2,1)S(1)}, u32[]{:S(2)}, u32[]{:S(2)}) async-start(bf16[32,32,256]{2,1,0:T(8,128)(2,1)} %get-tuple-element.81), calls=%async_computation.1 | async-start | bytes 1048576 | tf_op jit(solution)/shard_map/all_to_all | solution.py:506
  122.0 30.7 %collective-permute-start.10 = (bf16[2048,128]{1,0:T(8,128)(2,1)}, bf16[2048,128]{1,0:T(8,128)(2,1)S(1)}, u32[]{:S(2)}, u32[]{:S(2)}) collective-permute-start(bf16[2048,128]{1,0:T(8,128)(2,1)} %copy-done.3), channel_id=1, source_target_pairs={{0,128},{32,160},{64,192},{96,224},{128,0},{160,32},{192,64},{224,... | collective-permute-start | bytes 1572872 | tf_op jit(solution)/shard_map/ppermute | solution.py:48
  130.9 8.9 %collective-permute-start.11 = (bf16[64,128]{1,0:T(8,128)(2,1)S(1)}, bf16[64,128]{1,0:T(8,128)(2,1)S(1)}, u32[]{:S(2)}, u32[]{:S(2)}) collective-permute-start(bf16[64,128]{1,0:T(8,128)(2,1)S(1)} %get-tuple-element.82), channel_id=1, source_target_pairs={{0,64},{32,96},{64,128},{96,160},{128,192},{160,224},{192,0},{224,... | collective-permute-start | bytes 49160 | tf_op jit(solution)/shard_map/ppermute | solution.py:48
  131.0 20.3 %collective-permute-start.12 = (bf16[64,128]{1,0:T(8,128)(2,1)S(1)}, bf16[64,128]{1,0:T(8,128)(2,1)S(1)}, u32[]{:S(2)}, u32[]{:S(2)}) collective-permute-start(bf16[64,128]{1,0:T(8,128)(2,1)S(1)} %get-tuple-element.83), channel_id=1, source_target_pairs={{0,192},{32,224},{64,0},{96,32},{128,64},{160,96},{192,128},{224,1... | collective-permute-start | bytes 49160 | tf_op jit(solution)/shard_map/ppermute | solution.py:48
  135.1 17.6 %collective-permute-start.13 = (bf16[64,128]{1,0:T(8,128)(2,1)S(1)}, bf16[64,128]{1,0:T(8,128)(2,1)S(1)}, u32[]{:S(2)}, u32[]{:S(2)}) collective-permute-start(bf16[64,128]{1,0:T(8,128)(2,1)S(1)} %get-tuple-element.84), channel_id=1, source_target_pairs={{0,128},{32,160},{64,192},{96,224},{128,0},{160,32},{192,64},{224,... | collective-permute-start | bytes 49160 | tf_op jit(solution)/shard_map/ppermute | solution.py:48
  152.9 2.8 %collective-permute-start.14 = (bf16[4224,128]{1,0:T(8,128)(2,1)S(1)}, bf16[4224,128]{1,0:T(8,128)(2,1)S(1)}, u32[]{:S(2)}, u32[]{:S(2)}) collective-permute-start(bf16[4224,128]{1,0:T(8,128)(2,1)S(1)} %gather_halves.5), channel_id=1, source_target_pairs={{0,32},{32,0},{64,96},{96,64},{128,160},{160,128},{192,224},{224,1... | collective-permute-start | bytes 3244040 | tf_op jit(solution)/shard_map/ppermute | solution.py:48

commit v4 on v3

--- a/solution.py
+++ b/solution.py
@@ -130,13 +130,14 @@
     for i, ref in enumerate((k_ref, v_ref)):
         for r in range(0, BLOCK, strip):
             pairs.append((ref.at[r : r + strip, :], held.at[i, r : r + strip, :]))
-    for copy in copy_all(pairs, sems):
-        copy.wait()
+    copies = copy_all(pairs, sems)
     pool_near = pooling(NEAR_ROWS, NEAR)
     group = lax.broadcasted_iota(jnp.int32, (TAIL, NEAR_ROWS), 1) // (FAR // NEAR)
     row = lax.broadcasted_iota(jnp.int32, (TAIL, NEAR_ROWS), 0)
     far = None
     for i in range(2):
+        for copy in copies[4 * i : 4 * i + 4]:
+            copy.wait()
         near = nn(pool_near, held[i]).astype(BF16)
         pool_far = jnp.where(row == group + i * FAR_ROWS, F32(NEAR / FAR), F32(0.0)).astype(BF16)
         far = nn(pool_far, near) if far is None else far + nn(pool_far, near)
@@ -255,6 +256,10 @@
     )(at, *parts, swapped)
 
 
+def highest(scores):
+    return jnp.max(scores.reshape(scores.shape[0] // 8, 8, scores.shape[1]), axis=0)
+
+
 def attend_kernel(at_ref, *refs):
     n = len(CHIPS)
     ins, swapped, far_ref, outs, far_out = refs[:n], refs[n], refs[n + 1], refs[n + 2 : 2 * n + 2], refs[2 * n + 2]
@@ -301,23 +306,28 @@
             far_from = wide2 + near
             total = far_from + FAR_ALL
             halves = [slice(b * BLOCK, (b + 1) * BLOCK) for b in range(2)]
+            tops = []
             for b, cols in enumerate(halves):
+                own = jnp.where(later, F32(BLOCKED), nt(key(blocks[b]), qs[b]))
+                s_s[BLOCK:wide2, cols] = own
+                tops.append(highest(own))
                 if blocks[b] == 0:
                     s_s[0:BLOCK, cols] = jnp.full((BLOCK, BLOCK), BLOCKED, F32)
                 else:
-                    s_s[0:BLOCK, cols] = nt(key(befores[b]), qs[b])
-                s_s[BLOCK:wide2, cols] = jnp.where(later, F32(BLOCKED), nt(key(blocks[b]), qs[b]))
+                    before = nt(key(befores[b]), qs[b])
+                    s_s[0:BLOCK, cols] = before
+                    tops[b] = jnp.maximum(tops[b], highest(before))
+            top = jnp.concatenate(tops, axis=1)
             s_s[wide2:far_from, :] = nt(kn_s[head, 0:near, :], q)
             s_s[far_from - NEAR_ROWS : far_from, 0:BLOCK] = jnp.full((NEAR_ROWS, BLOCK), BLOCKED, F32)
             for i in range(0, FAR_ALL, BLOCK):
-                s_s[far_from + i : far_from + i + BLOCK, :] = nt(kf[i : i + BLOCK, :], q) + far_bias[i : i + BLOCK]
+                scores = nt(kf[i : i + BLOCK, :], q) + far_bias[i : i + BLOCK]
+                s_s[far_from + i : far_from + i + BLOCK, :] = scores
+                top = jnp.maximum(top, highest(scores))
             chunks = [(0, BLOCK), (BLOCK, BLOCK)]
             chunks += [(wide2 + i, min(BLOCK, near - i)) for i in range(0, near, BLOCK)]
             chunks += [(far_from + i, BLOCK) for i in range(0, FAR_ALL, BLOCK)]
-            top = None
-            for start, size in chunks:
-                here = jnp.max(s_s[start : start + size, :].reshape(size // 8, 8, wide2), axis=0)
-                top = here if top is None else jnp.maximum(top, here)
+            top = jnp.maximum(top, highest(s_s[wide2:far_from, :]))
             top = jnp.max(top, axis=0, keepdims=True)
             norm = None
             for start, size in chunks:

time: 160 us -> 160 us (level)
  no operation moved by 1% of the time
where the time goes in v4:
time: 160 us; the launch traced here: 159 us
  waiting for transfers between devices  81.2 us (51%)
  starting transfers between devices  49.7 us (31%)
  Pallas kernels  25.4 us (16%)
    ppermute x15, waiting for transfers between devices, move(): lax.ppermute(buffer, 'wide', [(s, target(s, step)) for s in range(WIDE)])  72.8 us
    ppermute x15, starting transfers between devices, move(): lax.ppermute(buffer, 'wide', [(s, target(s, step)) for s in range(WIDE)])  32.6 us
    pallas_call x1, Pallas kernels, attend(): pl.pallas_call(attend_kernel, out_shape=[jax.ShapeDtypeStruct((2 * PART,...  12.5 us
    all_to_all x1, starting transfers between devices, shards(): lax.all_to_all(terms, 'narrow', 0, 0, tiled=True)  8.54 us
    all_to_all x1, starting transfers between devices, shards(): lax.all_to_all(collect(at, tails, swapped), 'narrow', 0, 0, tiled=True)  8.53 us
    all_to_all x1, waiting for transfers between devices, shards(): lax.all_to_all(terms, 'narrow', 0, 0, tiled=True)  5.4 us
    pallas_call x1, Pallas kernels, pack(): pl.pallas_call(pack_kernel, out_shape=[part] * n, in_specs=[pl.BlockSpec(...  3.88 us
  transfers between devices with their start and end apart: 17, of which 13 were waited for; matrix products, arithmetic and copies ran while one was open for 0% of the time, Pallas kernels for 4%

profile of v4, /device:TPU:34, one launch (start us, length us, event | category | flops | bytes accessed | tf_op | source)
XLA Modules:
  0.0 158.9 jit_solution(2900704271345410993)
XLA Ops:
  0.6 0.7 pad_add_fusion.at_ref
  1.3 3.0 %tails_of.1 = (bf16[64,128]{1,0:T(8,128)(2,1)}, bf16[64,128]{1,0:T(8,128)(2,1)}, bf16[64,128]{1,0:T(8,128)(2,1)}, bf16[64,128]{1,0:T(8,128)(2,1)}) custom-call(s32[2]{0:T(128)} %pad_add_fusion.at_ref, bf16[128,2048]{1,0:T(8,128)(2,1)} %k_ref.3, bf16[128,2048]{1,0:T(8,128)(2,1)} %v_ref.3), custom_call_target="tpu_custom_call" | custom-call | tf_op jit(solution)/shard_map/tails_of/pallas_call | solution.py:156
  4.3 3.3 %collective-permute-start = (bf16[64,128]{1,0:T(8,128)(2,1)}, bf16[64,128]{1,0:T(8,128)(2,1)S(1)}, u32[]{:S(2)}, u32[]{:S(2)}) collective-permute-start(bf16[64,128]{1,0:T(8,128)(2,1)} %get-tuple-element.45), channel_id=1, source_target_pairs={{0,64},{32,96},{64,128},{96,160},{128,192},{160,224},{192,0},{224,... | collective-permute-start | bytes 49160 | tf_op jit(solution)/shard_map/ppermute | solution.py:48
  7.7 2.2 %collective-permute-start.1 = (bf16[64,128]{1,0:T(8,128)(2,1)}, bf16[64,128]{1,0:T(8,128)(2,1)S(1)}, u32[]{:S(2)}, u32[]{:S(2)}) collective-permute-start(bf16[64,128]{1,0:T(8,128)(2,1)} %get-tuple-element.46), channel_id=1, source_target_pairs={{0,192},{32,224},{64,0},{96,32},{128,64},{160,96},{192,128},{224,1... | collective-permute-start | bytes 49160 | tf_op jit(solution)/shard_map/ppermute | solution.py:48
  9.9 4.9 %collective-permute-start.2 = (bf16[64,128]{1,0:T(8,128)(2,1)}, bf16[64,128]{1,0:T(8,128)(2,1)S(1)}, u32[]{:S(2)}, u32[]{:S(2)}) collective-permute-start(bf16[64,128]{1,0:T(8,128)(2,1)} %get-tuple-element.47), channel_id=1, source_target_pairs={{0,128},{32,160},{64,192},{96,224},{128,0},{160,32},{192,64},{224,... | collective-permute-start | bytes 49160 | tf_op jit(solution)/shard_map/ppermute | solution.py:48
  14.8 3.9 %pack.1 = (bf16[2048,128]{1,0:T(8,128)(2,1)}, bf16[2048,128]{1,0:T(8,128)(2,1)}, bf16[2048,128]{1,0:T(8,128)(2,1)}, bf16[2048,128]{1,0:T(8,128)(2,1)}) custom-call(s32[2]{0:T(128)} %pad_add_fusion.at_ref, bf16[128,2048]{1,0:T(8,128)(2,1)} %k_ref.3, bf16[128,2048]{1,0:T(8,128)(2,1)} %v_ref.3, bf16[128,2048]{1,0:T(8,128)(2,1)} %q_ref.1, bf16[128,2048]{1,0:T(8,128)(2,1)} %g_ref.1), custom_call_target="tpu_custom_call" | custom-call | bytes 4194304 | tf_op jit(solution)/shard_map/pack/pallas_call | solution.py:201
  18.7 0.0 copy-start.4
  18.7 0.0 copy-start
  18.8 0.0 collective-permute-done.refs_0_
  18.8 0.0 collective-permute-done.1.refs_1_
  18.8 0.0 collective-permute-done.2.refs_2_
  18.8 0.1 gather_halves.3
  18.9 0.1 collective-permute-start.3
  19.0 1.2 collective-permute-done.3.refs_4_
  20.2 0.3 collective-permute-start.4
  20.5 3.8 %collective-permute-start.5 = (bf16[2048,128]{1,0:T(8,128)(2,1)}, bf16[2048,128]{1,0:T(8,128)(2,1)S(1)}, u32[]{:S(2)}, u32[]{:S(2)}) collective-permute-start(bf16[2048,128]{1,0:T(8,128)(2,1)} %get-tuple-element.63), channel_id=1, source_target_pairs={{0,192},{32,224},{64,0},{96,32},{128,64},{160,96},{192,128},{224,1... | collective-permute-start | bytes 1572872 | tf_op jit(solution)/shard_map/ppermute | solution.py:48
  24.3 1.9 %collect.1 = bf16[32,32,256]{2,1,0:T(8,128)(2,1)} custom-call(s32[2]{0:T(128)S(1)} %copy-done.2, bf16[64,128]{1,0:T(8,128)(2,1)S(1)} %collective-permute-done.refs_0_, bf16[64,128]{1,0:T(8,128)(2,1)S(1)} %collective-permute-done.1.refs_1_, bf16[64,128]{1,0:T(8,128)(2,1)S(1)} %collective-permute-done.2.refs_2_, bf16[64,128]{1,0:T(8,128)(2,1)S(1)} %copy-done.1, ...), custom_call_target="tpu_custom_call" | custom-call | tf_op jit(solution)/shard_map/collect/pallas_call | solution.py:248
  26.2 8.5 %all-to-all-start = ((bf16[32,32,256]{2,1,0:T(8,128)(2,1)}), bf16[32,32,256]{2,1,0:T(8,128)(2,1)S(1)}, u32[]{:S(2)}, u32[]{:S(2)}) async-start(bf16[32,32,256]{2,1,0:T(8,128)(2,1)} %collect.1), calls=%async_computation | async-start | bytes 1048576 | tf_op jit(solution)/shard_map/all_to_all | solution.py:512
  34.8 12.7 %collective-permute-done.4.refs_0_ = bf16[2048,128]{1,0:T(8,128)(2,1)S(1)} collective-permute-done((bf16[2048,128]{1,0:T(8,128)(2,1)}, bf16[2048,128]{1,0:T(8,128)(2,1)S(1)}, u32[]{:S(2)}, u32[]{:S(2)}) %collective-permute-start.4) | collective-permute-done | bytes 524320 | tf_op jit(solution)/shard_map/ppermute | solution.py:48
  47.4 0.2 collective-permute-done.5.refs_1_
  47.6 3.9 %collective-permute-start.6 = (bf16[2048,128]{1,0:T(8,128)(2,1)S(1)}, bf16[2048,128]{1,0:T(8,128)(2,1)S(1)}, u32[]{:S(2)}, u32[]{:S(2)}) collective-permute-start(bf16[2048,128]{1,0:T(8,128)(2,1)S(1)} %copy-done.4), channel_id=1, source_target_pairs={{0,128},{32,160},{64,192},{96,224},{128,0},{160,32},{192,64},{224,... | collective-permute-start | bytes 1572872 | tf_op jit(solution)/shard_map/ppermute | solution.py:48
  51.5 3.0 %all-to-all-done.refs_5_ = bf16[32,32,256]{2,1,0:T(8,128)(2,1)S(1)} async-done(((bf16[32,32,256]{2,1,0:T(8,128)(2,1)}), bf16[32,32,256]{2,1,0:T(8,128)(2,1)S(1)}, u32[]{:S(2)}, u32[]{:S(2)}) %all-to-all-start) | async-done | bytes 524320 | tf_op jit(solution)/shard_map/all_to_all | solution.py:512
  54.6 24.4 %collective-permute-done.6.refs_2_ = bf16[2048,128]{1,0:T(8,128)(2,1)S(1)} collective-permute-done((bf16[2048,128]{1,0:T(8,128)(2,1)S(1)}, bf16[2048,128]{1,0:T(8,128)(2,1)S(1)}, u32[]{:S(2)}, u32[]{:S(2)}) %collective-permute-start.6) | collective-permute-done | bytes 524320 | tf_op jit(solution)/shard_map/ppermute | solution.py:48
  78.9 0.1 gather_halves.4
  79.0 0.3 collective-permute-start.7
  79.3 2.6 %collective-permute-done.7.refs_4_ = bf16[4096,128]{1,0:T(8,128)(2,1)S(1)} collective-permute-done((bf16[4096,128]{1,0:T(8,128)(2,1)S(1)}, bf16[4096,128]{1,0:T(8,128)(2,1)S(1)}, u32[]{:S(2)}, u32[]{:S(2)}) %collective-permute-start.7) | collective-permute-done | bytes 1048608 | tf_op jit(solution)/shard_map/ppermute | solution.py:48
  82.0 12.5 %attend.1 = (bf16[2048,128]{1,0:T(8,128)(2,1)}, bf16[2048,128]{1,0:T(8,128)(2,1)}, bf16[2048,128]{1,0:T(8,128)(2,1)S(1)}, bf16[2048,128]{1,0:T(8,128)(2,1)S(1)}, bf16[32,32,256]{2,1,0:T(8,128)(2,1)}) custom-call(s32[2]{0:T(128)S(1)} %copy-done.2, bf16[2048,128]{1,0:T(8,128)(2,1)S(1)} %collective-permute-done.4.refs_0_, ...), custom_call_target="tpu_custom_call" | custom-call | flops 3200000000 | bytes 4194304 | tf_op jit(solution)/shard_map/attend/pallas_call | solution.py:402
  94.5 0.0 copy-start.3
  94.5 0.8 copy-done.3
  95.3 0.0 collective-permute-start.8
  95.3 4.1 %collective-permute-start.9 = (bf16[2048,128]{1,0:T(8,128)(2,1)}, bf16[2048,128]{1,0:T(8,128)(2,1)S(1)}, u32[]{:S(2)}, u32[]{:S(2)}) collective-permute-start(bf16[2048,128]{1,0:T(8,128)(2,1)} %get-tuple-element.75), channel_id=1, source_target_pairs={{0,192},{32,224},{64,0},{96,32},{128,64},{160,96},{192,128},{224,1... | collective-permute-start | bytes 1572872 | tf_op jit(solution)/shard_map/ppermute | solution.py:48
  99.4 8.5 %all-to-all-start.1 = ((bf16[32,32,256]{2,1,0:T(8,128)(2,1)}), bf16[32,32,256]{2,1,0:T(8,128)(2,1)S(1)}, u32[]{:S(2)}, u32[]{:S(2)}) async-start(bf16[32,32,256]{2,1,0:T(8,128)(2,1)} %get-tuple-element.81), calls=%async_computation.1 | async-start | bytes 1048576 | tf_op jit(solution)/shard_map/all_to_all | solution.py:516
  108.0 13.0 %collective-permute-done.8.refs_0_ = bf16[2048,128]{1,0:T(8,128)(2,1)S(1)} collective-permute-done((bf16[2048,128]{1,0:T(8,128)(2,1)}, bf16[2048,128]{1,0:T(8,128)(2,1)S(1)}, u32[]{:S(2)}, u32[]{:S(2)}) %collective-permute-start.8) | collective-permute-done | bytes 524320 | tf_op jit(solution)/shard_map/ppermute | solution.py:48
  121.0 1.0 collective-permute-done.9.refs_1_
  122.0 2.8 %collective-permute-start.10 = (bf16[2048,128]{1,0:T(8,128)(2,1)}, bf16[2048,128]{1,0:T(8,128)(2,1)S(1)}, u32[]{:S(2)}, u32[]{:S(2)}) collective-permute-start(bf16[2048,128]{1,0:T(8,128)(2,1)} %copy-done.3), channel_id=1, source_target_pairs={{0,128},{32,160},{64,192},{96,224},{128,0},{160,32},{192,64},{224,... | collective-permute-start | bytes 1572872 | tf_op jit(solution)/shard_map/ppermute | solution.py:48
  124.8 5.4 %all-to-all-done.1.terms_ref = bf16[32,32,256]{2,1,0:T(8,128)(2,1)S(1)} async-done(((bf16[32,32,256]{2,1,0:T(8,128)(2,1)}), bf16[32,32,256]{2,1,0:T(8,128)(2,1)S(1)}, u32[]{:S(2)}, u32[]{:S(2)}) %all-to-all-start.1) | async-done | bytes 524320 | tf_op jit(solution)/shard_map/all_to_all | solution.py:516
  130.2 0.8 total.1
  130.9 0.1 collective-permute-start.11
  131.0 4.1 %collective-permute-start.12 = (bf16[64,128]{1,0:T(8,128)(2,1)S(1)}, bf16[64,128]{1,0:T(8,128)(2,1)S(1)}, u32[]{:S(2)}, u32[]{:S(2)}) collective-permute-start(bf16[64,128]{1,0:T(8,128)(2,1)S(1)} %get-tuple-element.83), channel_id=1, source_target_pairs={{0,192},{32,224},{64,0},{96,32},{128,64},{160,96},{192,128},{224,1... | collective-permute-start | bytes 49160 | tf_op jit(solution)/shard_map/ppermute | solution.py:48
  135.1 2.5 %collective-permute-start.13 = (bf16[64,128]{1,0:T(8,128)(2,1)S(1)}, bf16[64,128]{1,0:T(8,128)(2,1)S(1)}, u32[]{:S(2)}, u32[]{:S(2)}) collective-permute-start(bf16[64,128]{1,0:T(8,128)(2,1)S(1)} %get-tuple-element.84), channel_id=1, source_target_pairs={{0,128},{32,160},{64,192},{96,224},{128,0},{160,32},{192,64},{224,... | collective-permute-start | bytes 49160 | tf_op jit(solution)/shard_map/ppermute | solution.py:48
  137.6 2.2 %collective-permute-done.11.refs_4_.refs_5_ = bf16[64,128]{1,0:T(8,128)(2,1)S(1)} collective-permute-done((bf16[64,128]{1,0:T(8,128)(2,1)S(1)}, bf16[64,128]{1,0:T(8,128)(2,1)S(1)}, u32[]{:S(2)}, u32[]{:S(2)}) %collective-permute-start.11) | collective-permute-done | bytes 16416 | tf_op jit(solution)/shard_map/ppermute | solution.py:48
  139.8 11.5 %collective-permute-done.12.refs_5_.refs_6_ = bf16[64,128]{1,0:T(8,128)(2,1)S(1)} collective-permute-done((bf16[64,128]{1,0:T(8,128)(2,1)S(1)}, bf16[64,128]{1,0:T(8,128)(2,1)S(1)}, u32[]{:S(2)}, u32[]{:S(2)}) %collective-permute-start.12) | collective-permute-done | bytes 16416 | tf_op jit(solution)/shard_map/ppermute | solution.py:48
  151.3 1.4 collective-permute-done.13.refs_6_.refs_7_
  152.7 0.0 collective-permute-done.10.refs_2_
  152.7 0.2 gather_halves.5
  152.9 0.1 collective-permute-start.14
  153.0 2.7 %collective-permute-done.14.refs_4_ = bf16[4224,128]{1,0:T(8,128)(2,1)S(1)} collective-permute-done((bf16[4224,128]{1,0:T(8,128)(2,1)S(1)}, bf16[4224,128]{1,0:T(8,128)(2,1)S(1)}, u32[]{:S(2)}, u32[]{:S(2)}) %collective-permute-start.14) | collective-permute-done | bytes 1081376 | tf_op jit(solution)/shard_map/ppermute | solution.py:48
  155.7 3.0 %unpack.1 = (bf16[128,2048]{1,0:T(8,128)(2,1)}, bf16[128,2048]{1,0:T(8,128)(2,1)}, bf16[128,2048]{1,0:T(8,128)(2,1)}, bf16[128,2048]{1,0:T(8,128)(2,1)}) custom-call(s32[2]{0:T(128)S(1)} %copy-done.2, bf16[2048,128]{1,0:T(8,128)(2,1)S(1)} %collective-permute-done.8.refs_0_, bf16[2048,128]{1,0:T(8,128)(2,1)S(1)} %collective-permute-done.9.refs_1_, ...), custom_call_target="tpu_custom_call" | custom-call | tf_op jit(solution)/shard_map/unpack/pallas_call | solution.py:486
  (6 shorter events, 0.0 us)
Async XLA Ops:
  4.3 14.5 %copy-start.1 = (bf16[64,128]{1,0:T(8,128)(2,1)S(1)}, bf16[64,128]{1,0:T(8,128)(2,1)}, u32[]{:S(2)}) copy-start(bf16[64,128]{1,0:T(8,128)(2,1)} %get-tuple-element.56.refs_3_) | copy-start | bytes 49156
  4.3 14.4 %collective-permute-start = (bf16[64,128]{1,0:T(8,128)(2,1)}, bf16[64,128]{1,0:T(8,128)(2,1)S(1)}, u32[]{:S(2)}, u32[]{:S(2)}) collective-permute-start(bf16[64,128]{1,0:T(8,128)(2,1)} %get-tuple-element.45), channel_id=1, source_target_pairs={{0,64},{32,96},{64,128},{96,160},{128,192},{160,224},{192,0},{224,... | collective-permute-start | bytes 49160 | tf_op jit(solution)/shard_map/ppermute | solution.py:48
  7.7 11.1 %collective-permute-start.1 = (bf16[64,128]{1,0:T(8,128)(2,1)}, bf16[64,128]{1,0:T(8,128)(2,1)S(1)}, u32[]{:S(2)}, u32[]{:S(2)}) collective-permute-start(bf16[64,128]{1,0:T(8,128)(2,1)} %get-tuple-element.46), channel_id=1, source_target_pairs={{0,192},{32,224},{64,0},{96,32},{128,64},{160,96},{192,128},{224,1... | collective-permute-start | bytes 49160 | tf_op jit(solution)/shard_map/ppermute | solution.py:48
  9.9 14.4 %copy-start.2 = (s32[2]{0:T(128)S(1)}, s32[2]{0:T(128)}, u32[]{:S(2)}) copy-start(s32[2]{0:T(128)} %pad_add_fusion.at_ref) | copy-start | bytes 28
  9.9 8.9 %collective-permute-start.2 = (bf16[64,128]{1,0:T(8,128)(2,1)}, bf16[64,128]{1,0:T(8,128)(2,1)S(1)}, u32[]{:S(2)}, u32[]{:S(2)}) collective-permute-start(bf16[64,128]{1,0:T(8,128)(2,1)} %get-tuple-element.47), channel_id=1, source_target_pairs={{0,128},{32,160},{64,192},{96,224},{128,0},{160,32},{192,64},{224,... | collective-permute-start | bytes 49160 | tf_op jit(solution)/shard_map/ppermute | solution.py:48
  18.7 28.9 %copy-start.4 = (bf16[2048,128]{1,0:T(8,128)(2,1)S(1)}, bf16[2048,128]{1,0:T(8,128)(2,1)}, u32[]{:S(2)}) copy-start(bf16[2048,128]{1,0:T(8,128)(2,1)} %get-tuple-element.67) | copy-start | bytes 1572868
  18.7 60.2 %copy-start = (bf16[2048,128]{1,0:T(8,128)(2,1)S(1)}, bf16[2048,128]{1,0:T(8,128)(2,1)}, u32[]{:S(2)}) copy-start(bf16[2048,128]{1,0:T(8,128)(2,1)} %get-tuple-element.72.refs_3_) | copy-start | bytes 1572868
  18.9 1.3 collective-permute-start.3
  20.2 27.2 %collective-permute-start.4 = (bf16[2048,128]{1,0:T(8,128)(2,1)}, bf16[2048,128]{1,0:T(8,128)(2,1)S(1)}, u32[]{:S(2)}, u32[]{:S(2)}) collective-permute-start(bf16[2048,128]{1,0:T(8,128)(2,1)} %get-tuple-element.62), channel_id=1, source_target_pairs={{0,64},{32,96},{64,128},{96,160},{128,192},{160,224},{192,0},{224,... | collective-permute-start | bytes 1572872 | tf_op jit(solution)/shard_map/ppermute | solution.py:48
  20.5 27.1 %collective-permute-start.5 = (bf16[2048,128]{1,0:T(8,128)(2,1)}, bf16[2048,128]{1,0:T(8,128)(2,1)S(1)}, u32[]{:S(2)}, u32[]{:S(2)}) collective-permute-start(bf16[2048,128]{1,0:T(8,128)(2,1)} %get-tuple-element.63), channel_id=1, source_target_pairs={{0,192},{32,224},{64,0},{96,32},{128,64},{160,96},{192,128},{224,1... | collective-permute-start | bytes 1572872 | tf_op jit(solution)/shard_map/ppermute | solution.py:48
  26.2 28.3 %all-to-all-start = ((bf16[32,32,256]{2,1,0:T(8,128)(2,1)}), bf16[32,32,256]{2,1,0:T(8,128)(2,1)S(1)}, u32[]{:S(2)}, u32[]{:S(2)}) async-start(bf16[32,32,256]{2,1,0:T(8,128)(2,1)} %collect.1), calls=%async_computation | async-start | bytes 1048576 | tf_op jit(solution)/shard_map/all_to_all | solution.py:512
  47.6 31.3 %collective-permute-start.6 = (bf16[2048,128]{1,0:T(8,128)(2,1)S(1)}, bf16[2048,128]{1,0:T(8,128)(2,1)S(1)}, u32[]{:S(2)}, u32[]{:S(2)}) collective-permute-start(bf16[2048,128]{1,0:T(8,128)(2,1)S(1)} %copy-done.4), channel_id=1, source_target_pairs={{0,128},{32,160},{64,192},{96,224},{128,0},{160,32},{192,64},{224,... | collective-permute-start | bytes 1572872 | tf_op jit(solution)/shard_map/ppermute | solution.py:48
  79.0 2.9 %collective-permute-start.7 = (bf16[4096,128]{1,0:T(8,128)(2,1)S(1)}, bf16[4096,128]{1,0:T(8,128)(2,1)S(1)}, u32[]{:S(2)}, u32[]{:S(2)}) collective-permute-start(bf16[4096,128]{1,0:T(8,128)(2,1)S(1)} %gather_halves.4), channel_id=1, source_target_pairs={{0,32},{32,0},{64,96},{96,64},{128,160},{160,128},{192,224},{224,1... | collective-permute-start | bytes 3145736 | tf_op jit(solution)/shard_map/ppermute | solution.py:48
  94.5 0.8 copy-start.3
  95.3 25.6 %collective-permute-start.8 = (bf16[2048,128]{1,0:T(8,128)(2,1)}, bf16[2048,128]{1,0:T(8,128)(2,1)S(1)}, u32[]{:S(2)}, u32[]{:S(2)}) collective-permute-start(bf16[2048,128]{1,0:T(8,128)(2,1)} %get-tuple-element.74), channel_id=1, source_target_pairs={{0,64},{32,96},{64,128},{96,160},{128,192},{160,224},{192,0},{224,... | collective-permute-start | bytes 1572872 | tf_op jit(solution)/shard_map/ppermute | solution.py:48
  95.3 26.7 %collective-permute-start.9 = (bf16[2048,128]{1,0:T(8,128)(2,1)}, bf16[2048,128]{1,0:T(8,128)(2,1)S(1)}, u32[]{:S(2)}, u32[]{:S(2)}) collective-permute-start(bf16[2048,128]{1,0:T(8,128)(2,1)} %get-tuple-element.75), channel_id=1, source_target_pairs={{0,192},{32,224},{64,0},{96,32},{128,64},{160,96},{192,128},{224,1... | collective-permute-start | bytes 1572872 | tf_op jit(solution)/shard_map/ppermute | solution.py:48
  99.4 30.7 %all-to-all-start.1 = ((bf16[32,32,256]{2,1,0:T(8,128)(2,1)}), bf16[32,32,256]{2,1,0:T(8,128)(2,1)S(1)}, u32[]{:S(2)}, u32[]{:S(2)}) async-start(bf16[32,32,256]{2,1,0:T(8,128)(2,1)} %get-tuple-element.81), calls=%async_computation.1 | async-start | bytes 1048576 | tf_op jit(solution)/shard_map/all_to_all | solution.py:516
  122.0 30.7 %collective-permute-start.10 = (bf16[2048,128]{1,0:T(8,128)(2,1)}, bf16[2048,128]{1,0:T(8,128)(2,1)S(1)}, u32[]{:S(2)}, u32[]{:S(2)}) collective-permute-start(bf16[2048,128]{1,0:T(8,128)(2,1)} %copy-done.3), channel_id=1, source_target_pairs={{0,128},{32,160},{64,192},{96,224},{128,0},{160,32},{192,64},{224,... | collective-permute-start | bytes 1572872 | tf_op jit(solution)/shard_map/ppermute | solution.py:48
  130.9 8.9 %collective-permute-start.11 = (bf16[64,128]{1,0:T(8,128)(2,1)S(1)}, bf16[64,128]{1,0:T(8,128)(2,1)S(1)}, u32[]{:S(2)}, u32[]{:S(2)}) collective-permute-start(bf16[64,128]{1,0:T(8,128)(2,1)S(1)} %get-tuple-element.82), channel_id=1, source_target_pairs={{0,64},{32,96},{64,128},{96,160},{128,192},{160,224},{192,0},{224,... | collective-permute-start | bytes 49160 | tf_op jit(solution)/shard_map/ppermute | solution.py:48
  131.0 20.2 %collective-permute-start.12 = (bf16[64,128]{1,0:T(8,128)(2,1)S(1)}, bf16[64,128]{1,0:T(8,128)(2,1)S(1)}, u32[]{:S(2)}, u32[]{:S(2)}) collective-permute-start(bf16[64,128]{1,0:T(8,128)(2,1)S(1)} %get-tuple-element.83), channel_id=1, source_target_pairs={{0,192},{32,224},{64,0},{96,32},{128,64},{160,96},{192,128},{224,1... | collective-permute-start | bytes 49160 | tf_op jit(solution)/shard_map/ppermute | solution.py:48
  135.1 17.5 %collective-permute-start.13 = (bf16[64,128]{1,0:T(8,128)(2,1)S(1)}, bf16[64,128]{1,0:T(8,128)(2,1)S(1)}, u32[]{:S(2)}, u32[]{:S(2)}) collective-permute-start(bf16[64,128]{1,0:T(8,128)(2,1)S(1)} %get-tuple-element.84), channel_id=1, source_target_pairs={{0,128},{32,160},{64,192},{96,224},{128,0},{160,32},{192,64},{224,... | collective-permute-start | bytes 49160 | tf_op jit(solution)/shard_map/ppermute | solution.py:48
  152.9 2.8 %collective-permute-start.14 = (bf16[4224,128]{1,0:T(8,128)(2,1)S(1)}, bf16[4224,128]{1,0:T(8,128)(2,1)S(1)}, u32[]{:S(2)}, u32[]{:S(2)}) collective-permute-start(bf16[4224,128]{1,0:T(8,128)(2,1)S(1)} %gather_halves.5), channel_id=1, source_target_pairs={{0,32},{32,0},{64,96},{96,64},{128,160},{160,128},{192,224},{224,1... | collective-permute-start | bytes 3244040 | tf_op jit(solution)/shard_map/ppermute | solution.py:48
